TPU v7x, 32 devices: a whole 2x2x4 slice. The times are simulated.
32 devices in a mesh: grp: 2 (over y), ctx: 4 (over z), head: 2 (over x), sub: 2 (over core).
Axes of the slice: x: 2, y: 2, z: 4, core: 2. Of those that a mesh axis runs over, the one named last changes fastest.
Arguments:
- queries: bfloat16 [512, 16384], P(('grp', 'ctx', 'head', 'sub')), parts along dimension 0, may hold values from -400 to 400
- kv_cache: bfloat16 [2, 8192, 1024], P(None, ('grp', 'ctx', 'sub'), 'head'), parts along dimension 1, may hold values from -6 to 6
- page_counts: int32 [8], P('grp'), parts along dimension 0, may hold values from 1 to 4, as said below
Outputs:
- attended: bfloat16 [512, 16384], P(('grp', 'ctx', 'head', 'sub')), parts along dimension 0
There are 2 independent parts, one for each index of `grp`. A program takes and returns all parts, laid end to end along the dimension named above; each array names one. Nothing has to cross between parts.
Inputs may be any that keep to these rules, and one draw needn't show every extreme that they name: `page_counts`: each count is at least 1, the counts sum to exactly 8, and one request has exactly 4 pages.
All inputs are finite; a program needn't handle non-finite values.
Results may differ from a plain program's by a relative error of at most 0.014.
Values may be sent and summed in bfloat16 or wider, within the bound.
No kernel may reach another device: no remote copies, remote signals or barrier semaphores. Data moves between devices by JAX's collectives and lax.ppermute only.
A program may use at most 64 MiB of HBM per device.

v0:
```python
import functools

import jax
import jax.numpy as jnp
from jax import lax
from jax.experimental import pallas as pl
from jax.experimental.pallas import tpu as pltpu
from jax.sharding import PartitionSpec as P

HQ = 128
KVH = 8
HD = 128
REQS = 4
QR = 64
PAGE = 256
SPAN = 256


NEG = -1e30
EXP2_SCALE = HD ** (-0.5) * 1.4426950408889634


def run(copies):
    for copy in copies:
        copy.start()
    for copy in copies:
        copy.wait()


def head_part(step, width):
    return pl.ds(pl.multiple_of((lax.axis_index("head") ^ step) * width, width), width)


def split_kernel(queries, *refs):
    outs, sems = refs[:-1], refs[-1]
    run([
        pltpu.make_async_copy(queries.at[:, head_part(step, out.shape[1])], out, sems.at[step])
        for step, out in enumerate(outs)
    ])


def join_kernel(keys, *refs):
    out, sems = refs[-2:]

    @pl.when(lax.axis_index("sub") == keys[0][1])
    def _():
        run([
            pltpu.make_async_copy(piece, out.at[:, head_part(step, piece.shape[1])], sems.at[i])
            for i, (piece, (step, _)) in enumerate(zip(refs, keys))
        ])


def worker_places(low_ctx):
    return (0, 0), (low_ctx, 1), (low_ctx + 1, 0), (low_ctx + 1, 1)


def own_request(low_ctx):
    ctx, sub = lax.axis_index("ctx"), lax.axis_index("sub")
    found = jnp.int32(-1)
    for request, place in enumerate(worker_places(low_ctx)):
        found = jnp.where((ctx == place[0]) & (sub == place[1]), request, found)
    return found


def gather_kernel(low_ctx, counts, own, near, far, after, out, sems):
    local_kv, most_pages = out.shape[:2]
    request = own_request(low_ctx)

    @pl.when(request >= 0)
    def _():
        start = jnp.int32(0)
        for r in range(REQS):
            start = start + jnp.where(r < request, counts[r], 0)
        count = counts[request]
        near_pair = jnp.where(request == 0, 1, request ^ 1)
        home_pair = jnp.where(request == 0, -1, request)

        def of_page(p):
            page = start + p
            page_rows = pl.ds(pl.multiple_of(lax.rem(page, 2) * PAGE, PAGE), PAGE)
            return page // 2, page_rows

        def home_copies(p, page_rows):
            return [
                pltpu.make_async_copy(own.at[i, page_rows, pl.ds(g * HD, HD)], out.at[g, p, i], sems.at[g, p, i])
                for g in range(local_kv) for i in range(2)
            ]

        for p in range(most_pages):
            pair, page_rows = of_page(p)
            @pl.when((p < count) & (pair == home_pair))
            def _():
                for copy in home_copies(p, page_rows):
                    copy.start()
        for p in range(most_pages):
            pair, page_rows = of_page(p)
            for ref, chosen in ((near, pair == near_pair), (far, (pair != near_pair) & (pair != home_pair))):
                @pl.when((p < count) & chosen)
                def _():
                    for g in range(local_kv):
                        for i in range(2):
                            out[g, p, i] = ref[i, page_rows, g * HD:(g + 1) * HD]
        for p in range(most_pages):
            pair, page_rows = of_page(p)
            @pl.when((p < count) & (pair == home_pair))
            def _():
                for copy in home_copies(p, page_rows):
                    copy.wait()


def attend_kernel(low_ctx, sub_count, keys, waits, counts, pages_in, *refs):
    queries, outs = refs[:len(keys)], refs[len(keys) + waits:]
    head = lax.axis_index("head")
    tokens, width = queries[0].shape
    local_kv, most_pages = pages_in.shape[:2]
    span = width // local_kv
    per_group = span // HD
    piece_rows = per_group * tokens
    rows = len(keys) * piece_rows

    def attend(pages):
        row = lax.broadcasted_iota(jnp.int32, (rows, PAGE), 0)
        token = lax.rem(row, tokens)
        for i, (step, source) in enumerate(keys):
            first_token = ((head ^ step) * sub_count + source) * tokens
            token = jnp.where(row // piece_rows == i, token + first_token, token)
        column = lax.broadcasted_iota(jnp.int32, (rows, PAGE), 1)
        visible = column <= PAGE - QR + token

        def scores_of(g):
            q_blocks = [ref[:, g * span:(g + 1) * span] for ref in queries]
            q_rows = jnp.concatenate([q[:, j * HD:(j + 1) * HD] for q in q_blocks for j in range(per_group)], axis=0)
            for p in range(pages):
                scores = lax.dot_general(
                    q_rows, pages_in[g, p, 0], (((1,), (1,)), ((), ())), preferred_element_type=jnp.float32
                )
                yield jnp.where(visible, scores, NEG) if p == pages - 1 else scores

        scores = list(scores_of(0))
        for g in range(local_kv):
            following = scores_of(g + 1) if g + 1 < local_kv else iter(())
            later = []
            top = jnp.max(functools.reduce(jnp.maximum, scores), axis=1, keepdims=True)
            totals, product = None, None
            for p in range(pages):
                later += [s for _, s in zip(range(1), following)]
                numerators = jnp.exp2((scores[p] - top) * EXP2_SCALE)
                part = jnp.dot(
                    numerators.astype(jnp.bfloat16), pages_in[g, p, 1], preferred_element_type=jnp.float32
                )
                totals = numerators if p == 0 else totals + numerators
                product = part if p == 0 else product + part
            totals = jnp.sum(totals, axis=1, keepdims=True)
            done = (product / totals).astype(jnp.bfloat16)
            for i, out in enumerate(outs):
                start = i * piece_rows
                out[:, g * span:(g + 1) * span] = jnp.concatenate(
                    [done[start + j * tokens:start + (j + 1) * tokens] for j in range(per_group)], axis=1
                )
            scores = later

    request = own_request(low_ctx)

    @pl.when(request >= 0)
    def _():
        count = counts[request]
        for pages in [*range(1, most_pages - REQS + 3), most_pages]:
            @pl.when(count == pages)
            def _():
                attend(pages)


def one_request_each(queries, kv_cache, page_counts):
    ctx_size, sub_size = lax.axis_size("ctx"), lax.axis_size("sub")
    head_count = lax.axis_size("head")
    low_ctx = ctx_size // 2
    most_pages = kv_cache.shape[1] // PAGE * ctx_size * sub_size // 4
    local_kv = kv_cache.shape[2] // HD
    tokens, width = queries.shape[0], queries.shape[1] // head_count
    anywhere = pl.BlockSpec(memory_space=pl.ANY)
    in_vmem = pl.BlockSpec(memory_space=pltpu.VMEM)
    q_piece = pltpu.VMEM((tokens, width), queries.dtype)

    def vmem(array):
        return pltpu.with_memory_space_constraint(array, pltpu.VMEM)

    def hbm(array):
        return pltpu.with_memory_space_constraint(array, pltpu.HBM)

    def moved(array, routes):
        def flat(place):
            return (place[0] * head_count + place[1]) * sub_size + place[2]

        return lax.ppermute(array, ("ctx", "head", "sub"), [(flat(a), flat(b)) for a, b in routes])

    def worker(request, head):
        ctx, sub = worker_places(low_ctx)[request]
        return ctx, head, sub

    heads = range(head_count)
    q_out = pl.pallas_call(
        split_kernel,
        out_shape=[q_piece] * head_count,
        in_specs=[anywhere],
        out_specs=[anywhere] * head_count,
        scratch_shapes=[pltpu.SemaphoreType.DMA((head_count,))],
        compiler_params=pltpu.CompilerParams(vmem_limit_bytes=2**20),
        name="split",
    )(hbm(queries))
    routes = {
        (step, s): [((r, h, s), worker(r, h ^ step)) for r in range(ctx_size) for h in heads]
        for s in range(sub_size) for step in heads[::-1]
    }
    q_in = {key: moved(q_out[key[0]], pairs) for key, pairs in routes.items()}

    pairs = [(low_ctx + n // 2, n % 2) for n in range(4)]
    workers = worker_places(low_ctx)
    near, far = (
        moved(kv_cache, [((*a[:1], h, *a[1:]), (*b[:1], h, *b[1:])) for a, b in sends for h in heads])
        for sends in (
            [(pairs[0], workers[1]), (pairs[1], workers[0]), (pairs[2], workers[3]), (pairs[3], workers[2])],
            [(pairs[0], workers[0]), (pairs[1], workers[2]), (pairs[2], workers[1])],
        )
    )
    first_here = pl.pallas_call(
        lambda *refs: None,
        out_shape=pltpu.VMEM((8, HD), jnp.float32),
        in_specs=[anywhere],
        out_specs=anywhere,
        compiler_params=pltpu.CompilerParams(vmem_limit_bytes=2**20),
        name="first_here",
    )(vmem(q_in[list(routes)[0]]))
    gathered = pl.pallas_call(
        functools.partial(gather_kernel, low_ctx),
        out_shape=pltpu.VMEM((local_kv, most_pages, 2, PAGE, HD), kv_cache.dtype),
        in_specs=[pl.BlockSpec(memory_space=pltpu.SMEM), anywhere] + [in_vmem] * 2 + [anywhere],
        out_specs=in_vmem,
        scratch_shapes=[pltpu.SemaphoreType.DMA((local_kv, most_pages, 2))],
        compiler_params=pltpu.CompilerParams(vmem_limit_bytes=2**20),
        name="gather",
    )(hbm(page_counts), hbm(kv_cache), vmem(near), vmem(far), vmem(first_here))

    back = {}
    after = []
    groups = [[(step, s) for step in heads[::-1]] for s in range(sub_size)]
    for keys in groups:
        outs = pl.pallas_call(
            functools.partial(attend_kernel, low_ctx, sub_size, keys, len(after)),
            out_shape=[q_piece] * len(keys),
            in_specs=[pl.BlockSpec(memory_space=pltpu.SMEM)] + [in_vmem] * (1 + len(keys)) + [anywhere] * len(after),
            out_specs=[in_vmem] * len(keys),
            compiler_params=pltpu.CompilerParams(vmem_limit_bytes=12 * 2**20),
            cost_estimate=pl.CostEstimate(flops=10**10, bytes_accessed=2**22, transcendentals=10**6),
            name=f"attend_{keys[0][1]}",
        )(hbm(page_counts), vmem(gathered), *[vmem(q_in[key]) for key in keys], *after)
        for key, out in zip(keys, outs):
            back[key] = moved(out, [(b, a) for a, b in routes[key]])
        after = [outs[0]]

    joined = []
    for keys in groups:
        joined = [
            pl.pallas_call(
                functools.partial(join_kernel, keys),
                out_shape=pltpu.HBM(queries.shape, queries.dtype),
                in_specs=[anywhere] * (len(keys) + len(joined)),
                out_specs=anywhere,
                scratch_shapes=[pltpu.SemaphoreType.DMA((len(keys),))],
                input_output_aliases={len(keys): 0} if joined else {},
                compiler_params=pltpu.CompilerParams(vmem_limit_bytes=2**20),
                name=f"join_{keys[0][1]}",
            )(*[vmem(back[key]) for key in keys], *map(hbm, joined))
        ]
    return joined[0]


def from_behind(array, axis, by):
    count = lax.axis_size(axis)
    pairs = [(i, i + by) for i in range(count) if 0 <= i + by < count]
    return lax.ppermute(array, axis, pairs)


def queries_to_pages(queries, kv_cache, page_counts):
    per_group = HQ // KVH
    local_heads = kv_cache.shape[2] // HD
    ctx_size = lax.axis_size("ctx")
    sub_size = lax.axis_size("sub")
    head_count = lax.axis_size("head")
    tok_rows = queries.shape[0]
    score_scale = HD ** (-0.5)
    regrouped = lax.all_to_all(queries, "head", split_axis=1, concat_axis=0, tiled=True)
    all_queries = lax.all_gather(regrouped, ("ctx", "sub"), axis=0, tiled=True)
    all_queries = all_queries.reshape(SPAN, local_heads, per_group, HD)
    page_ends = jnp.cumsum(page_counts)
    ctx_rows = SPAN // ctx_size
    offsets = jnp.arange(QR, dtype=jnp.int32)
    columns = jnp.arange(PAGE, dtype=jnp.int32)
    flat_index = lax.axis_index("ctx") * sub_size + lax.axis_index("sub")
    pages_here = kv_cache.shape[1] // PAGE
    base_pages = pages_here * ctx_size * sub_size // 2
    initial = (
        jnp.full((SPAN, local_heads, per_group), NEG, jnp.float32),
        jnp.zeros((SPAN, local_heads, per_group), jnp.float32),
        jnp.zeros((SPAN, local_heads, per_group, HD), jnp.float32),
    )
    half_rows = kv_cache.shape[1] // 2
    arrived = from_behind(kv_cache[:, half_rows:], "ctx", -(ctx_size // 2))
    is_lower = lax.axis_index("ctx") < ctx_size // 2
    source_flat = flat_index + ctx_size // 2 * sub_size
    working = jnp.where(is_lower, arrived, kv_cache[:, :half_rows])
    first_page = jnp.where(
        is_lower, source_flat * pages_here + pages_here // 2, flat_index * pages_here
    )
    page_total = working.shape[1] // PAGE

    def add_page(page_turn, running):
        page_index = first_page + page_turn
        relative = page_index - base_pages
        counted = jnp.sum((relative >= page_ends).astype(jnp.int32))
        request = jnp.where(relative < 0, REQS, counted)

        def update(partial_value):
            run_max, run_sum, run_out = partial_value
            request_id = jnp.minimum(request, REQS - 1)
            row_start = request_id * QR
            gathered = row_start + offsets
            within = gathered % ctx_rows
            ctx_block = gathered // ctx_rows
            sub_part = within // (head_count * tok_rows)
            head_part = within // tok_rows % head_count
            tok_part = within % tok_rows
            natural = ctx_block * ctx_rows + (head_part * sub_size + sub_part) * tok_rows + tok_part
            query_pos = (page_ends[request_id] + base_pages) * PAGE - QR + natural - row_start
            key_pos = page_index * PAGE + columns
            visible = key_pos[None, :] <= query_pos[:, None]
            page_keys = working[0].reshape(PAGE, local_heads, HD)
            page_values = working[1].reshape(PAGE, local_heads, HD)
            query_rows = lax.dynamic_slice_in_dim(all_queries, row_start, QR, 0)
            scores = (
                jnp.einsum(
                    "qkgd,pkd->qkgp", query_rows, page_keys, preferred_element_type=jnp.float32
                )
                * score_scale
            )
            scores = jnp.where(visible[:, None, None, :], scores, NEG)
            old_max = lax.dynamic_slice_in_dim(run_max, row_start, QR, 0)
            old_sum = lax.dynamic_slice_in_dim(run_sum, row_start, QR, 0)
            old_out = lax.dynamic_slice_in_dim(run_out, row_start, QR, 0)
            new_max = jnp.maximum(old_max, jnp.max(scores, axis=3))
            factor = jnp.exp(old_max - new_max)
            numerators = jnp.exp(scores - new_max[..., None])
            new_sum = old_sum * factor + jnp.sum(numerators, axis=3)
            product = jnp.einsum(
                "qkgp,pkd->qkgd",
                numerators.astype(jnp.bfloat16),
                page_values,
                preferred_element_type=jnp.float32,
            )
            new_out = old_out * factor[..., None] + product
            return (
                lax.dynamic_update_slice_in_dim(run_max, new_max, row_start, 0),
                lax.dynamic_update_slice_in_dim(run_sum, new_sum, row_start, 0),
                lax.dynamic_update_slice_in_dim(run_out, new_out, row_start, 0),
            )

        def unchanged(partial_value):
            return partial_value

        return lax.cond(request < REQS, update, unchanged, running)

    run_max, run_sum, run_out = lax.fori_loop(0, page_total, add_page, initial)
    share = SPAN // (ctx_size * sub_size)
    global_max = lax.pmax(run_max, ("ctx", "sub"))
    factor = jnp.exp(run_max - global_max)
    sums_here, outs_here = (
        lax.psum_scatter(
            (run_sum * factor).astype(jnp.bfloat16), ("ctx", "sub"), scatter_dimension=0, tiled=True
        ).astype(jnp.float32),
        lax.psum_scatter(
            (run_out * factor[..., None]).astype(jnp.bfloat16),
            ("ctx", "sub"),
            scatter_dimension=0,
            tiled=True,
        ).astype(jnp.float32),
    )
    finished = (outs_here / sums_here[..., None]).astype(jnp.bfloat16)
    finished = finished.reshape(share, local_heads * per_group * HD)
    return lax.all_to_all(finished, "head", split_axis=0, concat_axis=1, tiled=True)


def per_device(queries, kv_cache, page_counts):
    ctx_size, sub_size, head_count = lax.axis_size("ctx"), lax.axis_size("sub"), lax.axis_size("head")
    small = (
        ctx_size == REQS == 4
        and head_count == sub_size == 2
        and kv_cache.shape[1] == 2 * PAGE
        and kv_cache.shape[2] % (sub_size * HD) == 0
        and queries.shape[0] % 16 == 0
        and queries.shape[0] * head_count * sub_size == QR
    )
    return (one_request_each if small else queries_to_pages)(queries, kv_cache, page_counts)


def solution(mesh):
    return jax.shard_map(
        per_device,
        mesh=mesh,
        in_specs=(
            P(("grp", "ctx", "head", "sub"), None),
            P(None, ("grp", "ctx", "sub"), "head"),
            P("grp"),
        ),
        out_specs=P(("grp", "ctx", "head", "sub"), None),
        check_vma=False,
    )
```

profile of v0, /device:TPU:17, one launch (start us, length us, event | category | flops | bytes accessed | tf_op | source)
XLA Modules:
  0.0 49.1 jit_solution(6829230361011448139)
XLA Ops:
  0.0 1.9 %collective-permute-start = (bf16[2,512,512]{2,1,0:T(8,128)(2,1)}, bf16[2,512,512]{2,1,0:T(8,128)(2,1)S(1)}, u32[]{:S(2)}, u32[]{:S(2)}) collective-permute-start(bf16[2,512,512]{2,1,0:T(8,128)(2,1)} %own.1), channel_id=1, source_target_pairs={{8,9},{10,11},{9,0},{11,2},{12,13},{14,15},{13,12},{15,14},{24,25}... | collective-permute-start | bytes 3145736 | tf_op jit(solution)/shard_map/ppermute | solution.py:194
  1.9 3.8 %collective-permute-start.1 = (bf16[2,512,512]{2,1,0:T(8,128)(2,1)}, bf16[2,512,512]{2,1,0:T(8,128)(2,1)S(1)}, u32[]{:S(2)}, u32[]{:S(2)}) collective-permute-start(bf16[2,512,512]{2,1,0:T(8,128)(2,1)} %own.1), channel_id=1, source_target_pairs={{8,0},{10,2},{9,12},{11,14},{12,9},{14,11},{24,16},{26,18},{25,28}... | collective-permute-start | bytes 3145736 | tf_op jit(solution)/shard_map/ppermute | solution.py:194
  5.7 1.1 %split.1 = (bf16[16,8192]{1,0:T(8,128)(2,1)S(1)}, bf16[16,8192]{1,0:T(8,128)(2,1)S(1)}) custom-call(bf16[16,16384]{1,0:T(8,128)(2,1)} %queries.1), custom_call_target="tpu_custom_call" | custom-call | tf_op jit(solution)/shard_map/split/pallas_call | solution.py:201
  6.8 1.3 %collective-permute-start.2 = (bf16[16,8192]{1,0:T(8,128)(2,1)S(1)}, bf16[16,8192]{1,0:T(8,128)(2,1)S(1)}, u32[]{:S(2)}, u32[]{:S(2)}) collective-permute-start(bf16[16,8192]{1,0:T(8,128)(2,1)S(1)} %get-tuple-element.11), channel_id=1, source_target_pairs={{0,2},{2,0},{4,11},{6,9},{8,14},{10,12},{12,15},{14,13},{16,18},{1... | collective-permute-start | bytes 786440 | tf_op jit(solution)/shard_map/ppermute | solution.py:194
  8.1 1.3 %collective-permute-start.5 = (bf16[16,8192]{1,0:T(8,128)(2,1)S(1)}, bf16[16,8192]{1,0:T(8,128)(2,1)S(1)}, u32[]{:S(2)}, u32[]{:S(2)}) collective-permute-start(bf16[16,8192]{1,0:T(8,128)(2,1)S(1)} %get-tuple-element.12), channel_id=1, source_target_pairs={{0,0},{2,2},{4,9},{6,11},{8,12},{10,14},{12,13},{14,15},{16,16},{1... | collective-permute-start | bytes 786440 | tf_op jit(solution)/shard_map/ppermute | solution.py:194
  9.4 4.6 %collective-permute-start.3 = (bf16[16,8192]{1,0:T(8,128)(2,1)S(1)}, bf16[16,8192]{1,0:T(8,128)(2,1)S(1)}, u32[]{:S(2)}, u32[]{:S(2)}) collective-permute-start(bf16[16,8192]{1,0:T(8,128)(2,1)S(1)} %get-tuple-element.11), channel_id=1, source_target_pairs={{1,2},{3,0},{5,11},{7,9},{9,14},{11,12},{13,15},{15,13},{17,18},{1... | collective-permute-start | bytes 786440 | tf_op jit(solution)/shard_map/ppermute | solution.py:194
  14.0 2.1 %collective-permute-done.2.refs_0_ = bf16[16,8192]{1,0:T(8,128)(2,1)S(1)} collective-permute-done((bf16[16,8192]{1,0:T(8,128)(2,1)S(1)}, bf16[16,8192]{1,0:T(8,128)(2,1)S(1)}, u32[]{:S(2)}, u32[]{:S(2)}) %collective-permute-start.2) | collective-permute-done | bytes 262176 | tf_op jit(solution)/shard_map/ppermute | solution.py:194
  16.1 4.6 %collective-permute-start.4 = (bf16[16,8192]{1,0:T(8,128)(2,1)S(1)}, bf16[16,8192]{1,0:T(8,128)(2,1)S(1)}, u32[]{:S(2)}, u32[]{:S(2)}) collective-permute-start(bf16[16,8192]{1,0:T(8,128)(2,1)S(1)} %get-tuple-element.12), channel_id=1, source_target_pairs={{1,0},{3,2},{5,9},{7,11},{9,12},{11,14},{13,13},{15,15},{17,16},{1... | collective-permute-start | bytes 786440 | tf_op jit(solution)/shard_map/ppermute | solution.py:194
  20.7 2.4 %collective-permute-done.near = bf16[2,512,512]{2,1,0:T(8,128)(2,1)S(1)} collective-permute-done((bf16[2,512,512]{2,1,0:T(8,128)(2,1)}, bf16[2,512,512]{2,1,0:T(8,128)(2,1)S(1)}, u32[]{:S(2)}, u32[]{:S(2)}) %collective-permute-start) | collective-permute-done | bytes 1048608 | tf_op jit(solution)/shard_map/ppermute | solution.py:194
  23.1 0.3 collective-permute-done.1.far
  23.3 2.3 %gather.1.pages_in = bf16[4,4,2,256,128]{4,3,2,1,0:T(8,128)(2,1)S(1)} custom-call(s32[4]{0:T(128)} %counts.5, bf16[2,512,512]{2,1,0:T(8,128)(2,1)} %own.1, bf16[2,512,512]{2,1,0:T(8,128)(2,1)S(1)} %collective-permute-done.near, bf16[2,512,512]{2,1,0:T(8,128)(2,1)S(1)} %collective-permute-done.1.far, f32[8,128]{1,0:T(8,128)S(1)} %first_here.1.after), custom_call_target="tpu_custom_call" | custom-call | tf_op jit(solution)/shard_map/gather/pallas_call | solution.py:233
  25.6 0.0 collective-permute-done.5.refs_1_
  25.6 3.8 %attend_0.1 = (bf16[16,8192]{1,0:T(8,128)(2,1)S(1)}, bf16[16,8192]{1,0:T(8,128)(2,1)S(1)}) custom-call(s32[4]{0:T(128)} %counts.5, bf16[4,4,2,256,128]{4,3,2,1,0:T(8,128)(2,1)S(1)} %gather.1.pages_in, bf16[16,8192]{1,0:T(8,128)(2,1)S(1)} %collective-permute-done.2.refs_0_, bf16[16,8192]{1,0:T(8,128)(2,1)S(1)} %collective-permute-done.5.refs_1_), custom_call_target="tpu_custom_call" | custom-call | flops 10000000000 | bytes 4194304 | tf_op jit(solution)/shard_map/attend_0/pallas_call | solution.py:247
  29.4 1.3 %collective-permute-start.8 = (bf16[16,8192]{1,0:T(8,128)(2,1)S(1)}, bf16[16,8192]{1,0:T(8,128)(2,1)S(1)}, u32[]{:S(2)}, u32[]{:S(2)}) collective-permute-start(bf16[16,8192]{1,0:T(8,128)(2,1)S(1)} %get-tuple-element.13.refs_2_), channel_id=1, source_target_pairs={{2,0},{0,2},{11,4},{9,6},{14,8},{12,10},{15,12},{13,14},{18,16},{1... | collective-permute-start | bytes 786440 | tf_op jit(solution)/shard_map/ppermute | solution.py:194
  30.7 1.3 %collective-permute-start.9 = (bf16[16,8192]{1,0:T(8,128)(2,1)S(1)}, bf16[16,8192]{1,0:T(8,128)(2,1)S(1)}, u32[]{:S(2)}, u32[]{:S(2)}) collective-permute-start(bf16[16,8192]{1,0:T(8,128)(2,1)S(1)} %get-tuple-element.16), channel_id=1, source_target_pairs={{0,0},{2,2},{9,4},{11,6},{12,8},{14,10},{13,12},{15,14},{16,16},{1... | collective-permute-start | bytes 786440 | tf_op jit(solution)/shard_map/ppermute | solution.py:194
  32.0 0.0 collective-permute-done.3.refs_0_
  32.0 0.0 collective-permute-done.4.refs_1_
  32.0 4.2 %attend_1.1 = (bf16[16,8192]{1,0:T(8,128)(2,1)S(1)}, bf16[16,8192]{1,0:T(8,128)(2,1)S(1)}) custom-call(s32[4]{0:T(128)} %counts.5, bf16[4,4,2,256,128]{4,3,2,1,0:T(8,128)(2,1)S(1)} %gather.1.pages_in, bf16[16,8192]{1,0:T(8,128)(2,1)S(1)} %collective-permute-done.3.refs_0_, bf16[16,8192]{1,0:T(8,128)(2,1)S(1)} %collective-permute-done.4.refs_1_, ...), custom_call_target="tpu_custom_call" | custom-call | flops 10000000000 | bytes 4194304 | tf_op jit(solution)/shard_map/attend_1/pallas_call | solution.py:247
  36.2 1.9 %collective-permute-start.6 = (bf16[16,8192]{1,0:T(8,128)(2,1)S(1)}, bf16[16,8192]{1,0:T(8,128)(2,1)S(1)}, u32[]{:S(2)}, u32[]{:S(2)}) collective-permute-start(bf16[16,8192]{1,0:T(8,128)(2,1)S(1)} %get-tuple-element.14), channel_id=1, source_target_pairs={{2,1},{0,3},{11,5},{9,7},{14,9},{12,11},{15,13},{13,15},{18,17},{1... | collective-permute-start | bytes 786440 | tf_op jit(solution)/shard_map/ppermute | solution.py:194
  38.2 1.9 %collective-permute-start.7 = (bf16[16,8192]{1,0:T(8,128)(2,1)S(1)}, bf16[16,8192]{1,0:T(8,128)(2,1)S(1)}, u32[]{:S(2)}, u32[]{:S(2)}) collective-permute-start(bf16[16,8192]{1,0:T(8,128)(2,1)S(1)} %get-tuple-element.15), channel_id=1, source_target_pairs={{0,1},{2,3},{9,5},{11,7},{12,9},{14,11},{13,13},{15,15},{16,17},{1... | collective-permute-start | bytes 786440 | tf_op jit(solution)/shard_map/ppermute | solution.py:194
  40.1 0.0 collective-permute-done.8.refs_0_
  40.1 0.0 collective-permute-done.9.refs_1_
  40.1 4.7 %collective-permute-done.6.refs_0_ = bf16[16,8192]{1,0:T(8,128)(2,1)S(1)} collective-permute-done((bf16[16,8192]{1,0:T(8,128)(2,1)S(1)}, bf16[16,8192]{1,0:T(8,128)(2,1)S(1)}, u32[]{:S(2)}, u32[]{:S(2)}) %collective-permute-start.6) | collective-permute-done | bytes 262176 | tf_op jit(solution)/shard_map/ppermute | solution.py:194
  44.8 3.3 %collective-permute-done.7.refs_1_ = bf16[16,8192]{1,0:T(8,128)(2,1)S(1)} collective-permute-done((bf16[16,8192]{1,0:T(8,128)(2,1)S(1)}, bf16[16,8192]{1,0:T(8,128)(2,1)S(1)}, u32[]{:S(2)}, u32[]{:S(2)}) %collective-permute-start.7) | collective-permute-done | bytes 262176 | tf_op jit(solution)/shard_map/ppermute | solution.py:194
  48.2 0.8 %join_1.1 = bf16[16,16384]{1,0:T(8,128)(2,1)} custom-call(bf16[16,8192]{1,0:T(8,128)(2,1)S(1)} %collective-permute-done.6.refs_0_, bf16[16,8192]{1,0:T(8,128)(2,1)S(1)} %collective-permute-done.7.refs_1_, bf16[16,16384]{1,0:T(8,128)(2,1)} %join_0.1.refs_2_), custom_call_target="tpu_custom_call", output_to_operand_aliasing={{}: (2, {})} | custom-call | tf_op jit(solution)/shard_map/join_1/pallas_call | solution.py:263
  (2 shorter events, 0.0 us)
Async XLA Ops:
  0.0 23.1 %collective-permute-start = (bf16[2,512,512]{2,1,0:T(8,128)(2,1)}, bf16[2,512,512]{2,1,0:T(8,128)(2,1)S(1)}, u32[]{:S(2)}, u32[]{:S(2)}) collective-permute-start(bf16[2,512,512]{2,1,0:T(8,128)(2,1)} %own.1), channel_id=1, source_target_pairs={{8,9},{10,11},{9,0},{11,2},{12,13},{14,15},{13,12},{15,14},{24,25}... | collective-permute-start | bytes 3145736 | tf_op jit(solution)/shard_map/ppermute | solution.py:194
  1.9 21.4 %collective-permute-start.1 = (bf16[2,512,512]{2,1,0:T(8,128)(2,1)}, bf16[2,512,512]{2,1,0:T(8,128)(2,1)S(1)}, u32[]{:S(2)}, u32[]{:S(2)}) collective-permute-start(bf16[2,512,512]{2,1,0:T(8,128)(2,1)} %own.1), channel_id=1, source_target_pairs={{8,0},{10,2},{9,12},{11,14},{12,9},{14,11},{24,16},{26,18},{25,28}... | collective-permute-start | bytes 3145736 | tf_op jit(solution)/shard_map/ppermute | solution.py:194
  6.8 9.3 %collective-permute-start.2 = (bf16[16,8192]{1,0:T(8,128)(2,1)S(1)}, bf16[16,8192]{1,0:T(8,128)(2,1)S(1)}, u32[]{:S(2)}, u32[]{:S(2)}) collective-permute-start(bf16[16,8192]{1,0:T(8,128)(2,1)S(1)} %get-tuple-element.11), channel_id=1, source_target_pairs={{0,2},{2,0},{4,11},{6,9},{8,14},{10,12},{12,15},{14,13},{16,18},{1... | collective-permute-start | bytes 786440 | tf_op jit(solution)/shard_map/ppermute | solution.py:194
  8.1 17.6 %collective-permute-start.5 = (bf16[16,8192]{1,0:T(8,128)(2,1)S(1)}, bf16[16,8192]{1,0:T(8,128)(2,1)S(1)}, u32[]{:S(2)}, u32[]{:S(2)}) collective-permute-start(bf16[16,8192]{1,0:T(8,128)(2,1)S(1)} %get-tuple-element.12), channel_id=1, source_target_pairs={{0,0},{2,2},{4,9},{6,11},{8,12},{10,14},{12,13},{14,15},{16,16},{1... | collective-permute-start | bytes 786440 | tf_op jit(solution)/shard_map/ppermute | solution.py:194
  9.4 22.7 %collective-permute-start.3 = (bf16[16,8192]{1,0:T(8,128)(2,1)S(1)}, bf16[16,8192]{1,0:T(8,128)(2,1)S(1)}, u32[]{:S(2)}, u32[]{:S(2)}) collective-permute-start(bf16[16,8192]{1,0:T(8,128)(2,1)S(1)} %get-tuple-element.11), channel_id=1, source_target_pairs={{1,2},{3,0},{5,11},{7,9},{9,14},{11,12},{13,15},{15,13},{17,18},{1... | collective-permute-start | bytes 786440 | tf_op jit(solution)/shard_map/ppermute | solution.py:194
  16.1 16.0 %collective-permute-start.4 = (bf16[16,8192]{1,0:T(8,128)(2,1)S(1)}, bf16[16,8192]{1,0:T(8,128)(2,1)S(1)}, u32[]{:S(2)}, u32[]{:S(2)}) collective-permute-start(bf16[16,8192]{1,0:T(8,128)(2,1)S(1)} %get-tuple-element.12), channel_id=1, source_target_pairs={{1,0},{3,2},{5,9},{7,11},{9,12},{11,14},{13,13},{15,15},{17,16},{1... | collective-permute-start | bytes 786440 | tf_op jit(solution)/shard_map/ppermute | solution.py:194
  29.4 10.7 %collective-permute-start.8 = (bf16[16,8192]{1,0:T(8,128)(2,1)S(1)}, bf16[16,8192]{1,0:T(8,128)(2,1)S(1)}, u32[]{:S(2)}, u32[]{:S(2)}) collective-permute-start(bf16[16,8192]{1,0:T(8,128)(2,1)S(1)} %get-tuple-element.13.refs_2_), channel_id=1, source_target_pairs={{2,0},{0,2},{11,4},{9,6},{14,8},{12,10},{15,12},{13,14},{18,16},{1... | collective-permute-start | bytes 786440 | tf_op jit(solution)/shard_map/ppermute | solution.py:194
  30.7 9.4 %collective-permute-start.9 = (bf16[16,8192]{1,0:T(8,128)(2,1)S(1)}, bf16[16,8192]{1,0:T(8,128)(2,1)S(1)}, u32[]{:S(2)}, u32[]{:S(2)}) collective-permute-start(bf16[16,8192]{1,0:T(8,128)(2,1)S(1)} %get-tuple-element.16), channel_id=1, source_target_pairs={{0,0},{2,2},{9,4},{11,6},{12,8},{14,10},{13,12},{15,14},{16,16},{1... | collective-permute-start | bytes 786440 | tf_op jit(solution)/shard_map/ppermute | solution.py:194
  36.2 8.6 %collective-permute-start.6 = (bf16[16,8192]{1,0:T(8,128)(2,1)S(1)}, bf16[16,8192]{1,0:T(8,128)(2,1)S(1)}, u32[]{:S(2)}, u32[]{:S(2)}) collective-permute-start(bf16[16,8192]{1,0:T(8,128)(2,1)S(1)} %get-tuple-element.14), channel_id=1, source_target_pairs={{2,1},{0,3},{11,5},{9,7},{14,9},{12,11},{15,13},{13,15},{18,17},{1... | collective-permute-start | bytes 786440 | tf_op jit(solution)/shard_map/ppermute | solution.py:194
  38.2 10.0 %collective-permute-start.7 = (bf16[16,8192]{1,0:T(8,128)(2,1)S(1)}, bf16[16,8192]{1,0:T(8,128)(2,1)S(1)}, u32[]{:S(2)}, u32[]{:S(2)}) collective-permute-start(bf16[16,8192]{1,0:T(8,128)(2,1)S(1)} %get-tuple-element.15), channel_id=1, source_target_pairs={{0,1},{2,3},{9,5},{11,7},{12,9},{14,11},{13,13},{15,15},{16,17},{1... | collective-permute-start | bytes 786440 | tf_op jit(solution)/shard_map/ppermute | solution.py:194
where the time goes:
time: 49.7 us; the launch traced here: 49.1 us
  starting transfers between devices  23.9 us (48%)
  waiting for transfers between devices  12.8 us (26%)
  Pallas kernels  12.1 us (24%)
    ppermute x10, starting transfers between devices, moved(): lax.ppermute(array, ('ctx', 'head', 'sub'), [(flat(a), flat(b)) for a, b...  23.9 us
    ppermute x10, waiting for transfers between devices, moved(): lax.ppermute(array, ('ctx', 'head', 'sub'), [(flat(a), flat(b)) for a, b...  12.8 us
    pallas_call x2, Pallas kernels, one_request_each(): pl.pallas_call(functools.partial(attend_kernel, low_ctx, sub_size, keys,...  7.93 us
    pallas_call x1, Pallas kernels, one_request_each(): pl.pallas_call(functools.partial(gather_kernel, low_ctx), out_shape=pltpu...  2.26 us
    pallas_call x1, Pallas kernels, one_request_each(): pl.pallas_call(split_kernel, out_shape=[q_piece] * head_count, in_specs=[...  1.06 us
  transfers between devices with their start and end apart: 10, of which 5 were waited for; matrix products, arithmetic and copies ran while one was open for 0% of the time, Pallas kernels for 23%

commit v1 on v0

--- a/solution.py
+++ b/solution.py
@@ -62,83 +62,89 @@
     return found
 
 
-def gather_kernel(low_ctx, counts, own, near, far, after, out, sems):
+def pages_of(low_ctx, counts, most_pages):
+    request = own_request(low_ctx)
+    start = jnp.int32(0)
+    for r in range(REQS):
+        start = start + jnp.where(r < request, counts[r], 0)
+    count = jnp.where(request >= 0, counts[jnp.maximum(request, 0)], 0)
+    home_pair = jnp.where(request == 0, -1, request)
+    near_pair = jnp.where(request == 0, 1, request ^ 1)
+    for p in range(most_pages):
+        page = start + p
+        pair = page // 2
+        which = jnp.where(pair == home_pair, 0, jnp.where(pair == near_pair, 1, 2))
+        yield p, p < count, which, pl.ds(pl.multiple_of(lax.rem(page, 2) * PAGE, PAGE), PAGE)
+
+
+def gather_home_kernel(low_ctx, counts, counts_in, own, after, out, counts_out, sems, counts_sem):
     local_kv, most_pages = out.shape[:2]
-    request = own_request(low_ctx)
-
-    @pl.when(request >= 0)
-    def _():
-        start = jnp.int32(0)
-        for r in range(REQS):
-            start = start + jnp.where(r < request, counts[r], 0)
-        count = counts[request]
-        near_pair = jnp.where(request == 0, 1, request ^ 1)
-        home_pair = jnp.where(request == 0, -1, request)
-
-        def of_page(p):
-            page = start + p
-            page_rows = pl.ds(pl.multiple_of(lax.rem(page, 2) * PAGE, PAGE), PAGE)
-            return page // 2, page_rows
-
-        def home_copies(p, page_rows):
-            return [
-                pltpu.make_async_copy(own.at[i, page_rows, pl.ds(g * HD, HD)], out.at[g, p, i], sems.at[g, p, i])
-                for g in range(local_kv) for i in range(2)
-            ]
-
-        for p in range(most_pages):
-            pair, page_rows = of_page(p)
-            @pl.when((p < count) & (pair == home_pair))
+    counts_copy = pltpu.make_async_copy(counts_in, counts_out, counts_sem)
+    counts_copy.start()
+    plan = [
+        (here & (which == 0), [
+            pltpu.make_async_copy(own.at[i, rows, pl.ds(g * HD, HD)], out.at[g, p, i], sems.at[g, p, i])
+            for g in range(local_kv) for i in range(2)
+        ])
+        for p, here, which, rows in pages_of(low_ctx, counts, most_pages)
+    ]
+    for here, copies in plan:
+        @pl.when(here)
+        def _():
+            for copy in copies:
+                copy.start()
+    for here, copies in plan:
+        @pl.when(here)
+        def _():
+            for copy in copies:
+                copy.wait()
+    counts_copy.wait()
+
+
+def gather_rest_kernel(low_ctx, counts, near, far, home, out):
+    local_kv, most_pages = out.shape[:2]
+    for p, here, which, rows in pages_of(low_ctx, counts, most_pages):
+        for n, ref in enumerate((near, far)):
+            @pl.when(here & (which == n + 1))
             def _():
-                for copy in home_copies(p, page_rows):
-                    copy.start()
-        for p in range(most_pages):
-            pair, page_rows = of_page(p)
-            for ref, chosen in ((near, pair == near_pair), (far, (pair != near_pair) & (pair != home_pair))):
-                @pl.when((p < count) & chosen)
-                def _():
-                    for g in range(local_kv):
-                        for i in range(2):
-                            out[g, p, i] = ref[i, page_rows, g * HD:(g + 1) * HD]
-        for p in range(most_pages):
-            pair, page_rows = of_page(p)
-            @pl.when((p < count) & (pair == home_pair))
-            def _():
-                for copy in home_copies(p, page_rows):
-                    copy.wait()
-
-
-def attend_kernel(low_ctx, sub_count, keys, waits, counts, pages_in, *refs):
-    queries, outs = refs[:len(keys)], refs[len(keys) + waits:]
+                for g in range(local_kv):
+                    for i in range(2):
+                        out[g, p, i] = ref[i, rows, g * HD:(g + 1) * HD]
+
+
+def attend_kernel(low_ctx, sub_count, groups, waits, counts, pages_in, *refs):
+    keys = [key for group in groups for key in group]
+    queries, outs = dict(zip(keys, refs)), dict(zip(keys, refs[len(keys) + waits:]))
     head = lax.axis_index("head")
-    tokens, width = queries[0].shape
+    tokens, width = refs[0].shape
     local_kv, most_pages = pages_in.shape[:2]
     span = width // local_kv
     per_group = span // HD
     piece_rows = per_group * tokens
-    rows = len(keys) * piece_rows
-
-    def attend(pages):
+    rows = len(groups[0]) * piece_rows
+
+    def visible_of(group):
         row = lax.broadcasted_iota(jnp.int32, (rows, PAGE), 0)
         token = lax.rem(row, tokens)
-        for i, (step, source) in enumerate(keys):
+        for i, (step, source) in enumerate(group):
             first_token = ((head ^ step) * sub_count + source) * tokens
             token = jnp.where(row // piece_rows == i, token + first_token, token)
-        column = lax.broadcasted_iota(jnp.int32, (rows, PAGE), 1)
-        visible = column <= PAGE - QR + token
-
-        def scores_of(g):
-            q_blocks = [ref[:, g * span:(g + 1) * span] for ref in queries]
+        return lax.broadcasted_iota(jnp.int32, (rows, PAGE), 1) <= PAGE - QR + token
+
+    def attend(pages):
+        def scores_of(group, g):
+            q_blocks = [queries[key][:, g * span:(g + 1) * span] for key in group]
             q_rows = jnp.concatenate([q[:, j * HD:(j + 1) * HD] for q in q_blocks for j in range(per_group)], axis=0)
             for p in range(pages):
                 scores = lax.dot_general(
                     q_rows, pages_in[g, p, 0], (((1,), (1,)), ((), ())), preferred_element_type=jnp.float32
                 )
-                yield jnp.where(visible, scores, NEG) if p == pages - 1 else scores
-
-        scores = list(scores_of(0))
-        for g in range(local_kv):
-            following = scores_of(g + 1) if g + 1 < local_kv else iter(())
+                yield jnp.where(visible_of(group), scores, NEG) if p == pages - 1 else scores
+
+        units = [(group, g) for group in groups for g in range(local_kv)]
+        scores = list(scores_of(*units[0]))
+        for n, (group, g) in enumerate(units):
+            following = scores_of(*units[n + 1]) if n + 1 < len(units) else iter(())
             later = []
             top = jnp.max(functools.reduce(jnp.maximum, scores), axis=1, keepdims=True)
             totals, product = None, None
@@ -152,9 +158,9 @@
                 product = part if p == 0 else product + part
             totals = jnp.sum(totals, axis=1, keepdims=True)
             done = (product / totals).astype(jnp.bfloat16)
-            for i, out in enumerate(outs):
+            for i, key in enumerate(group):
                 start = i * piece_rows
-                out[:, g * span:(g + 1) * span] = jnp.concatenate(
+                outs[key][:, g * span:(g + 1) * span] = jnp.concatenate(
                     [done[start + j * tokens:start + (j + 1) * tokens] for j in range(per_group)], axis=1
                 )
             scores = later
@@ -211,7 +217,23 @@
         (step, s): [((r, h, s), worker(r, h ^ step)) for r in range(ctx_size) for h in heads]
         for s in range(sub_size) for step in heads[::-1]
     }
-    q_in = {key: moved(q_out[key[0]], pairs) for key, pairs in routes.items()}
+    first, last = list(routes)[0], list(routes)[-1]
+    q_in = {first: moved(q_out[first[0]], routes[first])}
+    home, counts = pl.pallas_call(
+        functools.partial(gather_home_kernel, low_ctx),
+        out_shape=[
+            pltpu.VMEM((local_kv, most_pages, 2, PAGE, HD), kv_cache.dtype),
+            pltpu.VMEM(page_counts.shape, page_counts.dtype),
+        ],
+        in_specs=[pl.BlockSpec(memory_space=pltpu.SMEM)] + [anywhere] * 3,
+        out_specs=[anywhere] * 2,
+        scratch_shapes=[pltpu.SemaphoreType.DMA((local_kv, most_pages, 2)), pltpu.SemaphoreType.DMA],
+        compiler_params=pltpu.CompilerParams(vmem_limit_bytes=2**20),
+        name="gather_home",
+    )(hbm(page_counts), hbm(page_counts), hbm(kv_cache), vmem(q_in[first]))
+    q_last, counts = lax.optimization_barrier((q_out[last[0]], counts))
+    for key in list(routes)[1:]:
+        q_in[key] = moved(q_last if key == last else q_out[key[0]], routes[key])
 
     pairs = [(low_ctx + n // 2, n % 2) for n in range(4)]
     workers = worker_places(low_ctx)
@@ -222,37 +244,29 @@
             [(pairs[0], workers[0]), (pairs[1], workers[2]), (pairs[2], workers[1])],
         )
     )
-    first_here = pl.pallas_call(
-        lambda *refs: None,
-        out_shape=pltpu.VMEM((8, HD), jnp.float32),
-        in_specs=[anywhere],
-        out_specs=anywhere,
+    gathered = pl.pallas_call(
+        functools.partial(gather_rest_kernel, low_ctx),
+        out_shape=pltpu.VMEM(home.shape, home.dtype),
+        in_specs=[pl.BlockSpec(memory_space=pltpu.SMEM)] + [in_vmem] * 2 + [anywhere],
+        out_specs=in_vmem,
+        input_output_aliases={3: 0},
         compiler_params=pltpu.CompilerParams(vmem_limit_bytes=2**20),
-        name="first_here",
-    )(vmem(q_in[list(routes)[0]]))
-    gathered = pl.pallas_call(
-        functools.partial(gather_kernel, low_ctx),
-        out_shape=pltpu.VMEM((local_kv, most_pages, 2, PAGE, HD), kv_cache.dtype),
-        in_specs=[pl.BlockSpec(memory_space=pltpu.SMEM), anywhere] + [in_vmem] * 2 + [anywhere],
-        out_specs=in_vmem,
-        scratch_shapes=[pltpu.SemaphoreType.DMA((local_kv, most_pages, 2))],
-        compiler_params=pltpu.CompilerParams(vmem_limit_bytes=2**20),
-        name="gather",
-    )(hbm(page_counts), hbm(kv_cache), vmem(near), vmem(far), vmem(first_here))
-
+        name="gather_rest",
+    )(vmem(counts), vmem(near), vmem(far), vmem(home))
+
+    groups = [[(step, s) for step in heads[::-1]] for s in range(sub_size)]
     back = {}
     after = []
-    groups = [[(step, s) for step in heads[::-1]] for s in range(sub_size)]
     for keys in groups:
         outs = pl.pallas_call(
-            functools.partial(attend_kernel, low_ctx, sub_size, keys, len(after)),
+            functools.partial(attend_kernel, low_ctx, sub_size, [keys], len(after)),
             out_shape=[q_piece] * len(keys),
             in_specs=[pl.BlockSpec(memory_space=pltpu.SMEM)] + [in_vmem] * (1 + len(keys)) + [anywhere] * len(after),
             out_specs=[in_vmem] * len(keys),
             compiler_params=pltpu.CompilerParams(vmem_limit_bytes=12 * 2**20),
             cost_estimate=pl.CostEstimate(flops=10**10, bytes_accessed=2**22, transcendentals=10**6),
             name=f"attend_{keys[0][1]}",
-        )(hbm(page_counts), vmem(gathered), *[vmem(q_in[key]) for key in keys], *after)
+        )(vmem(counts), vmem(gathered), *[vmem(q_in[key]) for key in keys], *after)
         for key, out in zip(keys, outs):
             back[key] = moved(out, [(b, a) for a, b in routes[key]])
         after = [outs[0]]

time: 49.7 us -> 48.9 us (0.984)
  the two profiles are of different devices: /device:TPU:17 before, /device:TPU:7 now
where the time goes in v1:
time: 48.9 us; the launch traced here: 48.5 us
  waiting for transfers between devices  25 us (51%)
  starting transfers between devices  17.5 us (36%)
  Pallas kernels  5.59 us (11%)
    ppermute x10, waiting for transfers between devices, moved(): lax.ppermute(array, ('ctx', 'head', 'sub'), [(flat(a), flat(b)) for a, b...  25 us
    ppermute x10, starting transfers between devices, moved(): lax.ppermute(array, ('ctx', 'head', 'sub'), [(flat(a), flat(b)) for a, b...  17.5 us
    pallas_call x1, Pallas kernels, one_request_each(): pl.pallas_call(functools.partial(gather_home_kernel, low_ctx), out_shape=...  1.7 us
    pallas_call x2, Pallas kernels, one_request_each(): pl.pallas_call(functools.partial(attend_kernel, low_ctx, sub_size, [keys]...  1.35 us
    pallas_call x1, Pallas kernels, one_request_each(): pl.pallas_call(split_kernel, out_shape=[q_piece] * head_count, in_specs=[...  1.06 us
  transfers between devices with their start and end apart: 10, of which 1 were waited for; matrix products, arithmetic and copies ran while one was open for 0% of the time, Pallas kernels for 10%

profile of v1, /device:TPU:7, one launch (start us, length us, event | category | flops | bytes accessed | tf_op | source)
XLA Modules:
  0.0 48.5 jit_solution(13955391849683958116)
XLA Ops:
  0.0 0.7 %collective-permute-start.1 = (bf16[2,512,512]{2,1,0:T(8,128)(2,1)}, bf16[2,512,512]{2,1,0:T(8,128)(2,1)S(1)}, u32[]{:S(2)}, u32[]{:S(2)}) collective-permute-start(bf16[2,512,512]{2,1,0:T(8,128)(2,1)} %own.1), channel_id=1, source_target_pairs={{8,9},{10,11},{9,0},{11,2},{12,13},{14,15},{13,12},{15,14},{24,25}... | collective-permute-start | bytes 3145736 | tf_op jit(solution)/shard_map/ppermute | solution.py:200
  0.7 0.7 %collective-permute-start.2 = (bf16[2,512,512]{2,1,0:T(8,128)(2,1)}, bf16[2,512,512]{2,1,0:T(8,128)(2,1)S(1)}, u32[]{:S(2)}, u32[]{:S(2)}) collective-permute-start(bf16[2,512,512]{2,1,0:T(8,128)(2,1)} %own.1), channel_id=1, source_target_pairs={{8,0},{10,2},{9,12},{11,14},{12,9},{14,11},{24,16},{26,18},{25,28}... | collective-permute-start | bytes 3145736 | tf_op jit(solution)/shard_map/ppermute | solution.py:200
  1.5 1.1 %split.1 = (bf16[16,8192]{1,0:T(8,128)(2,1)S(1)}, bf16[16,8192]{1,0:T(8,128)(2,1)S(1)}) custom-call(bf16[16,16384]{1,0:T(8,128)(2,1)} %queries.1), custom_call_target="tpu_custom_call" | custom-call | tf_op jit(solution)/shard_map/split/pallas_call | solution.py:207
  2.5 0.7 %collective-permute-start = (bf16[16,8192]{1,0:T(8,128)(2,1)S(1)}, bf16[16,8192]{1,0:T(8,128)(2,1)S(1)}, u32[]{:S(2)}, u32[]{:S(2)}) collective-permute-start(bf16[16,8192]{1,0:T(8,128)(2,1)S(1)} %get-tuple-element.16), channel_id=1, source_target_pairs={{0,2},{2,0},{4,11},{6,9},{8,14},{10,12},{12,15},{14,13},{16,18},{1... | collective-permute-start | bytes 786440 | tf_op jit(solution)/shard_map/ppermute | solution.py:200
  3.2 0.7 %collective-permute-start.5 = (bf16[16,8192]{1,0:T(8,128)(2,1)S(1)}, bf16[16,8192]{1,0:T(8,128)(2,1)S(1)}, u32[]{:S(2)}, u32[]{:S(2)}) collective-permute-start(bf16[16,8192]{1,0:T(8,128)(2,1)S(1)} %get-tuple-element.20), channel_id=1, source_target_pairs={{0,0},{2,2},{4,9},{6,11},{8,12},{10,14},{12,13},{14,15},{16,16},{1... | collective-permute-start | bytes 786440 | tf_op jit(solution)/shard_map/ppermute | solution.py:200
  3.9 6.6 %collective-permute-start.3 = (bf16[16,8192]{1,0:T(8,128)(2,1)S(1)}, bf16[16,8192]{1,0:T(8,128)(2,1)S(1)}, u32[]{:S(2)}, u32[]{:S(2)}) collective-permute-start(bf16[16,8192]{1,0:T(8,128)(2,1)S(1)} %get-tuple-element.16), channel_id=1, source_target_pairs={{1,2},{3,0},{5,11},{7,9},{9,14},{11,12},{13,15},{15,13},{17,18},{1... | collective-permute-start | bytes 786440 | tf_op jit(solution)/shard_map/ppermute | solution.py:200
  10.5 0.0 collective-permute-done.after.refs_0_
  10.5 1.7 %gather_home.1 = (bf16[4,4,2,256,128]{4,3,2,1,0:T(8,128)(2,1)S(1)}, s32[4]{0:T(128)S(1)}) custom-call(s32[4]{0:T(128)} %counts_in.1, s32[4]{0:T(128)} %counts_in.1, bf16[2,512,512]{2,1,0:T(8,128)(2,1)} %own.1, bf16[16,8192]{1,0:T(8,128)(2,1)S(1)} %collective-permute-done.after.refs_0_), custom_call_target="tpu_custom_call" | custom-call | tf_op jit(solution)/shard_map/gather_home/pallas_call | solution.py:222
  12.2 4.2 %collective-permute-start.4 = (bf16[16,8192]{1,0:T(8,128)(2,1)S(1)}, bf16[16,8192]{1,0:T(8,128)(2,1)S(1)}, u32[]{:S(2)}, u32[]{:S(2)}) collective-permute-start(bf16[16,8192]{1,0:T(8,128)(2,1)S(1)} %get-tuple-element.20), channel_id=1, source_target_pairs={{1,0},{3,2},{5,9},{7,11},{9,12},{11,14},{13,13},{15,15},{17,16},{1... | collective-permute-start | bytes 786440 | tf_op jit(solution)/shard_map/ppermute | solution.py:200
  16.4 0.0 collective-permute-done.1.near
  16.4 0.0 collective-permute-done.2.far
  16.4 0.6 %gather_rest.1.pages_in = bf16[4,4,2,256,128]{4,3,2,1,0:T(8,128)(2,1)S(1)} custom-call(s32[4]{0:T(128)S(1)} %get-tuple-element.18.counts, bf16[2,512,512]{2,1,0:T(8,128)(2,1)S(1)} %collective-permute-done.1.near, bf16[2,512,512]{2,1,0:T(8,128)(2,1)S(1)} %collective-permute-done.2.far, ...), custom_call_target="tpu_custom_call", output_to_operand_aliasing={{}: (3, {})} | custom-call | tf_op jit(solution)/shard_map/gather_rest/pallas_call | solution.py:247
  17.1 0.0 collective-permute-done.5.refs_1_
  17.1 0.6 %attend_0.1 = (bf16[16,8192]{1,0:T(8,128)(2,1)S(1)}, bf16[16,8192]{1,0:T(8,128)(2,1)S(1)}) custom-call(s32[4]{0:T(128)S(1)} %get-tuple-element.18.counts, bf16[4,4,2,256,128]{4,3,2,1,0:T(8,128)(2,1)S(1)} %gather_rest.1.pages_in, bf16[16,8192]{1,0:T(8,128)(2,1)S(1)} %collective-permute-done.after.refs_0_, bf16[16,8192]{1,0:T(8,128)(2,1)S(1)} %collective-permute-done.5.refs_1_), custom_call_target="tpu_custom_call" | custom-call | flops 10000000000 | bytes 4194304 | tf_op jit(solution)/shard_map/attend_0/pallas_call | solution.py:261
  17.7 0.7 %collective-permute-start.8 = (bf16[16,8192]{1,0:T(8,128)(2,1)S(1)}, bf16[16,8192]{1,0:T(8,128)(2,1)S(1)}, u32[]{:S(2)}, u32[]{:S(2)}) collective-permute-start(bf16[16,8192]{1,0:T(8,128)(2,1)S(1)} %get-tuple-element.21.refs_2_), channel_id=1, source_target_pairs={{2,0},{0,2},{11,4},{9,6},{14,8},{12,10},{15,12},{13,14},{18,16},{1... | collective-permute-start | bytes 786440 | tf_op jit(solution)/shard_map/ppermute | solution.py:200
  18.3 0.7 %collective-permute-start.9 = (bf16[16,8192]{1,0:T(8,128)(2,1)S(1)}, bf16[16,8192]{1,0:T(8,128)(2,1)S(1)}, u32[]{:S(2)}, u32[]{:S(2)}) collective-permute-start(bf16[16,8192]{1,0:T(8,128)(2,1)S(1)} %get-tuple-element.24), channel_id=1, source_target_pairs={{0,0},{2,2},{9,4},{11,6},{12,8},{14,10},{13,12},{15,14},{16,16},{1... | collective-permute-start | bytes 786440 | tf_op jit(solution)/shard_map/ppermute | solution.py:200
  19.0 0.0 collective-permute-done.3.refs_0_
  19.0 0.0 collective-permute-done.4.refs_1_
  19.1 0.8 %attend_1.1 = (bf16[16,8192]{1,0:T(8,128)(2,1)S(1)}, bf16[16,8192]{1,0:T(8,128)(2,1)S(1)}) custom-call(s32[4]{0:T(128)S(1)} %get-tuple-element.18.counts, bf16[4,4,2,256,128]{4,3,2,1,0:T(8,128)(2,1)S(1)} %gather_rest.1.pages_in, bf16[16,8192]{1,0:T(8,128)(2,1)S(1)} %collective-permute-done.3.refs_0_, bf16[16,8192]{1,0:T(8,128)(2,1)S(1)} %collective-permute-done.4.refs_1_, ...), custom_call_target="tpu_custom_call" | custom-call | flops 10000000000 | bytes 4194304 | tf_op jit(solution)/shard_map/attend_1/pallas_call | solution.py:261
  19.8 1.3 %collective-permute-start.6 = (bf16[16,8192]{1,0:T(8,128)(2,1)S(1)}, bf16[16,8192]{1,0:T(8,128)(2,1)S(1)}, u32[]{:S(2)}, u32[]{:S(2)}) collective-permute-start(bf16[16,8192]{1,0:T(8,128)(2,1)S(1)} %get-tuple-element.22), channel_id=1, source_target_pairs={{2,1},{0,3},{11,5},{9,7},{14,9},{12,11},{15,13},{13,15},{18,17},{1... | collective-permute-start | bytes 786440 | tf_op jit(solution)/shard_map/ppermute | solution.py:200
  21.1 1.3 %collective-permute-start.7 = (bf16[16,8192]{1,0:T(8,128)(2,1)S(1)}, bf16[16,8192]{1,0:T(8,128)(2,1)S(1)}, u32[]{:S(2)}, u32[]{:S(2)}) collective-permute-start(bf16[16,8192]{1,0:T(8,128)(2,1)S(1)} %get-tuple-element.23), channel_id=1, source_target_pairs={{0,1},{2,3},{9,5},{11,7},{12,9},{14,11},{13,13},{15,15},{16,17},{1... | collective-permute-start | bytes 786440 | tf_op jit(solution)/shard_map/ppermute | solution.py:200
  22.4 0.0 collective-permute-done.8.refs_0_
  22.5 0.0 collective-permute-done.9.refs_1_
  22.5 25.0 %collective-permute-done.6.refs_0_ = bf16[16,8192]{1,0:T(8,128)(2,1)S(1)} collective-permute-done((bf16[16,8192]{1,0:T(8,128)(2,1)S(1)}, bf16[16,8192]{1,0:T(8,128)(2,1)S(1)}, u32[]{:S(2)}, u32[]{:S(2)}) %collective-permute-start.6) | collective-permute-done | bytes 262176 | tf_op jit(solution)/shard_map/ppermute | solution.py:200
  47.5 0.0 collective-permute-done.7.refs_1_
  47.5 0.8 %join_1.1 = bf16[16,16384]{1,0:T(8,128)(2,1)} custom-call(bf16[16,8192]{1,0:T(8,128)(2,1)S(1)} %collective-permute-done.6.refs_0_, bf16[16,8192]{1,0:T(8,128)(2,1)S(1)} %collective-permute-done.7.refs_1_, bf16[16,16384]{1,0:T(8,128)(2,1)} %join_0.1.refs_2_), custom_call_target="tpu_custom_call", output_to_operand_aliasing={{}: (2, {})} | custom-call | tf_op jit(solution)/shard_map/join_1/pallas_call | solution.py:277
  (1 shorter events, 0.0 us)
Async XLA Ops:
  0.0 16.4 %collective-permute-start.1 = (bf16[2,512,512]{2,1,0:T(8,128)(2,1)}, bf16[2,512,512]{2,1,0:T(8,128)(2,1)S(1)}, u32[]{:S(2)}, u32[]{:S(2)}) collective-permute-start(bf16[2,512,512]{2,1,0:T(8,128)(2,1)} %own.1), channel_id=1, source_target_pairs={{8,9},{10,11},{9,0},{11,2},{12,13},{14,15},{13,12},{15,14},{24,25}... | collective-permute-start | bytes 3145736 | tf_op jit(solution)/shard_map/ppermute | solution.py:200
  0.7 15.7 %collective-permute-start.2 = (bf16[2,512,512]{2,1,0:T(8,128)(2,1)}, bf16[2,512,512]{2,1,0:T(8,128)(2,1)S(1)}, u32[]{:S(2)}, u32[]{:S(2)}) collective-permute-start(bf16[2,512,512]{2,1,0:T(8,128)(2,1)} %own.1), channel_id=1, source_target_pairs={{8,0},{10,2},{9,12},{11,14},{12,9},{14,11},{24,16},{26,18},{25,28}... | collective-permute-start | bytes 3145736 | tf_op jit(solution)/shard_map/ppermute | solution.py:200
  2.5 8.0 %collective-permute-start = (bf16[16,8192]{1,0:T(8,128)(2,1)S(1)}, bf16[16,8192]{1,0:T(8,128)(2,1)S(1)}, u32[]{:S(2)}, u32[]{:S(2)}) collective-permute-start(bf16[16,8192]{1,0:T(8,128)(2,1)S(1)} %get-tuple-element.16), channel_id=1, source_target_pairs={{0,2},{2,0},{4,11},{6,9},{8,14},{10,12},{12,15},{14,13},{16,18},{1... | collective-permute-start | bytes 786440 | tf_op jit(solution)/shard_map/ppermute | solution.py:200
  3.2 13.9 %collective-permute-start.5 = (bf16[16,8192]{1,0:T(8,128)(2,1)S(1)}, bf16[16,8192]{1,0:T(8,128)(2,1)S(1)}, u32[]{:S(2)}, u32[]{:S(2)}) collective-permute-start(bf16[16,8192]{1,0:T(8,128)(2,1)S(1)} %get-tuple-element.20), channel_id=1, source_target_pairs={{0,0},{2,2},{4,9},{6,11},{8,12},{10,14},{12,13},{14,15},{16,16},{1... | collective-permute-start | bytes 786440 | tf_op jit(solution)/shard_map/ppermute | solution.py:200
  3.9 15.1 %collective-permute-start.3 = (bf16[16,8192]{1,0:T(8,128)(2,1)S(1)}, bf16[16,8192]{1,0:T(8,128)(2,1)S(1)}, u32[]{:S(2)}, u32[]{:S(2)}) collective-permute-start(bf16[16,8192]{1,0:T(8,128)(2,1)S(1)} %get-tuple-element.16), channel_id=1, source_target_pairs={{1,2},{3,0},{5,11},{7,9},{9,14},{11,12},{13,15},{15,13},{17,18},{1... | collective-permute-start | bytes 786440 | tf_op jit(solution)/shard_map/ppermute | solution.py:200
  12.2 6.8 %collective-permute-start.4 = (bf16[16,8192]{1,0:T(8,128)(2,1)S(1)}, bf16[16,8192]{1,0:T(8,128)(2,1)S(1)}, u32[]{:S(2)}, u32[]{:S(2)}) collective-permute-start(bf16[16,8192]{1,0:T(8,128)(2,1)S(1)} %get-tuple-element.20), channel_id=1, source_target_pairs={{1,0},{3,2},{5,9},{7,11},{9,12},{11,14},{13,13},{15,15},{17,16},{1... | collective-permute-start | bytes 786440 | tf_op jit(solution)/shard_map/ppermute | solution.py:200
  17.7 4.8 %collective-permute-start.8 = (bf16[16,8192]{1,0:T(8,128)(2,1)S(1)}, bf16[16,8192]{1,0:T(8,128)(2,1)S(1)}, u32[]{:S(2)}, u32[]{:S(2)}) collective-permute-start(bf16[16,8192]{1,0:T(8,128)(2,1)S(1)} %get-tuple-element.21.refs_2_), channel_id=1, source_target_pairs={{2,0},{0,2},{11,4},{9,6},{14,8},{12,10},{15,12},{13,14},{18,16},{1... | collective-permute-start | bytes 786440 | tf_op jit(solution)/shard_map/ppermute | solution.py:200
  18.3 4.1 %collective-permute-start.9 = (bf16[16,8192]{1,0:T(8,128)(2,1)S(1)}, bf16[16,8192]{1,0:T(8,128)(2,1)S(1)}, u32[]{:S(2)}, u32[]{:S(2)}) collective-permute-start(bf16[16,8192]{1,0:T(8,128)(2,1)S(1)} %get-tuple-element.24), channel_id=1, source_target_pairs={{0,0},{2,2},{9,4},{11,6},{12,8},{14,10},{13,12},{15,14},{16,16},{1... | collective-permute-start | bytes 786440 | tf_op jit(solution)/shard_map/ppermute | solution.py:200
  19.8 27.7 %collective-permute-start.6 = (bf16[16,8192]{1,0:T(8,128)(2,1)S(1)}, bf16[16,8192]{1,0:T(8,128)(2,1)S(1)}, u32[]{:S(2)}, u32[]{:S(2)}) collective-permute-start(bf16[16,8192]{1,0:T(8,128)(2,1)S(1)} %get-tuple-element.22), channel_id=1, source_target_pairs={{2,1},{0,3},{11,5},{9,7},{14,9},{12,11},{15,13},{13,15},{18,17},{1... | collective-permute-start | bytes 786440 | tf_op jit(solution)/shard_map/ppermute | solution.py:200
  21.1 26.4 %collective-permute-start.7 = (bf16[16,8192]{1,0:T(8,128)(2,1)S(1)}, bf16[16,8192]{1,0:T(8,128)(2,1)S(1)}, u32[]{:S(2)}, u32[]{:S(2)}) collective-permute-start(bf16[16,8192]{1,0:T(8,128)(2,1)S(1)} %get-tuple-element.23), channel_id=1, source_target_pairs={{0,1},{2,3},{9,5},{11,7},{12,9},{14,11},{13,13},{15,15},{16,17},{1... | collective-permute-start | bytes 786440 | tf_op jit(solution)/shard_map/ppermute | solution.py:200

commit v2 on v1

--- a/solution.py
+++ b/solution.py
@@ -51,7 +51,7 @@
 
 
 def worker_places(low_ctx):
-    return (0, 0), (low_ctx, 1), (low_ctx + 1, 0), (low_ctx + 1, 1)
+    return (0, 0), (low_ctx, 1), (low_ctx + 1, 1), (low_ctx + 1, 0)
 
 
 def own_request(low_ctx):
@@ -68,8 +68,8 @@
     for r in range(REQS):
         start = start + jnp.where(r < request, counts[r], 0)
     count = jnp.where(request >= 0, counts[jnp.maximum(request, 0)], 0)
-    home_pair = jnp.where(request == 0, -1, request)
-    near_pair = jnp.where(request == 0, 1, request ^ 1)
+    home_pair = jnp.where(request == 0, -1, jnp.where(request == 1, 1, 5 - request))
+    near_pair = jnp.where(request == 0, 1, home_pair ^ 1)
     for p in range(most_pages):
         page = start + p
         pair = page // 2
@@ -240,7 +240,7 @@
     near, far = (
         moved(kv_cache, [((*a[:1], h, *a[1:]), (*b[:1], h, *b[1:])) for a, b in sends for h in heads])
         for sends in (
-            [(pairs[0], workers[1]), (pairs[1], workers[0]), (pairs[2], workers[3]), (pairs[3], workers[2])],
+            [(pairs[0], workers[1]), (pairs[1], workers[0]), (pairs[2], workers[2]), (pairs[3], workers[3])],
             [(pairs[0], workers[0]), (pairs[1], workers[2]), (pairs[2], workers[1])],
         )
     )

time: 48.9 us -> 48.3 us (0.988)
  the two profiles are of different devices: /device:TPU:7 before, /device:TPU:1 now
where the time goes in v2:
time: 48.3 us; the launch traced here: 48.8 us
  waiting for transfers between devices  25 us (52%)
  starting transfers between devices  17.9 us (37%)
  Pallas kernels  5.59 us (12%)
    ppermute x10, waiting for transfers between devices, moved(): lax.ppermute(array, ('ctx', 'head', 'sub'), [(flat(a), flat(b)) for a, b...  25 us
    ppermute x10, starting transfers between devices, moved(): lax.ppermute(array, ('ctx', 'head', 'sub'), [(flat(a), flat(b)) for a, b...  17.9 us
    pallas_call x1, Pallas kernels, one_request_each(): pl.pallas_call(functools.partial(gather_home_kernel, low_ctx), out_shape=...  1.7 us
    pallas_call x2, Pallas kernels, one_request_each(): pl.pallas_call(functools.partial(attend_kernel, low_ctx, sub_size, [keys]...  1.35 us
    pallas_call x1, Pallas kernels, one_request_each(): pl.pallas_call(split_kernel, out_shape=[q_piece] * head_count, in_specs=[...  1.06 us
  transfers between devices with their start and end apart: 10, of which 1 were waited for; matrix products, arithmetic and copies ran while one was open for 0% of the time, Pallas kernels for 10%

profile of v2, /device:TPU:1, one launch (start us, length us, event | category | flops | bytes accessed | tf_op | source)
XLA Modules:
  0.0 48.8 jit_solution(14615689818172744819)
XLA Ops:
  0.0 0.7 %collective-permute-start.1 = (bf16[2,512,512]{2,1,0:T(8,128)(2,1)}, bf16[2,512,512]{2,1,0:T(8,128)(2,1)S(1)}, u32[]{:S(2)}, u32[]{:S(2)}) collective-permute-start(bf16[2,512,512]{2,1,0:T(8,128)(2,1)} %own.1), channel_id=1, source_target_pairs={{8,9},{10,11},{9,0},{11,2},{12,13},{14,15},{13,12},{15,14},{24,25}... | collective-permute-start | bytes 3145736 | tf_op jit(solution)/shard_map/ppermute | solution.py:200
  0.7 0.7 %collective-permute-start.2 = (bf16[2,512,512]{2,1,0:T(8,128)(2,1)}, bf16[2,512,512]{2,1,0:T(8,128)(2,1)S(1)}, u32[]{:S(2)}, u32[]{:S(2)}) collective-permute-start(bf16[2,512,512]{2,1,0:T(8,128)(2,1)} %own.1), channel_id=1, source_target_pairs={{8,0},{10,2},{9,13},{11,15},{12,9},{14,11},{24,16},{26,18},{25,29}... | collective-permute-start | bytes 3145736 | tf_op jit(solution)/shard_map/ppermute | solution.py:200
  1.5 1.1 %split.1 = (bf16[16,8192]{1,0:T(8,128)(2,1)S(1)}, bf16[16,8192]{1,0:T(8,128)(2,1)S(1)}) custom-call(bf16[16,16384]{1,0:T(8,128)(2,1)} %queries.1), custom_call_target="tpu_custom_call" | custom-call | tf_op jit(solution)/shard_map/split/pallas_call | solution.py:207
  2.5 0.7 %collective-permute-start = (bf16[16,8192]{1,0:T(8,128)(2,1)S(1)}, bf16[16,8192]{1,0:T(8,128)(2,1)S(1)}, u32[]{:S(2)}, u32[]{:S(2)}) collective-permute-start(bf16[16,8192]{1,0:T(8,128)(2,1)S(1)} %get-tuple-element.16), channel_id=1, source_target_pairs={{0,2},{2,0},{4,11},{6,9},{8,15},{10,13},{12,14},{14,12},{16,18},{1... | collective-permute-start | bytes 786440 | tf_op jit(solution)/shard_map/ppermute | solution.py:200
  3.2 0.7 %collective-permute-start.5 = (bf16[16,8192]{1,0:T(8,128)(2,1)S(1)}, bf16[16,8192]{1,0:T(8,128)(2,1)S(1)}, u32[]{:S(2)}, u32[]{:S(2)}) collective-permute-start(bf16[16,8192]{1,0:T(8,128)(2,1)S(1)} %get-tuple-element.20), channel_id=1, source_target_pairs={{0,0},{2,2},{4,9},{6,11},{8,13},{10,15},{12,12},{14,14},{16,16},{1... | collective-permute-start | bytes 786440 | tf_op jit(solution)/shard_map/ppermute | solution.py:200
  3.9 6.9 %collective-permute-start.3 = (bf16[16,8192]{1,0:T(8,128)(2,1)S(1)}, bf16[16,8192]{1,0:T(8,128)(2,1)S(1)}, u32[]{:S(2)}, u32[]{:S(2)}) collective-permute-start(bf16[16,8192]{1,0:T(8,128)(2,1)S(1)} %get-tuple-element.16), channel_id=1, source_target_pairs={{1,2},{3,0},{5,11},{7,9},{9,15},{11,13},{13,14},{15,12},{17,18},{1... | collective-permute-start | bytes 786440 | tf_op jit(solution)/shard_map/ppermute | solution.py:200
  10.8 0.0 collective-permute-done.after.refs_0_
  10.8 1.7 %gather_home.1 = (bf16[4,4,2,256,128]{4,3,2,1,0:T(8,128)(2,1)S(1)}, s32[4]{0:T(128)S(1)}) custom-call(s32[4]{0:T(128)} %counts_in.1, s32[4]{0:T(128)} %counts_in.1, bf16[2,512,512]{2,1,0:T(8,128)(2,1)} %own.1, bf16[16,8192]{1,0:T(8,128)(2,1)S(1)} %collective-permute-done.after.refs_0_), custom_call_target="tpu_custom_call" | custom-call | tf_op jit(solution)/shard_map/gather_home/pallas_call | solution.py:222
  12.5 4.2 %collective-permute-start.4 = (bf16[16,8192]{1,0:T(8,128)(2,1)S(1)}, bf16[16,8192]{1,0:T(8,128)(2,1)S(1)}, u32[]{:S(2)}, u32[]{:S(2)}) collective-permute-start(bf16[16,8192]{1,0:T(8,128)(2,1)S(1)} %get-tuple-element.20), channel_id=1, source_target_pairs={{1,0},{3,2},{5,9},{7,11},{9,13},{11,15},{13,12},{15,14},{17,16},{1... | collective-permute-start | bytes 786440 | tf_op jit(solution)/shard_map/ppermute | solution.py:200
  16.8 0.0 collective-permute-done.1.near
  16.8 0.0 collective-permute-done.2.far
  16.8 0.6 %gather_rest.1.pages_in = bf16[4,4,2,256,128]{4,3,2,1,0:T(8,128)(2,1)S(1)} custom-call(s32[4]{0:T(128)S(1)} %get-tuple-element.18.counts, bf16[2,512,512]{2,1,0:T(8,128)(2,1)S(1)} %collective-permute-done.1.near, bf16[2,512,512]{2,1,0:T(8,128)(2,1)S(1)} %collective-permute-done.2.far, ...), custom_call_target="tpu_custom_call", output_to_operand_aliasing={{}: (3, {})} | custom-call | tf_op jit(solution)/shard_map/gather_rest/pallas_call | solution.py:247
  17.4 0.0 collective-permute-done.5.refs_1_
  17.4 0.6 %attend_0.1 = (bf16[16,8192]{1,0:T(8,128)(2,1)S(1)}, bf16[16,8192]{1,0:T(8,128)(2,1)S(1)}) custom-call(s32[4]{0:T(128)S(1)} %get-tuple-element.18.counts, bf16[4,4,2,256,128]{4,3,2,1,0:T(8,128)(2,1)S(1)} %gather_rest.1.pages_in, bf16[16,8192]{1,0:T(8,128)(2,1)S(1)} %collective-permute-done.after.refs_0_, bf16[16,8192]{1,0:T(8,128)(2,1)S(1)} %collective-permute-done.5.refs_1_), custom_call_target="tpu_custom_call" | custom-call | flops 10000000000 | bytes 4194304 | tf_op jit(solution)/shard_map/attend_0/pallas_call | solution.py:261
  18.0 0.7 %collective-permute-start.8 = (bf16[16,8192]{1,0:T(8,128)(2,1)S(1)}, bf16[16,8192]{1,0:T(8,128)(2,1)S(1)}, u32[]{:S(2)}, u32[]{:S(2)}) collective-permute-start(bf16[16,8192]{1,0:T(8,128)(2,1)S(1)} %get-tuple-element.21.refs_2_), channel_id=1, source_target_pairs={{2,0},{0,2},{11,4},{9,6},{15,8},{13,10},{14,12},{12,14},{18,16},{1... | collective-permute-start | bytes 786440 | tf_op jit(solution)/shard_map/ppermute | solution.py:200
  18.7 0.7 %collective-permute-start.9 = (bf16[16,8192]{1,0:T(8,128)(2,1)S(1)}, bf16[16,8192]{1,0:T(8,128)(2,1)S(1)}, u32[]{:S(2)}, u32[]{:S(2)}) collective-permute-start(bf16[16,8192]{1,0:T(8,128)(2,1)S(1)} %get-tuple-element.24), channel_id=1, source_target_pairs={{0,0},{2,2},{9,4},{11,6},{13,8},{15,10},{12,12},{14,14},{16,16},{1... | collective-permute-start | bytes 786440 | tf_op jit(solution)/shard_map/ppermute | solution.py:200
  19.4 0.0 collective-permute-done.3.refs_0_
  19.4 0.0 collective-permute-done.4.refs_1_
  19.4 0.8 %attend_1.1 = (bf16[16,8192]{1,0:T(8,128)(2,1)S(1)}, bf16[16,8192]{1,0:T(8,128)(2,1)S(1)}) custom-call(s32[4]{0:T(128)S(1)} %get-tuple-element.18.counts, bf16[4,4,2,256,128]{4,3,2,1,0:T(8,128)(2,1)S(1)} %gather_rest.1.pages_in, bf16[16,8192]{1,0:T(8,128)(2,1)S(1)} %collective-permute-done.3.refs_0_, bf16[16,8192]{1,0:T(8,128)(2,1)S(1)} %collective-permute-done.4.refs_1_, ...), custom_call_target="tpu_custom_call" | custom-call | flops 10000000000 | bytes 4194304 | tf_op jit(solution)/shard_map/attend_1/pallas_call | solution.py:261
  20.2 1.3 %collective-permute-start.6 = (bf16[16,8192]{1,0:T(8,128)(2,1)S(1)}, bf16[16,8192]{1,0:T(8,128)(2,1)S(1)}, u32[]{:S(2)}, u32[]{:S(2)}) collective-permute-start(bf16[16,8192]{1,0:T(8,128)(2,1)S(1)} %get-tuple-element.22), channel_id=1, source_target_pairs={{2,1},{0,3},{11,5},{9,7},{15,9},{13,11},{14,13},{12,15},{18,17},{1... | collective-permute-start | bytes 786440 | tf_op jit(solution)/shard_map/ppermute | solution.py:200
  21.5 1.3 %collective-permute-start.7 = (bf16[16,8192]{1,0:T(8,128)(2,1)S(1)}, bf16[16,8192]{1,0:T(8,128)(2,1)S(1)}, u32[]{:S(2)}, u32[]{:S(2)}) collective-permute-start(bf16[16,8192]{1,0:T(8,128)(2,1)S(1)} %get-tuple-element.23), channel_id=1, source_target_pairs={{0,1},{2,3},{9,5},{11,7},{13,9},{15,11},{12,13},{14,15},{16,17},{1... | collective-permute-start | bytes 786440 | tf_op jit(solution)/shard_map/ppermute | solution.py:200
  22.8 0.0 collective-permute-done.8.refs_0_
  22.8 0.0 collective-permute-done.9.refs_1_
  22.9 25.0 %collective-permute-done.6.refs_0_ = bf16[16,8192]{1,0:T(8,128)(2,1)S(1)} collective-permute-done((bf16[16,8192]{1,0:T(8,128)(2,1)S(1)}, bf16[16,8192]{1,0:T(8,128)(2,1)S(1)}, u32[]{:S(2)}, u32[]{:S(2)}) %collective-permute-start.6) | collective-permute-done | bytes 262176 | tf_op jit(solution)/shard_map/ppermute | solution.py:200
  47.8 0.0 collective-permute-done.7.refs_1_
  47.8 0.8 %join_1.1 = bf16[16,16384]{1,0:T(8,128)(2,1)} custom-call(bf16[16,8192]{1,0:T(8,128)(2,1)S(1)} %collective-permute-done.6.refs_0_, bf16[16,8192]{1,0:T(8,128)(2,1)S(1)} %collective-permute-done.7.refs_1_, bf16[16,16384]{1,0:T(8,128)(2,1)} %join_0.1.refs_2_), custom_call_target="tpu_custom_call", output_to_operand_aliasing={{}: (2, {})} | custom-call | tf_op jit(solution)/shard_map/join_1/pallas_call | solution.py:277
  (1 shorter events, 0.0 us)
Async XLA Ops:
  0.0 16.8 %collective-permute-start.1 = (bf16[2,512,512]{2,1,0:T(8,128)(2,1)}, bf16[2,512,512]{2,1,0:T(8,128)(2,1)S(1)}, u32[]{:S(2)}, u32[]{:S(2)}) collective-permute-start(bf16[2,512,512]{2,1,0:T(8,128)(2,1)} %own.1), channel_id=1, source_target_pairs={{8,9},{10,11},{9,0},{11,2},{12,13},{14,15},{13,12},{15,14},{24,25}... | collective-permute-start | bytes 3145736 | tf_op jit(solution)/shard_map/ppermute | solution.py:200
  0.7 16.1 %collective-permute-start.2 = (bf16[2,512,512]{2,1,0:T(8,128)(2,1)}, bf16[2,512,512]{2,1,0:T(8,128)(2,1)S(1)}, u32[]{:S(2)}, u32[]{:S(2)}) collective-permute-start(bf16[2,512,512]{2,1,0:T(8,128)(2,1)} %own.1), channel_id=1, source_target_pairs={{8,0},{10,2},{9,13},{11,15},{12,9},{14,11},{24,16},{26,18},{25,29}... | collective-permute-start | bytes 3145736 | tf_op jit(solution)/shard_map/ppermute | solution.py:200
  2.5 8.3 %collective-permute-start = (bf16[16,8192]{1,0:T(8,128)(2,1)S(1)}, bf16[16,8192]{1,0:T(8,128)(2,1)S(1)}, u32[]{:S(2)}, u32[]{:S(2)}) collective-permute-start(bf16[16,8192]{1,0:T(8,128)(2,1)S(1)} %get-tuple-element.16), channel_id=1, source_target_pairs={{0,2},{2,0},{4,11},{6,9},{8,15},{10,13},{12,14},{14,12},{16,18},{1... | collective-permute-start | bytes 786440 | tf_op jit(solution)/shard_map/ppermute | solution.py:200
  3.2 14.2 %collective-permute-start.5 = (bf16[16,8192]{1,0:T(8,128)(2,1)S(1)}, bf16[16,8192]{1,0:T(8,128)(2,1)S(1)}, u32[]{:S(2)}, u32[]{:S(2)}) collective-permute-start(bf16[16,8192]{1,0:T(8,128)(2,1)S(1)} %get-tuple-element.20), channel_id=1, source_target_pairs={{0,0},{2,2},{4,9},{6,11},{8,13},{10,15},{12,12},{14,14},{16,16},{1... | collective-permute-start | bytes 786440 | tf_op jit(solution)/shard_map/ppermute | solution.py:200
  3.9 15.5 %collective-permute-start.3 = (bf16[16,8192]{1,0:T(8,128)(2,1)S(1)}, bf16[16,8192]{1,0:T(8,128)(2,1)S(1)}, u32[]{:S(2)}, u32[]{:S(2)}) collective-permute-start(bf16[16,8192]{1,0:T(8,128)(2,1)S(1)} %get-tuple-element.16), channel_id=1, source_target_pairs={{1,2},{3,0},{5,11},{7,9},{9,15},{11,13},{13,14},{15,12},{17,18},{1... | collective-permute-start | bytes 786440 | tf_op jit(solution)/shard_map/ppermute | solution.py:200
  12.5 6.9 %collective-permute-start.4 = (bf16[16,8192]{1,0:T(8,128)(2,1)S(1)}, bf16[16,8192]{1,0:T(8,128)(2,1)S(1)}, u32[]{:S(2)}, u32[]{:S(2)}) collective-permute-start(bf16[16,8192]{1,0:T(8,128)(2,1)S(1)} %get-tuple-element.20), channel_id=1, source_target_pairs={{1,0},{3,2},{5,9},{7,11},{9,13},{11,15},{13,12},{15,14},{17,16},{1... | collective-permute-start | bytes 786440 | tf_op jit(solution)/shard_map/ppermute | solution.py:200
  18.0 4.8 %collective-permute-start.8 = (bf16[16,8192]{1,0:T(8,128)(2,1)S(1)}, bf16[16,8192]{1,0:T(8,128)(2,1)S(1)}, u32[]{:S(2)}, u32[]{:S(2)}) collective-permute-start(bf16[16,8192]{1,0:T(8,128)(2,1)S(1)} %get-tuple-element.21.refs_2_), channel_id=1, source_target_pairs={{2,0},{0,2},{11,4},{9,6},{15,8},{13,10},{14,12},{12,14},{18,16},{1... | collective-permute-start | bytes 786440 | tf_op jit(solution)/shard_map/ppermute | solution.py:200
  18.7 4.1 %collective-permute-start.9 = (bf16[16,8192]{1,0:T(8,128)(2,1)S(1)}, bf16[16,8192]{1,0:T(8,128)(2,1)S(1)}, u32[]{:S(2)}, u32[]{:S(2)}) collective-permute-start(bf16[16,8192]{1,0:T(8,128)(2,1)S(1)} %get-tuple-element.24), channel_id=1, source_target_pairs={{0,0},{2,2},{9,4},{11,6},{13,8},{15,10},{12,12},{14,14},{16,16},{1... | collective-permute-start | bytes 786440 | tf_op jit(solution)/shard_map/ppermute | solution.py:200
  20.2 27.6 %collective-permute-start.6 = (bf16[16,8192]{1,0:T(8,128)(2,1)S(1)}, bf16[16,8192]{1,0:T(8,128)(2,1)S(1)}, u32[]{:S(2)}, u32[]{:S(2)}) collective-permute-start(bf16[16,8192]{1,0:T(8,128)(2,1)S(1)} %get-tuple-element.22), channel_id=1, source_target_pairs={{2,1},{0,3},{11,5},{9,7},{15,9},{13,11},{14,13},{12,15},{18,17},{1... | collective-permute-start | bytes 786440 | tf_op jit(solution)/shard_map/ppermute | solution.py:200
  21.5 26.3 %collective-permute-start.7 = (bf16[16,8192]{1,0:T(8,128)(2,1)S(1)}, bf16[16,8192]{1,0:T(8,128)(2,1)S(1)}, u32[]{:S(2)}, u32[]{:S(2)}) collective-permute-start(bf16[16,8192]{1,0:T(8,128)(2,1)S(1)} %get-tuple-element.23), channel_id=1, source_target_pairs={{0,1},{2,3},{9,5},{11,7},{13,9},{15,11},{12,13},{14,15},{16,17},{1... | collective-permute-start | bytes 786440 | tf_op jit(solution)/shard_map/ppermute | solution.py:200

commit v3 on v2

--- a/solution.py
+++ b/solution.py
@@ -101,9 +101,13 @@
     counts_copy.wait()
 
 
-def gather_rest_kernel(low_ctx, counts, near, far, home, out):
+def gather_rest(low_ctx, counts, home, far, near, out):
     local_kv, most_pages = out.shape[:2]
     for p, here, which, rows in pages_of(low_ctx, counts, most_pages):
+        @pl.when(here & (which == 0))
+        def _():
+            for g in range(local_kv):
+                out[g, p] = home[g, p]
         for n, ref in enumerate((near, far)):
             @pl.when(here & (which == n + 1))
             def _():
@@ -112,9 +116,13 @@
                         out[g, p, i] = ref[i, rows, g * HD:(g + 1) * HD]
 
 
-def attend_kernel(low_ctx, sub_count, groups, waits, counts, pages_in, *refs):
+def attend_kernel(low_ctx, sub_count, groups, others, counts, home, *refs):
     keys = [key for group in groups for key in group]
-    queries, outs = dict(zip(keys, refs)), dict(zip(keys, refs[len(keys) + waits:]))
+    queries, outs = dict(zip(keys, refs)), dict(zip(keys, refs[len(keys) + others:]))
+    pages_in = home
+    if others:
+        pages_in = refs[-1]
+        gather_rest(low_ctx, counts, home, *refs[len(keys):len(keys) + others], pages_in)
     head = lax.axis_index("head")
     tokens, width = refs[0].shape
     local_kv, most_pages = pages_in.shape[:2]
@@ -244,32 +252,23 @@
             [(pairs[0], workers[0]), (pairs[1], workers[2]), (pairs[2], workers[1])],
         )
     )
-    gathered = pl.pallas_call(
-        functools.partial(gather_rest_kernel, low_ctx),
-        out_shape=pltpu.VMEM(home.shape, home.dtype),
-        in_specs=[pl.BlockSpec(memory_space=pltpu.SMEM)] + [in_vmem] * 2 + [anywhere],
-        out_specs=in_vmem,
-        input_output_aliases={3: 0},
-        compiler_params=pltpu.CompilerParams(vmem_limit_bytes=2**20),
-        name="gather_rest",
-    )(vmem(counts), vmem(near), vmem(far), vmem(home))
-
     groups = [[(step, s) for step in heads[::-1]] for s in range(sub_size)]
     back = {}
-    after = []
+    pages, others = home, [vmem(far), vmem(near)]
     for keys in groups:
         outs = pl.pallas_call(
-            functools.partial(attend_kernel, low_ctx, sub_size, [keys], len(after)),
-            out_shape=[q_piece] * len(keys),
-            in_specs=[pl.BlockSpec(memory_space=pltpu.SMEM)] + [in_vmem] * (1 + len(keys)) + [anywhere] * len(after),
-            out_specs=[in_vmem] * len(keys),
+            functools.partial(attend_kernel, low_ctx, sub_size, [keys], len(others)),
+            out_shape=[q_piece] * len(keys) + [pltpu.VMEM(home.shape, home.dtype)] * bool(others),
+            in_specs=[pl.BlockSpec(memory_space=pltpu.SMEM)] + [in_vmem] * (1 + len(keys) + len(others)),
+            out_specs=[in_vmem] * (len(keys) + bool(others)),
             compiler_params=pltpu.CompilerParams(vmem_limit_bytes=12 * 2**20),
             cost_estimate=pl.CostEstimate(flops=10**10, bytes_accessed=2**22, transcendentals=10**6),
             name=f"attend_{keys[0][1]}",
-        )(vmem(counts), vmem(gathered), *[vmem(q_in[key]) for key in keys], *after)
+        )(vmem(counts), vmem(pages), *[vmem(q_in[key]) for key in keys], *others)
         for key, out in zip(keys, outs):
             back[key] = moved(out, [(b, a) for a, b in routes[key]])
-        after = [outs[0]]
+        if others:
+            pages, others = outs[-1], []
 
     joined = []
     for keys in groups:

time: 48.3 us -> 48.5 us (level); the launches traced: 48.8 us -> 48.3 us
  Pallas kernels: 5.59 us -> 5.05 us
    pallas_call x1 -> x0, Pallas kernels: 0.64 us -> none  [one_request_each(): pl.pallas_call(functools.partial(gather_rest_kernel, low_ctx), out_shape=...]
  transfers between devices with their start and end apart: 10 -> 10, of which waited for: 1 -> 1; matrix products, arithmetic and copies ran while one was open for 0% -> 0% of each run, Pallas kernels for 10% -> 9%
where the time goes in v3:
time: 48.5 us; the launch traced here: 48.3 us
  waiting for transfers between devices  25 us (52%)
  starting transfers between devices  17.9 us (37%)
  Pallas kernels  5.05 us (10%)
    ppermute x10, waiting for transfers between devices, moved(): lax.ppermute(array, ('ctx', 'head', 'sub'), [(flat(a), flat(b)) for a, b...  25 us
    ppermute x10, starting transfers between devices, moved(): lax.ppermute(array, ('ctx', 'head', 'sub'), [(flat(a), flat(b)) for a, b...  17.9 us
    pallas_call x1, Pallas kernels, one_request_each(): pl.pallas_call(functools.partial(gather_home_kernel, low_ctx), out_shape=...  1.7 us
    pallas_call x2, Pallas kernels, one_request_each(): pl.pallas_call(functools.partial(attend_kernel, low_ctx, sub_size, [keys]...  1.45 us
    pallas_call x1, Pallas kernels, one_request_each(): pl.pallas_call(split_kernel, out_shape=[q_piece] * head_count, in_specs=[...  1.06 us
  transfers between devices with their start and end apart: 10, of which 1 were waited for; matrix products, arithmetic and copies ran while one was open for 0% of the time, Pallas kernels for 9%

profile of v3, /device:TPU:1, one launch (start us, length us, event | category | flops | bytes accessed | tf_op | source)
XLA Modules:
  0.0 48.3 jit_solution(1657362783751437720)
XLA Ops:
  0.0 0.7 %collective-permute-start.3 = (bf16[2,512,512]{2,1,0:T(8,128)(2,1)}, bf16[2,512,512]{2,1,0:T(8,128)(2,1)S(1)}, u32[]{:S(2)}, u32[]{:S(2)}) collective-permute-start(bf16[2,512,512]{2,1,0:T(8,128)(2,1)} %own.1), channel_id=1, source_target_pairs={{8,9},{10,11},{9,0},{11,2},{12,13},{14,15},{13,12},{15,14},{24,25}... | collective-permute-start | bytes 3145736 | tf_op jit(solution)/shard_map/ppermute | solution.py:208
  0.7 0.7 %collective-permute-start.2 = (bf16[2,512,512]{2,1,0:T(8,128)(2,1)}, bf16[2,512,512]{2,1,0:T(8,128)(2,1)S(1)}, u32[]{:S(2)}, u32[]{:S(2)}) collective-permute-start(bf16[2,512,512]{2,1,0:T(8,128)(2,1)} %own.1), channel_id=1, source_target_pairs={{8,0},{10,2},{9,13},{11,15},{12,9},{14,11},{24,16},{26,18},{25,29}... | collective-permute-start | bytes 3145736 | tf_op jit(solution)/shard_map/ppermute | solution.py:208
  1.5 1.1 %split.1 = (bf16[16,8192]{1,0:T(8,128)(2,1)S(1)}, bf16[16,8192]{1,0:T(8,128)(2,1)S(1)}) custom-call(bf16[16,16384]{1,0:T(8,128)(2,1)} %queries.1), custom_call_target="tpu_custom_call" | custom-call | tf_op jit(solution)/shard_map/split/pallas_call | solution.py:215
  2.5 0.7 %collective-permute-start = (bf16[16,8192]{1,0:T(8,128)(2,1)S(1)}, bf16[16,8192]{1,0:T(8,128)(2,1)S(1)}, u32[]{:S(2)}, u32[]{:S(2)}) collective-permute-start(bf16[16,8192]{1,0:T(8,128)(2,1)S(1)} %get-tuple-element.17), channel_id=1, source_target_pairs={{0,2},{2,0},{4,11},{6,9},{8,15},{10,13},{12,14},{14,12},{16,18},{1... | collective-permute-start | bytes 786440 | tf_op jit(solution)/shard_map/ppermute | solution.py:208
  3.2 0.7 %collective-permute-start.1 = (bf16[16,8192]{1,0:T(8,128)(2,1)S(1)}, bf16[16,8192]{1,0:T(8,128)(2,1)S(1)}, u32[]{:S(2)}, u32[]{:S(2)}) collective-permute-start(bf16[16,8192]{1,0:T(8,128)(2,1)S(1)} %get-tuple-element.22), channel_id=1, source_target_pairs={{0,0},{2,2},{4,9},{6,11},{8,13},{10,15},{12,12},{14,14},{16,16},{1... | collective-permute-start | bytes 786440 | tf_op jit(solution)/shard_map/ppermute | solution.py:208
  3.9 6.9 %collective-permute-start.4 = (bf16[16,8192]{1,0:T(8,128)(2,1)S(1)}, bf16[16,8192]{1,0:T(8,128)(2,1)S(1)}, u32[]{:S(2)}, u32[]{:S(2)}) collective-permute-start(bf16[16,8192]{1,0:T(8,128)(2,1)S(1)} %get-tuple-element.17), channel_id=1, source_target_pairs={{1,2},{3,0},{5,11},{7,9},{9,15},{11,13},{13,14},{15,12},{17,18},{1... | collective-permute-start | bytes 786440 | tf_op jit(solution)/shard_map/ppermute | solution.py:208
  10.8 0.0 collective-permute-done.after.refs_0_
  10.8 1.7 %gather_home.1 = (bf16[4,4,2,256,128]{4,3,2,1,0:T(8,128)(2,1)S(1)}, s32[4]{0:T(128)S(1)}) custom-call(s32[4]{0:T(128)} %counts_in.1, s32[4]{0:T(128)} %counts_in.1, bf16[2,512,512]{2,1,0:T(8,128)(2,1)} %own.1, bf16[16,8192]{1,0:T(8,128)(2,1)S(1)} %collective-permute-done.after.refs_0_), custom_call_target="tpu_custom_call" | custom-call | tf_op jit(solution)/shard_map/gather_home/pallas_call | solution.py:230
  12.5 4.2 %collective-permute-start.5 = (bf16[16,8192]{1,0:T(8,128)(2,1)S(1)}, bf16[16,8192]{1,0:T(8,128)(2,1)S(1)}, u32[]{:S(2)}, u32[]{:S(2)}) collective-permute-start(bf16[16,8192]{1,0:T(8,128)(2,1)S(1)} %get-tuple-element.22), channel_id=1, source_target_pairs={{1,0},{3,2},{5,9},{7,11},{9,13},{11,15},{13,12},{15,14},{17,16},{1... | collective-permute-start | bytes 786440 | tf_op jit(solution)/shard_map/ppermute | solution.py:208
  16.8 0.0 collective-permute-done.1.refs_1_
  16.8 0.0 collective-permute-done.3.refs_3_
  16.8 0.0 collective-permute-done.2.refs_2_
  16.8 0.7 %attend_0.1 = (bf16[16,8192]{1,0:T(8,128)(2,1)S(1)}, bf16[16,8192]{1,0:T(8,128)(2,1)S(1)}, bf16[4,4,2,256,128]{4,3,2,1,0:T(8,128)(2,1)S(1)}) custom-call(s32[4]{0:T(128)S(1)} %get-tuple-element.19.counts, bf16[4,4,2,256,128]{4,3,2,1,0:T(8,128)(2,1)S(1)} %get-tuple-element.20.home, bf16[16,8192]{1,0:T(8,128)(2,1)S(1)} %collective-permute-done.after.refs_0_, ...), custom_call_target="tpu_custom_call" | custom-call | flops 10000000000 | bytes 4194304 | tf_op jit(solution)/shard_map/attend_0/pallas_call | solution.py:259
  17.5 0.7 %collective-permute-start.8 = (bf16[16,8192]{1,0:T(8,128)(2,1)S(1)}, bf16[16,8192]{1,0:T(8,128)(2,1)S(1)}, u32[]{:S(2)}, u32[]{:S(2)}) collective-permute-start(bf16[16,8192]{1,0:T(8,128)(2,1)S(1)} %get-tuple-element.25), channel_id=1, source_target_pairs={{2,0},{0,2},{11,4},{9,6},{15,8},{13,10},{14,12},{12,14},{18,16},{1... | collective-permute-start | bytes 786440 | tf_op jit(solution)/shard_map/ppermute | solution.py:208
  18.2 0.7 %collective-permute-start.9 = (bf16[16,8192]{1,0:T(8,128)(2,1)S(1)}, bf16[16,8192]{1,0:T(8,128)(2,1)S(1)}, u32[]{:S(2)}, u32[]{:S(2)}) collective-permute-start(bf16[16,8192]{1,0:T(8,128)(2,1)S(1)} %get-tuple-element.26), channel_id=1, source_target_pairs={{0,0},{2,2},{9,4},{11,6},{13,8},{15,10},{12,12},{14,14},{16,16},{1... | collective-permute-start | bytes 786440 | tf_op jit(solution)/shard_map/ppermute | solution.py:208
  18.8 0.0 collective-permute-done.4.refs_0_
  18.9 0.0 collective-permute-done.5.refs_1_
  18.9 0.8 %attend_1.1 = (bf16[16,8192]{1,0:T(8,128)(2,1)S(1)}, bf16[16,8192]{1,0:T(8,128)(2,1)S(1)}) custom-call(s32[4]{0:T(128)S(1)} %get-tuple-element.19.counts, bf16[4,4,2,256,128]{4,3,2,1,0:T(8,128)(2,1)S(1)} %get-tuple-element.21.home, bf16[16,8192]{1,0:T(8,128)(2,1)S(1)} %collective-permute-done.4.refs_0_, bf16[16,8192]{1,0:T(8,128)(2,1)S(1)} %collective-permute-done.5.refs_1_), custom_call_target="tpu_custom_call" | custom-call | flops 10000000000 | bytes 4194304 | tf_op jit(solution)/shard_map/attend_1/pallas_call | solution.py:259
  19.7 1.3 %collective-permute-start.6 = (bf16[16,8192]{1,0:T(8,128)(2,1)S(1)}, bf16[16,8192]{1,0:T(8,128)(2,1)S(1)}, u32[]{:S(2)}, u32[]{:S(2)}) collective-permute-start(bf16[16,8192]{1,0:T(8,128)(2,1)S(1)} %get-tuple-element.23), channel_id=1, source_target_pairs={{2,1},{0,3},{11,5},{9,7},{15,9},{13,11},{14,13},{12,15},{18,17},{1... | collective-permute-start | bytes 786440 | tf_op jit(solution)/shard_map/ppermute | solution.py:208
  21.0 1.3 %collective-permute-start.7 = (bf16[16,8192]{1,0:T(8,128)(2,1)S(1)}, bf16[16,8192]{1,0:T(8,128)(2,1)S(1)}, u32[]{:S(2)}, u32[]{:S(2)}) collective-permute-start(bf16[16,8192]{1,0:T(8,128)(2,1)S(1)} %get-tuple-element.24), channel_id=1, source_target_pairs={{0,1},{2,3},{9,5},{11,7},{13,9},{15,11},{12,13},{14,15},{16,17},{1... | collective-permute-start | bytes 786440 | tf_op jit(solution)/shard_map/ppermute | solution.py:208
  22.3 0.0 collective-permute-done.8.refs_0_
  22.3 0.0 collective-permute-done.9.refs_1_
  22.3 25.0 %collective-permute-done.6.refs_0_ = bf16[16,8192]{1,0:T(8,128)(2,1)S(1)} collective-permute-done((bf16[16,8192]{1,0:T(8,128)(2,1)S(1)}, bf16[16,8192]{1,0:T(8,128)(2,1)S(1)}, u32[]{:S(2)}, u32[]{:S(2)}) %collective-permute-start.6) | collective-permute-done | bytes 262176 | tf_op jit(solution)/shard_map/ppermute | solution.py:208
  47.3 0.0 collective-permute-done.7.refs_1_
  47.3 0.8 %join_1.1 = bf16[16,16384]{1,0:T(8,128)(2,1)} custom-call(bf16[16,8192]{1,0:T(8,128)(2,1)S(1)} %collective-permute-done.6.refs_0_, bf16[16,8192]{1,0:T(8,128)(2,1)S(1)} %collective-permute-done.7.refs_1_, bf16[16,16384]{1,0:T(8,128)(2,1)} %join_0.1.refs_2_), custom_call_target="tpu_custom_call", output_to_operand_aliasing={{}: (2, {})} | custom-call | tf_op jit(solution)/shard_map/join_1/pallas_call | solution.py:276
  (1 shorter events, 0.0 us)
Async XLA Ops:
  0.0 16.8 %collective-permute-start.3 = (bf16[2,512,512]{2,1,0:T(8,128)(2,1)}, bf16[2,512,512]{2,1,0:T(8,128)(2,1)S(1)}, u32[]{:S(2)}, u32[]{:S(2)}) collective-permute-start(bf16[2,512,512]{2,1,0:T(8,128)(2,1)} %own.1), channel_id=1, source_target_pairs={{8,9},{10,11},{9,0},{11,2},{12,13},{14,15},{13,12},{15,14},{24,25}... | collective-permute-start | bytes 3145736 | tf_op jit(solution)/shard_map/ppermute | solution.py:208
  0.7 16.1 %collective-permute-start.2 = (bf16[2,512,512]{2,1,0:T(8,128)(2,1)}, bf16[2,512,512]{2,1,0:T(8,128)(2,1)S(1)}, u32[]{:S(2)}, u32[]{:S(2)}) collective-permute-start(bf16[2,512,512]{2,1,0:T(8,128)(2,1)} %own.1), channel_id=1, source_target_pairs={{8,0},{10,2},{9,13},{11,15},{12,9},{14,11},{24,16},{26,18},{25,29}... | collective-permute-start | bytes 3145736 | tf_op jit(solution)/shard_map/ppermute | solution.py:208
  2.5 8.3 %collective-permute-start = (bf16[16,8192]{1,0:T(8,128)(2,1)S(1)}, bf16[16,8192]{1,0:T(8,128)(2,1)S(1)}, u32[]{:S(2)}, u32[]{:S(2)}) collective-permute-start(bf16[16,8192]{1,0:T(8,128)(2,1)S(1)} %get-tuple-element.17), channel_id=1, source_target_pairs={{0,2},{2,0},{4,11},{6,9},{8,15},{10,13},{12,14},{14,12},{16,18},{1... | collective-permute-start | bytes 786440 | tf_op jit(solution)/shard_map/ppermute | solution.py:208
  3.2 13.6 %collective-permute-start.1 = (bf16[16,8192]{1,0:T(8,128)(2,1)S(1)}, bf16[16,8192]{1,0:T(8,128)(2,1)S(1)}, u32[]{:S(2)}, u32[]{:S(2)}) collective-permute-start(bf16[16,8192]{1,0:T(8,128)(2,1)S(1)} %get-tuple-element.22), channel_id=1, source_target_pairs={{0,0},{2,2},{4,9},{6,11},{8,13},{10,15},{12,12},{14,14},{16,16},{1... | collective-permute-start | bytes 786440 | tf_op jit(solution)/shard_map/ppermute | solution.py:208
  3.9 15.0 %collective-permute-start.4 = (bf16[16,8192]{1,0:T(8,128)(2,1)S(1)}, bf16[16,8192]{1,0:T(8,128)(2,1)S(1)}, u32[]{:S(2)}, u32[]{:S(2)}) collective-permute-start(bf16[16,8192]{1,0:T(8,128)(2,1)S(1)} %get-tuple-element.17), channel_id=1, source_target_pairs={{1,2},{3,0},{5,11},{7,9},{9,15},{11,13},{13,14},{15,12},{17,18},{1... | collective-permute-start | bytes 786440 | tf_op jit(solution)/shard_map/ppermute | solution.py:208
  12.5 6.3 %collective-permute-start.5 = (bf16[16,8192]{1,0:T(8,128)(2,1)S(1)}, bf16[16,8192]{1,0:T(8,128)(2,1)S(1)}, u32[]{:S(2)}, u32[]{:S(2)}) collective-permute-start(bf16[16,8192]{1,0:T(8,128)(2,1)S(1)} %get-tuple-element.22), channel_id=1, source_target_pairs={{1,0},{3,2},{5,9},{7,11},{9,13},{11,15},{13,12},{15,14},{17,16},{1... | collective-permute-start | bytes 786440 | tf_op jit(solution)/shard_map/ppermute | solution.py:208
  17.5 4.8 %collective-permute-start.8 = (bf16[16,8192]{1,0:T(8,128)(2,1)S(1)}, bf16[16,8192]{1,0:T(8,128)(2,1)S(1)}, u32[]{:S(2)}, u32[]{:S(2)}) collective-permute-start(bf16[16,8192]{1,0:T(8,128)(2,1)S(1)} %get-tuple-element.25), channel_id=1, source_target_pairs={{2,0},{0,2},{11,4},{9,6},{15,8},{13,10},{14,12},{12,14},{18,16},{1... | collective-permute-start | bytes 786440 | tf_op jit(solution)/shard_map/ppermute | solution.py:208
  18.2 4.1 %collective-permute-start.9 = (bf16[16,8192]{1,0:T(8,128)(2,1)S(1)}, bf16[16,8192]{1,0:T(8,128)(2,1)S(1)}, u32[]{:S(2)}, u32[]{:S(2)}) collective-permute-start(bf16[16,8192]{1,0:T(8,128)(2,1)S(1)} %get-tuple-element.26), channel_id=1, source_target_pairs={{0,0},{2,2},{9,4},{11,6},{13,8},{15,10},{12,12},{14,14},{16,16},{1... | collective-permute-start | bytes 786440 | tf_op jit(solution)/shard_map/ppermute | solution.py:208
  19.7 27.6 %collective-permute-start.6 = (bf16[16,8192]{1,0:T(8,128)(2,1)S(1)}, bf16[16,8192]{1,0:T(8,128)(2,1)S(1)}, u32[]{:S(2)}, u32[]{:S(2)}) collective-permute-start(bf16[16,8192]{1,0:T(8,128)(2,1)S(1)} %get-tuple-element.23), channel_id=1, source_target_pairs={{2,1},{0,3},{11,5},{9,7},{15,9},{13,11},{14,13},{12,15},{18,17},{1... | collective-permute-start | bytes 786440 | tf_op jit(solution)/shard_map/ppermute | solution.py:208
  21.0 26.3 %collective-permute-start.7 = (bf16[16,8192]{1,0:T(8,128)(2,1)S(1)}, bf16[16,8192]{1,0:T(8,128)(2,1)S(1)}, u32[]{:S(2)}, u32[]{:S(2)}) collective-permute-start(bf16[16,8192]{1,0:T(8,128)(2,1)S(1)} %get-tuple-element.24), channel_id=1, source_target_pairs={{0,1},{2,3},{9,5},{11,7},{13,9},{15,11},{12,13},{14,15},{16,17},{1... | collective-permute-start | bytes 786440 | tf_op jit(solution)/shard_map/ppermute | solution.py:208

commit v4 on v3

--- a/solution.py
+++ b/solution.py
@@ -78,12 +78,12 @@
 
 
 def gather_home_kernel(low_ctx, counts, counts_in, own, after, out, counts_out, sems, counts_sem):
-    local_kv, most_pages = out.shape[:2]
+    local_kv, _, most_pages = out.shape[:3]
     counts_copy = pltpu.make_async_copy(counts_in, counts_out, counts_sem)
     counts_copy.start()
     plan = [
         (here & (which == 0), [
-            pltpu.make_async_copy(own.at[i, rows, pl.ds(g * HD, HD)], out.at[g, p, i], sems.at[g, p, i])
+            pltpu.make_async_copy(own.at[i, rows, pl.ds(g * HD, HD)], out.at[g, i, p], sems.at[g, i, p])
             for g in range(local_kv) for i in range(2)
         ])
         for p, here, which, rows in pages_of(low_ctx, counts, most_pages)
@@ -102,18 +102,18 @@
 
 
 def gather_rest(low_ctx, counts, home, far, near, out):
-    local_kv, most_pages = out.shape[:2]
+    local_kv, _, most_pages = out.shape[:3]
     for p, here, which, rows in pages_of(low_ctx, counts, most_pages):
         @pl.when(here & (which == 0))
         def _():
             for g in range(local_kv):
-                out[g, p] = home[g, p]
+                out[g, :, p] = home[g, :, p]
         for n, ref in enumerate((near, far)):
             @pl.when(here & (which == n + 1))
             def _():
                 for g in range(local_kv):
                     for i in range(2):
-                        out[g, p, i] = ref[i, rows, g * HD:(g + 1) * HD]
+                        out[g, i, p] = ref[i, rows, g * HD:(g + 1) * HD]
 
 
 def attend_kernel(low_ctx, sub_count, groups, others, counts, home, *refs):
@@ -125,46 +125,46 @@
         gather_rest(low_ctx, counts, home, *refs[len(keys):len(keys) + others], pages_in)
     head = lax.axis_index("head")
     tokens, width = refs[0].shape
-    local_kv, most_pages = pages_in.shape[:2]
+    local_kv, _, most_pages = pages_in.shape[:3]
     span = width // local_kv
     per_group = span // HD
     piece_rows = per_group * tokens
     rows = len(groups[0]) * piece_rows
 
-    def visible_of(group):
+    def attend(pages):
+        span_rows = pages * PAGE
         row = lax.broadcasted_iota(jnp.int32, (rows, PAGE), 0)
-        token = lax.rem(row, tokens)
-        for i, (step, source) in enumerate(group):
-            first_token = ((head ^ step) * sub_count + source) * tokens
-            token = jnp.where(row // piece_rows == i, token + first_token, token)
-        return lax.broadcasted_iota(jnp.int32, (rows, PAGE), 1) <= PAGE - QR + token
-
-    def attend(pages):
+        column = lax.broadcasted_iota(jnp.int32, (rows, PAGE), 1)
+
+        def visible_of(group):
+            token = lax.rem(row, tokens)
+            for i, (step, source) in enumerate(group):
+                first_token = ((head ^ step) * sub_count + source) * tokens
+                token = jnp.where(row // piece_rows == i, token + first_token, token)
+            return column <= PAGE - QR + token
+
+        def of_pages(g, i):
+            return pages_in[g, i, 0:pages].reshape(span_rows, HD)
+
         def scores_of(group, g):
             q_blocks = [queries[key][:, g * span:(g + 1) * span] for key in group]
             q_rows = jnp.concatenate([q[:, j * HD:(j + 1) * HD] for q in q_blocks for j in range(per_group)], axis=0)
-            for p in range(pages):
-                scores = lax.dot_general(
-                    q_rows, pages_in[g, p, 0], (((1,), (1,)), ((), ())), preferred_element_type=jnp.float32
-                )
-                yield jnp.where(visible_of(group), scores, NEG) if p == pages - 1 else scores
+            scores = lax.dot_general(
+                q_rows, of_pages(g, 0), (((1,), (1,)), ((), ())), preferred_element_type=jnp.float32
+            )
+            scores = [scores[:, p * PAGE:(p + 1) * PAGE] for p in range(pages)]
+            scores[-1] = jnp.where(visible_of(group), scores[-1], NEG)
+            return scores
 
         units = [(group, g) for group in groups for g in range(local_kv)]
-        scores = list(scores_of(*units[0]))
+        scores = scores_of(*units[0])
         for n, (group, g) in enumerate(units):
-            following = scores_of(*units[n + 1]) if n + 1 < len(units) else iter(())
-            later = []
+            later = scores_of(*units[n + 1]) if n + 1 < len(units) else None
             top = jnp.max(functools.reduce(jnp.maximum, scores), axis=1, keepdims=True)
-            totals, product = None, None
-            for p in range(pages):
-                later += [s for _, s in zip(range(1), following)]
-                numerators = jnp.exp2((scores[p] - top) * EXP2_SCALE)
-                part = jnp.dot(
-                    numerators.astype(jnp.bfloat16), pages_in[g, p, 1], preferred_element_type=jnp.float32
-                )
-                totals = numerators if p == 0 else totals + numerators
-                product = part if p == 0 else product + part
-            totals = jnp.sum(totals, axis=1, keepdims=True)
+            numerators = [jnp.exp2((s - top) * EXP2_SCALE) for s in scores]
+            totals = jnp.sum(functools.reduce(jnp.add, numerators), axis=1, keepdims=True)
+            weights = jnp.concatenate([s.astype(jnp.bfloat16) for s in numerators], axis=1)
+            product = jnp.dot(weights, of_pages(g, 1), preferred_element_type=jnp.float32)
             done = (product / totals).astype(jnp.bfloat16)
             for i, key in enumerate(group):
                 start = i * piece_rows
@@ -230,12 +230,12 @@
     home, counts = pl.pallas_call(
         functools.partial(gather_home_kernel, low_ctx),
         out_shape=[
-            pltpu.VMEM((local_kv, most_pages, 2, PAGE, HD), kv_cache.dtype),
+            pltpu.VMEM((local_kv, 2, most_pages, PAGE, HD), kv_cache.dtype),
             pltpu.VMEM(page_counts.shape, page_counts.dtype),
         ],
         in_specs=[pl.BlockSpec(memory_space=pltpu.SMEM)] + [anywhere] * 3,
         out_specs=[anywhere] * 2,
-        scratch_shapes=[pltpu.SemaphoreType.DMA((local_kv, most_pages, 2)), pltpu.SemaphoreType.DMA],
+        scratch_shapes=[pltpu.SemaphoreType.DMA((local_kv, 2, most_pages)), pltpu.SemaphoreType.DMA],
         compiler_params=pltpu.CompilerParams(vmem_limit_bytes=2**20),
         name="gather_home",
     )(hbm(page_counts), hbm(page_counts), hbm(kv_cache), vmem(q_in[first]))

time: 48.5 us -> 48.3 us (level)
  the two profiles are of different devices: /device:TPU:1 before, /device:TPU:5 now
where the time goes in v4:
time: 48.3 us; the launch traced here: 47.9 us
  waiting for transfers between devices  25.2 us (52%)
  starting transfers between devices  17.3 us (36%)
  Pallas kernels  5.05 us (10%)
    ppermute x10, waiting for transfers between devices, moved(): lax.ppermute(array, ('ctx', 'head', 'sub'), [(flat(a), flat(b)) for a, b...  25.2 us
    ppermute x10, starting transfers between devices, moved(): lax.ppermute(array, ('ctx', 'head', 'sub'), [(flat(a), flat(b)) for a, b...  17.3 us
    pallas_call x1, Pallas kernels, one_request_each(): pl.pallas_call(functools.partial(gather_home_kernel, low_ctx), out_shape=...  1.7 us
    pallas_call x2, Pallas kernels, one_request_each(): pl.pallas_call(functools.partial(attend_kernel, low_ctx, sub_size, [keys]...  1.45 us
    pallas_call x1, Pallas kernels, one_request_each(): pl.pallas_call(split_kernel, out_shape=[q_piece] * head_count, in_specs=[...  1.06 us
  transfers between devices with their start and end apart: 10, of which 1 were waited for; matrix products, arithmetic and copies ran while one was open for 0% of the time, Pallas kernels for 9%

profile of v4, /device:TPU:5, one launch (start us, length us, event | category | flops | bytes accessed | tf_op | source)
XLA Modules:
  0.0 47.9 jit_solution(14423868410186334964)
XLA Ops:
  0.0 0.7 %collective-permute-start.3 = (bf16[2,512,512]{2,1,0:T(8,128)(2,1)}, bf16[2,512,512]{2,1,0:T(8,128)(2,1)S(1)}, u32[]{:S(2)}, u32[]{:S(2)}) collective-permute-start(bf16[2,512,512]{2,1,0:T(8,128)(2,1)} %own.1), channel_id=1, source_target_pairs={{8,9},{10,11},{9,0},{11,2},{12,13},{14,15},{13,12},{15,14},{24,25}... | collective-permute-start | bytes 3145736 | tf_op jit(solution)/shard_map/ppermute | solution.py:208
  0.7 0.7 %collective-permute-start.2 = (bf16[2,512,512]{2,1,0:T(8,128)(2,1)}, bf16[2,512,512]{2,1,0:T(8,128)(2,1)S(1)}, u32[]{:S(2)}, u32[]{:S(2)}) collective-permute-start(bf16[2,512,512]{2,1,0:T(8,128)(2,1)} %own.1), channel_id=1, source_target_pairs={{8,0},{10,2},{9,13},{11,15},{12,9},{14,11},{24,16},{26,18},{25,29}... | collective-permute-start | bytes 3145736 | tf_op jit(solution)/shard_map/ppermute | solution.py:208
  1.5 1.1 %split.1 = (bf16[16,8192]{1,0:T(8,128)(2,1)S(1)}, bf16[16,8192]{1,0:T(8,128)(2,1)S(1)}) custom-call(bf16[16,16384]{1,0:T(8,128)(2,1)} %queries.1), custom_call_target="tpu_custom_call" | custom-call | tf_op jit(solution)/shard_map/split/pallas_call | solution.py:215
  2.5 0.7 %collective-permute-start = (bf16[16,8192]{1,0:T(8,128)(2,1)S(1)}, bf16[16,8192]{1,0:T(8,128)(2,1)S(1)}, u32[]{:S(2)}, u32[]{:S(2)}) collective-permute-start(bf16[16,8192]{1,0:T(8,128)(2,1)S(1)} %get-tuple-element.17), channel_id=1, source_target_pairs={{0,2},{2,0},{4,11},{6,9},{8,15},{10,13},{12,14},{14,12},{16,18},{1... | collective-permute-start | bytes 786440 | tf_op jit(solution)/shard_map/ppermute | solution.py:208
  3.2 0.7 %collective-permute-start.1 = (bf16[16,8192]{1,0:T(8,128)(2,1)S(1)}, bf16[16,8192]{1,0:T(8,128)(2,1)S(1)}, u32[]{:S(2)}, u32[]{:S(2)}) collective-permute-start(bf16[16,8192]{1,0:T(8,128)(2,1)S(1)} %get-tuple-element.22), channel_id=1, source_target_pairs={{0,0},{2,2},{4,9},{6,11},{8,13},{10,15},{12,12},{14,14},{16,16},{1... | collective-permute-start | bytes 786440 | tf_op jit(solution)/shard_map/ppermute | solution.py:208
  3.9 6.6 %collective-permute-start.4 = (bf16[16,8192]{1,0:T(8,128)(2,1)S(1)}, bf16[16,8192]{1,0:T(8,128)(2,1)S(1)}, u32[]{:S(2)}, u32[]{:S(2)}) collective-permute-start(bf16[16,8192]{1,0:T(8,128)(2,1)S(1)} %get-tuple-element.17), channel_id=1, source_target_pairs={{1,2},{3,0},{5,11},{7,9},{9,15},{11,13},{13,14},{15,12},{17,18},{1... | collective-permute-start | bytes 786440 | tf_op jit(solution)/shard_map/ppermute | solution.py:208
  10.5 0.0 collective-permute-done.after.refs_0_
  10.5 1.7 %gather_home.1 = (bf16[4,2,4,256,128]{4,3,2,1,0:T(8,128)(2,1)S(1)}, s32[4]{0:T(128)S(1)}) custom-call(s32[4]{0:T(128)} %counts_in.1, s32[4]{0:T(128)} %counts_in.1, bf16[2,512,512]{2,1,0:T(8,128)(2,1)} %own.1, bf16[16,8192]{1,0:T(8,128)(2,1)S(1)} %collective-permute-done.after.refs_0_), custom_call_target="tpu_custom_call" | custom-call | tf_op jit(solution)/shard_map/gather_home/pallas_call | solution.py:230
  12.2 4.0 %collective-permute-start.5 = (bf16[16,8192]{1,0:T(8,128)(2,1)S(1)}, bf16[16,8192]{1,0:T(8,128)(2,1)S(1)}, u32[]{:S(2)}, u32[]{:S(2)}) collective-permute-start(bf16[16,8192]{1,0:T(8,128)(2,1)S(1)} %get-tuple-element.22), channel_id=1, source_target_pairs={{1,0},{3,2},{5,9},{7,11},{9,13},{11,15},{13,12},{15,14},{17,16},{1... | collective-permute-start | bytes 786440 | tf_op jit(solution)/shard_map/ppermute | solution.py:208
  16.2 0.0 collective-permute-done.1.refs_1_
  16.2 0.0 collective-permute-done.3.refs_3_
  16.2 0.0 collective-permute-done.2.refs_2_
  16.3 0.7 %attend_0.1 = (bf16[16,8192]{1,0:T(8,128)(2,1)S(1)}, bf16[16,8192]{1,0:T(8,128)(2,1)S(1)}, bf16[4,2,4,256,128]{4,3,2,1,0:T(8,128)(2,1)S(1)}) custom-call(s32[4]{0:T(128)S(1)} %get-tuple-element.19.counts, bf16[4,2,4,256,128]{4,3,2,1,0:T(8,128)(2,1)S(1)} %get-tuple-element.20.home, bf16[16,8192]{1,0:T(8,128)(2,1)S(1)} %collective-permute-done.after.refs_0_, ...), custom_call_target="tpu_custom_call" | custom-call | flops 10000000000 | bytes 4194304 | tf_op jit(solution)/shard_map/attend_0/pallas_call | solution.py:259
  16.9 0.7 %collective-permute-start.8 = (bf16[16,8192]{1,0:T(8,128)(2,1)S(1)}, bf16[16,8192]{1,0:T(8,128)(2,1)S(1)}, u32[]{:S(2)}, u32[]{:S(2)}) collective-permute-start(bf16[16,8192]{1,0:T(8,128)(2,1)S(1)} %get-tuple-element.25), channel_id=1, source_target_pairs={{2,0},{0,2},{11,4},{9,6},{15,8},{13,10},{14,12},{12,14},{18,16},{1... | collective-permute-start | bytes 786440 | tf_op jit(solution)/shard_map/ppermute | solution.py:208
  17.6 0.7 %collective-permute-start.9 = (bf16[16,8192]{1,0:T(8,128)(2,1)S(1)}, bf16[16,8192]{1,0:T(8,128)(2,1)S(1)}, u32[]{:S(2)}, u32[]{:S(2)}) collective-permute-start(bf16[16,8192]{1,0:T(8,128)(2,1)S(1)} %get-tuple-element.26), channel_id=1, source_target_pairs={{0,0},{2,2},{9,4},{11,6},{13,8},{15,10},{12,12},{14,14},{16,16},{1... | collective-permute-start | bytes 786440 | tf_op jit(solution)/shard_map/ppermute | solution.py:208
  18.3 0.0 collective-permute-done.4.refs_0_
  18.3 0.0 collective-permute-done.5.refs_1_
  18.3 0.8 %attend_1.1 = (bf16[16,8192]{1,0:T(8,128)(2,1)S(1)}, bf16[16,8192]{1,0:T(8,128)(2,1)S(1)}) custom-call(s32[4]{0:T(128)S(1)} %get-tuple-element.19.counts, bf16[4,2,4,256,128]{4,3,2,1,0:T(8,128)(2,1)S(1)} %get-tuple-element.21.home, bf16[16,8192]{1,0:T(8,128)(2,1)S(1)} %collective-permute-done.4.refs_0_, bf16[16,8192]{1,0:T(8,128)(2,1)S(1)} %collective-permute-done.5.refs_1_), custom_call_target="tpu_custom_call" | custom-call | flops 10000000000 | bytes 4194304 | tf_op jit(solution)/shard_map/attend_1/pallas_call | solution.py:259
  19.1 1.3 %collective-permute-start.6 = (bf16[16,8192]{1,0:T(8,128)(2,1)S(1)}, bf16[16,8192]{1,0:T(8,128)(2,1)S(1)}, u32[]{:S(2)}, u32[]{:S(2)}) collective-permute-start(bf16[16,8192]{1,0:T(8,128)(2,1)S(1)} %get-tuple-element.23), channel_id=1, source_target_pairs={{2,1},{0,3},{11,5},{9,7},{15,9},{13,11},{14,13},{12,15},{18,17},{1... | collective-permute-start | bytes 786440 | tf_op jit(solution)/shard_map/ppermute | solution.py:208
  20.4 1.3 %collective-permute-start.7 = (bf16[16,8192]{1,0:T(8,128)(2,1)S(1)}, bf16[16,8192]{1,0:T(8,128)(2,1)S(1)}, u32[]{:S(2)}, u32[]{:S(2)}) collective-permute-start(bf16[16,8192]{1,0:T(8,128)(2,1)S(1)} %get-tuple-element.24), channel_id=1, source_target_pairs={{0,1},{2,3},{9,5},{11,7},{13,9},{15,11},{12,13},{14,15},{16,17},{1... | collective-permute-start | bytes 786440 | tf_op jit(solution)/shard_map/ppermute | solution.py:208
  21.7 0.0 collective-permute-done.8.refs_0_
  21.7 0.0 collective-permute-done.9.refs_1_
  21.8 25.1 %collective-permute-done.6.refs_0_ = bf16[16,8192]{1,0:T(8,128)(2,1)S(1)} collective-permute-done((bf16[16,8192]{1,0:T(8,128)(2,1)S(1)}, bf16[16,8192]{1,0:T(8,128)(2,1)S(1)}, u32[]{:S(2)}, u32[]{:S(2)}) %collective-permute-start.6) | collective-permute-done | bytes 262176 | tf_op jit(solution)/shard_map/ppermute | solution.py:208
  46.9 0.0 collective-permute-done.7.refs_1_
  46.9 0.8 %join_1.1 = bf16[16,16384]{1,0:T(8,128)(2,1)} custom-call(bf16[16,8192]{1,0:T(8,128)(2,1)S(1)} %collective-permute-done.6.refs_0_, bf16[16,8192]{1,0:T(8,128)(2,1)S(1)} %collective-permute-done.7.refs_1_, bf16[16,16384]{1,0:T(8,128)(2,1)} %join_0.1.refs_2_), custom_call_target="tpu_custom_call", output_to_operand_aliasing={{}: (2, {})} | custom-call | tf_op jit(solution)/shard_map/join_1/pallas_call | solution.py:276
  (1 shorter events, 0.0 us)
Async XLA Ops:
  0.0 16.2 %collective-permute-start.3 = (bf16[2,512,512]{2,1,0:T(8,128)(2,1)}, bf16[2,512,512]{2,1,0:T(8,128)(2,1)S(1)}, u32[]{:S(2)}, u32[]{:S(2)}) collective-permute-start(bf16[2,512,512]{2,1,0:T(8,128)(2,1)} %own.1), channel_id=1, source_target_pairs={{8,9},{10,11},{9,0},{11,2},{12,13},{14,15},{13,12},{15,14},{24,25}... | collective-permute-start | bytes 3145736 | tf_op jit(solution)/shard_map/ppermute | solution.py:208
  0.7 15.5 %collective-permute-start.2 = (bf16[2,512,512]{2,1,0:T(8,128)(2,1)}, bf16[2,512,512]{2,1,0:T(8,128)(2,1)S(1)}, u32[]{:S(2)}, u32[]{:S(2)}) collective-permute-start(bf16[2,512,512]{2,1,0:T(8,128)(2,1)} %own.1), channel_id=1, source_target_pairs={{8,0},{10,2},{9,13},{11,15},{12,9},{14,11},{24,16},{26,18},{25,29}... | collective-permute-start | bytes 3145736 | tf_op jit(solution)/shard_map/ppermute | solution.py:208
  2.5 8.0 %collective-permute-start = (bf16[16,8192]{1,0:T(8,128)(2,1)S(1)}, bf16[16,8192]{1,0:T(8,128)(2,1)S(1)}, u32[]{:S(2)}, u32[]{:S(2)}) collective-permute-start(bf16[16,8192]{1,0:T(8,128)(2,1)S(1)} %get-tuple-element.17), channel_id=1, source_target_pairs={{0,2},{2,0},{4,11},{6,9},{8,15},{10,13},{12,14},{14,12},{16,18},{1... | collective-permute-start | bytes 786440 | tf_op jit(solution)/shard_map/ppermute | solution.py:208
  3.2 13.0 %collective-permute-start.1 = (bf16[16,8192]{1,0:T(8,128)(2,1)S(1)}, bf16[16,8192]{1,0:T(8,128)(2,1)S(1)}, u32[]{:S(2)}, u32[]{:S(2)}) collective-permute-start(bf16[16,8192]{1,0:T(8,128)(2,1)S(1)} %get-tuple-element.22), channel_id=1, source_target_pairs={{0,0},{2,2},{4,9},{6,11},{8,13},{10,15},{12,12},{14,14},{16,16},{1... | collective-permute-start | bytes 786440 | tf_op jit(solution)/shard_map/ppermute | solution.py:208
  3.9 14.4 %collective-permute-start.4 = (bf16[16,8192]{1,0:T(8,128)(2,1)S(1)}, bf16[16,8192]{1,0:T(8,128)(2,1)S(1)}, u32[]{:S(2)}, u32[]{:S(2)}) collective-permute-start(bf16[16,8192]{1,0:T(8,128)(2,1)S(1)} %get-tuple-element.17), channel_id=1, source_target_pairs={{1,2},{3,0},{5,11},{7,9},{9,15},{11,13},{13,14},{15,12},{17,18},{1... | collective-permute-start | bytes 786440 | tf_op jit(solution)/shard_map/ppermute | solution.py:208
  12.2 6.1 %collective-permute-start.5 = (bf16[16,8192]{1,0:T(8,128)(2,1)S(1)}, bf16[16,8192]{1,0:T(8,128)(2,1)S(1)}, u32[]{:S(2)}, u32[]{:S(2)}) collective-permute-start(bf16[16,8192]{1,0:T(8,128)(2,1)S(1)} %get-tuple-element.22), channel_id=1, source_target_pairs={{1,0},{3,2},{5,9},{7,11},{9,13},{11,15},{13,12},{15,14},{17,16},{1... | collective-permute-start | bytes 786440 | tf_op jit(solution)/shard_map/ppermute | solution.py:208
  16.9 4.8 %collective-permute-start.8 = (bf16[16,8192]{1,0:T(8,128)(2,1)S(1)}, bf16[16,8192]{1,0:T(8,128)(2,1)S(1)}, u32[]{:S(2)}, u32[]{:S(2)}) collective-permute-start(bf16[16,8192]{1,0:T(8,128)(2,1)S(1)} %get-tuple-element.25), channel_id=1, source_target_pairs={{2,0},{0,2},{11,4},{9,6},{15,8},{13,10},{14,12},{12,14},{18,16},{1... | collective-permute-start | bytes 786440 | tf_op jit(solution)/shard_map/ppermute | solution.py:208
  17.6 4.1 %collective-permute-start.9 = (bf16[16,8192]{1,0:T(8,128)(2,1)S(1)}, bf16[16,8192]{1,0:T(8,128)(2,1)S(1)}, u32[]{:S(2)}, u32[]{:S(2)}) collective-permute-start(bf16[16,8192]{1,0:T(8,128)(2,1)S(1)} %get-tuple-element.26), channel_id=1, source_target_pairs={{0,0},{2,2},{9,4},{11,6},{13,8},{15,10},{12,12},{14,14},{16,16},{1... | collective-permute-start | bytes 786440 | tf_op jit(solution)/shard_map/ppermute | solution.py:208
  19.1 27.8 %collective-permute-start.6 = (bf16[16,8192]{1,0:T(8,128)(2,1)S(1)}, bf16[16,8192]{1,0:T(8,128)(2,1)S(1)}, u32[]{:S(2)}, u32[]{:S(2)}) collective-permute-start(bf16[16,8192]{1,0:T(8,128)(2,1)S(1)} %get-tuple-element.23), channel_id=1, source_target_pairs={{2,1},{0,3},{11,5},{9,7},{15,9},{13,11},{14,13},{12,15},{18,17},{1... | collective-permute-start | bytes 786440 | tf_op jit(solution)/shard_map/ppermute | solution.py:208
  20.4 26.5 %collective-permute-start.7 = (bf16[16,8192]{1,0:T(8,128)(2,1)S(1)}, bf16[16,8192]{1,0:T(8,128)(2,1)S(1)}, u32[]{:S(2)}, u32[]{:S(2)}) collective-permute-start(bf16[16,8192]{1,0:T(8,128)(2,1)S(1)} %get-tuple-element.24), channel_id=1, source_target_pairs={{0,1},{2,3},{9,5},{11,7},{13,9},{15,11},{12,13},{14,15},{16,17},{1... | collective-permute-start | bytes 786440 | tf_op jit(solution)/shard_map/ppermute | solution.py:208

commit v5 on v4

--- a/solution.py
+++ b/solution.py
@@ -161,11 +161,10 @@
         for n, (group, g) in enumerate(units):
             later = scores_of(*units[n + 1]) if n + 1 < len(units) else None
             top = jnp.max(functools.reduce(jnp.maximum, scores), axis=1, keepdims=True)
-            numerators = [jnp.exp2((s - top) * EXP2_SCALE) for s in scores]
-            totals = jnp.sum(functools.reduce(jnp.add, numerators), axis=1, keepdims=True)
-            weights = jnp.concatenate([s.astype(jnp.bfloat16) for s in numerators], axis=1)
-            product = jnp.dot(weights, of_pages(g, 1), preferred_element_type=jnp.float32)
-            done = (product / totals).astype(jnp.bfloat16)
+            weights = [jnp.exp2(((s - top) * EXP2_SCALE).astype(jnp.bfloat16)) for s in scores]
+            values = jnp.concatenate([of_pages(g, 1), jnp.ones((span_rows, HD), jnp.bfloat16)], axis=1)
+            product = jnp.dot(jnp.concatenate(weights, axis=1), values, preferred_element_type=jnp.float32)
+            done = (product[:, :HD] / product[:, HD:]).astype(jnp.bfloat16)
             for i, key in enumerate(group):
                 start = i * piece_rows
                 outs[key][:, g * span:(g + 1) * span] = jnp.concatenate(

time: 48.3 us -> 48.2 us (level)
  no operation moved by 1% of the time
where the time goes in v5:
time: 48.2 us; the launch traced here: 47.7 us
  waiting for transfers between devices  24.9 us (52%)
  starting transfers between devices  17.3 us (36%)
  Pallas kernels  5.05 us (10%)
    ppermute x10, waiting for transfers between devices, moved(): lax.ppermute(array, ('ctx', 'head', 'sub'), [(flat(a), flat(b)) for a, b...  24.9 us
    ppermute x10, starting transfers between devices, moved(): lax.ppermute(array, ('ctx', 'head', 'sub'), [(flat(a), flat(b)) for a, b...  17.3 us
    pallas_call x1, Pallas kernels, one_request_each(): pl.pallas_call(functools.partial(gather_home_kernel, low_ctx), out_shape=...  1.7 us
    pallas_call x2, Pallas kernels, one_request_each(): pl.pallas_call(functools.partial(attend_kernel, low_ctx, sub_size, [keys]...  1.45 us
    pallas_call x1, Pallas kernels, one_request_each(): pl.pallas_call(split_kernel, out_shape=[q_piece] * head_count, in_specs=[...  1.06 us
  transfers between devices with their start and end apart: 10, of which 1 were waited for; matrix products, arithmetic and copies ran while one was open for 0% of the time, Pallas kernels for 9%

profile of v5, /device:TPU:5, one launch (start us, length us, event | category | flops | bytes accessed | tf_op | source)
XLA Modules:
  0.0 47.7 jit_solution(4442209120155854425)
XLA Ops:
  0.0 0.7 %collective-permute-start.3 = (bf16[2,512,512]{2,1,0:T(8,128)(2,1)}, bf16[2,512,512]{2,1,0:T(8,128)(2,1)S(1)}, u32[]{:S(2)}, u32[]{:S(2)}) collective-permute-start(bf16[2,512,512]{2,1,0:T(8,128)(2,1)} %own.1), channel_id=1, source_target_pairs={{8,9},{10,11},{9,0},{11,2},{12,13},{14,15},{13,12},{15,14},{24,25}... | collective-permute-start | bytes 3145736 | tf_op jit(solution)/shard_map/ppermute | solution.py:207
  0.7 0.7 %collective-permute-start.2 = (bf16[2,512,512]{2,1,0:T(8,128)(2,1)}, bf16[2,512,512]{2,1,0:T(8,128)(2,1)S(1)}, u32[]{:S(2)}, u32[]{:S(2)}) collective-permute-start(bf16[2,512,512]{2,1,0:T(8,128)(2,1)} %own.1), channel_id=1, source_target_pairs={{8,0},{10,2},{9,13},{11,15},{12,9},{14,11},{24,16},{26,18},{25,29}... | collective-permute-start | bytes 3145736 | tf_op jit(solution)/shard_map/ppermute | solution.py:207
  1.5 1.1 %split.1 = (bf16[16,8192]{1,0:T(8,128)(2,1)S(1)}, bf16[16,8192]{1,0:T(8,128)(2,1)S(1)}) custom-call(bf16[16,16384]{1,0:T(8,128)(2,1)} %queries.1), custom_call_target="tpu_custom_call" | custom-call | tf_op jit(solution)/shard_map/split/pallas_call | solution.py:214
  2.5 0.7 %collective-permute-start = (bf16[16,8192]{1,0:T(8,128)(2,1)S(1)}, bf16[16,8192]{1,0:T(8,128)(2,1)S(1)}, u32[]{:S(2)}, u32[]{:S(2)}) collective-permute-start(bf16[16,8192]{1,0:T(8,128)(2,1)S(1)} %get-tuple-element.17), channel_id=1, source_target_pairs={{0,2},{2,0},{4,11},{6,9},{8,15},{10,13},{12,14},{14,12},{16,18},{1... | collective-permute-start | bytes 786440 | tf_op jit(solution)/shard_map/ppermute | solution.py:207
  3.2 0.7 %collective-permute-start.1 = (bf16[16,8192]{1,0:T(8,128)(2,1)S(1)}, bf16[16,8192]{1,0:T(8,128)(2,1)S(1)}, u32[]{:S(2)}, u32[]{:S(2)}) collective-permute-start(bf16[16,8192]{1,0:T(8,128)(2,1)S(1)} %get-tuple-element.22), channel_id=1, source_target_pairs={{0,0},{2,2},{4,9},{6,11},{8,13},{10,15},{12,12},{14,14},{16,16},{1... | collective-permute-start | bytes 786440 | tf_op jit(solution)/shard_map/ppermute | solution.py:207
  3.9 6.6 %collective-permute-start.4 = (bf16[16,8192]{1,0:T(8,128)(2,1)S(1)}, bf16[16,8192]{1,0:T(8,128)(2,1)S(1)}, u32[]{:S(2)}, u32[]{:S(2)}) collective-permute-start(bf16[16,8192]{1,0:T(8,128)(2,1)S(1)} %get-tuple-element.17), channel_id=1, source_target_pairs={{1,2},{3,0},{5,11},{7,9},{9,15},{11,13},{13,14},{15,12},{17,18},{1... | collective-permute-start | bytes 786440 | tf_op jit(solution)/shard_map/ppermute | solution.py:207
  10.5 0.0 collective-permute-done.after.refs_0_
  10.5 1.7 %gather_home.1 = (bf16[4,2,4,256,128]{4,3,2,1,0:T(8,128)(2,1)S(1)}, s32[4]{0:T(128)S(1)}) custom-call(s32[4]{0:T(128)} %counts_in.1, s32[4]{0:T(128)} %counts_in.1, bf16[2,512,512]{2,1,0:T(8,128)(2,1)} %own.1, bf16[16,8192]{1,0:T(8,128)(2,1)S(1)} %collective-permute-done.after.refs_0_), custom_call_target="tpu_custom_call" | custom-call | tf_op jit(solution)/shard_map/gather_home/pallas_call | solution.py:229
  12.2 4.0 %collective-permute-start.5 = (bf16[16,8192]{1,0:T(8,128)(2,1)S(1)}, bf16[16,8192]{1,0:T(8,128)(2,1)S(1)}, u32[]{:S(2)}, u32[]{:S(2)}) collective-permute-start(bf16[16,8192]{1,0:T(8,128)(2,1)S(1)} %get-tuple-element.22), channel_id=1, source_target_pairs={{1,0},{3,2},{5,9},{7,11},{9,13},{11,15},{13,12},{15,14},{17,16},{1... | collective-permute-start | bytes 786440 | tf_op jit(solution)/shard_map/ppermute | solution.py:207
  16.2 0.0 collective-permute-done.1.refs_1_
  16.2 0.0 collective-permute-done.3.refs_3_
  16.2 0.0 collective-permute-done.2.refs_2_
  16.3 0.7 %attend_0.1 = (bf16[16,8192]{1,0:T(8,128)(2,1)S(1)}, bf16[16,8192]{1,0:T(8,128)(2,1)S(1)}, bf16[4,2,4,256,128]{4,3,2,1,0:T(8,128)(2,1)S(1)}) custom-call(s32[4]{0:T(128)S(1)} %get-tuple-element.19.counts, bf16[4,2,4,256,128]{4,3,2,1,0:T(8,128)(2,1)S(1)} %get-tuple-element.20.home, bf16[16,8192]{1,0:T(8,128)(2,1)S(1)} %collective-permute-done.after.refs_0_, ...), custom_call_target="tpu_custom_call" | custom-call | flops 10000000000 | bytes 4194304 | tf_op jit(solution)/shard_map/attend_0/pallas_call | solution.py:258
  16.9 0.7 %collective-permute-start.8 = (bf16[16,8192]{1,0:T(8,128)(2,1)S(1)}, bf16[16,8192]{1,0:T(8,128)(2,1)S(1)}, u32[]{:S(2)}, u32[]{:S(2)}) collective-permute-start(bf16[16,8192]{1,0:T(8,128)(2,1)S(1)} %get-tuple-element.25), channel_id=1, source_target_pairs={{2,0},{0,2},{11,4},{9,6},{15,8},{13,10},{14,12},{12,14},{18,16},{1... | collective-permute-start | bytes 786440 | tf_op jit(solution)/shard_map/ppermute | solution.py:207
  17.6 0.7 %collective-permute-start.9 = (bf16[16,8192]{1,0:T(8,128)(2,1)S(1)}, bf16[16,8192]{1,0:T(8,128)(2,1)S(1)}, u32[]{:S(2)}, u32[]{:S(2)}) collective-permute-start(bf16[16,8192]{1,0:T(8,128)(2,1)S(1)} %get-tuple-element.26), channel_id=1, source_target_pairs={{0,0},{2,2},{9,4},{11,6},{13,8},{15,10},{12,12},{14,14},{16,16},{1... | collective-permute-start | bytes 786440 | tf_op jit(solution)/shard_map/ppermute | solution.py:207
  18.3 0.0 collective-permute-done.4.refs_0_
  18.3 0.0 collective-permute-done.5.refs_1_
  18.3 0.8 %attend_1.1 = (bf16[16,8192]{1,0:T(8,128)(2,1)S(1)}, bf16[16,8192]{1,0:T(8,128)(2,1)S(1)}) custom-call(s32[4]{0:T(128)S(1)} %get-tuple-element.19.counts, bf16[4,2,4,256,128]{4,3,2,1,0:T(8,128)(2,1)S(1)} %get-tuple-element.21.home, bf16[16,8192]{1,0:T(8,128)(2,1)S(1)} %collective-permute-done.4.refs_0_, bf16[16,8192]{1,0:T(8,128)(2,1)S(1)} %collective-permute-done.5.refs_1_), custom_call_target="tpu_custom_call" | custom-call | flops 10000000000 | bytes 4194304 | tf_op jit(solution)/shard_map/attend_1/pallas_call | solution.py:258
  19.1 1.3 %collective-permute-start.6 = (bf16[16,8192]{1,0:T(8,128)(2,1)S(1)}, bf16[16,8192]{1,0:T(8,128)(2,1)S(1)}, u32[]{:S(2)}, u32[]{:S(2)}) collective-permute-start(bf16[16,8192]{1,0:T(8,128)(2,1)S(1)} %get-tuple-element.23), channel_id=1, source_target_pairs={{2,1},{0,3},{11,5},{9,7},{15,9},{13,11},{14,13},{12,15},{18,17},{1... | collective-permute-start | bytes 786440 | tf_op jit(solution)/shard_map/ppermute | solution.py:207
  20.4 1.3 %collective-permute-start.7 = (bf16[16,8192]{1,0:T(8,128)(2,1)S(1)}, bf16[16,8192]{1,0:T(8,128)(2,1)S(1)}, u32[]{:S(2)}, u32[]{:S(2)}) collective-permute-start(bf16[16,8192]{1,0:T(8,128)(2,1)S(1)} %get-tuple-element.24), channel_id=1, source_target_pairs={{0,1},{2,3},{9,5},{11,7},{13,9},{15,11},{12,13},{14,15},{16,17},{1... | collective-permute-start | bytes 786440 | tf_op jit(solution)/shard_map/ppermute | solution.py:207
  21.7 0.0 collective-permute-done.8.refs_0_
  21.7 0.0 collective-permute-done.9.refs_1_
  21.8 24.9 %collective-permute-done.6.refs_0_ = bf16[16,8192]{1,0:T(8,128)(2,1)S(1)} collective-permute-done((bf16[16,8192]{1,0:T(8,128)(2,1)S(1)}, bf16[16,8192]{1,0:T(8,128)(2,1)S(1)}, u32[]{:S(2)}, u32[]{:S(2)}) %collective-permute-start.6) | collective-permute-done | bytes 262176 | tf_op jit(solution)/shard_map/ppermute | solution.py:207
  46.7 0.0 collective-permute-done.7.refs_1_
  46.7 0.8 %join_1.1 = bf16[16,16384]{1,0:T(8,128)(2,1)} custom-call(bf16[16,8192]{1,0:T(8,128)(2,1)S(1)} %collective-permute-done.6.refs_0_, bf16[16,8192]{1,0:T(8,128)(2,1)S(1)} %collective-permute-done.7.refs_1_, bf16[16,16384]{1,0:T(8,128)(2,1)} %join_0.1.refs_2_), custom_call_target="tpu_custom_call", output_to_operand_aliasing={{}: (2, {})} | custom-call | tf_op jit(solution)/shard_map/join_1/pallas_call | solution.py:275
  (1 shorter events, 0.0 us)
Async XLA Ops:
  0.0 16.2 %collective-permute-start.3 = (bf16[2,512,512]{2,1,0:T(8,128)(2,1)}, bf16[2,512,512]{2,1,0:T(8,128)(2,1)S(1)}, u32[]{:S(2)}, u32[]{:S(2)}) collective-permute-start(bf16[2,512,512]{2,1,0:T(8,128)(2,1)} %own.1), channel_id=1, source_target_pairs={{8,9},{10,11},{9,0},{11,2},{12,13},{14,15},{13,12},{15,14},{24,25}... | collective-permute-start | bytes 3145736 | tf_op jit(solution)/shard_map/ppermute | solution.py:207
  0.7 15.5 %collective-permute-start.2 = (bf16[2,512,512]{2,1,0:T(8,128)(2,1)}, bf16[2,512,512]{2,1,0:T(8,128)(2,1)S(1)}, u32[]{:S(2)}, u32[]{:S(2)}) collective-permute-start(bf16[2,512,512]{2,1,0:T(8,128)(2,1)} %own.1), channel_id=1, source_target_pairs={{8,0},{10,2},{9,13},{11,15},{12,9},{14,11},{24,16},{26,18},{25,29}... | collective-permute-start | bytes 3145736 | tf_op jit(solution)/shard_map/ppermute | solution.py:207
  2.5 8.0 %collective-permute-start = (bf16[16,8192]{1,0:T(8,128)(2,1)S(1)}, bf16[16,8192]{1,0:T(8,128)(2,1)S(1)}, u32[]{:S(2)}, u32[]{:S(2)}) collective-permute-start(bf16[16,8192]{1,0:T(8,128)(2,1)S(1)} %get-tuple-element.17), channel_id=1, source_target_pairs={{0,2},{2,0},{4,11},{6,9},{8,15},{10,13},{12,14},{14,12},{16,18},{1... | collective-permute-start | bytes 786440 | tf_op jit(solution)/shard_map/ppermute | solution.py:207
  3.2 13.0 %collective-permute-start.1 = (bf16[16,8192]{1,0:T(8,128)(2,1)S(1)}, bf16[16,8192]{1,0:T(8,128)(2,1)S(1)}, u32[]{:S(2)}, u32[]{:S(2)}) collective-permute-start(bf16[16,8192]{1,0:T(8,128)(2,1)S(1)} %get-tuple-element.22), channel_id=1, source_target_pairs={{0,0},{2,2},{4,9},{6,11},{8,13},{10,15},{12,12},{14,14},{16,16},{1... | collective-permute-start | bytes 786440 | tf_op jit(solution)/shard_map/ppermute | solution.py:207
  3.9 14.4 %collective-permute-start.4 = (bf16[16,8192]{1,0:T(8,128)(2,1)S(1)}, bf16[16,8192]{1,0:T(8,128)(2,1)S(1)}, u32[]{:S(2)}, u32[]{:S(2)}) collective-permute-start(bf16[16,8192]{1,0:T(8,128)(2,1)S(1)} %get-tuple-element.17), channel_id=1, source_target_pairs={{1,2},{3,0},{5,11},{7,9},{9,15},{11,13},{13,14},{15,12},{17,18},{1... | collective-permute-start | bytes 786440 | tf_op jit(solution)/shard_map/ppermute | solution.py:207
  12.2 6.1 %collective-permute-start.5 = (bf16[16,8192]{1,0:T(8,128)(2,1)S(1)}, bf16[16,8192]{1,0:T(8,128)(2,1)S(1)}, u32[]{:S(2)}, u32[]{:S(2)}) collective-permute-start(bf16[16,8192]{1,0:T(8,128)(2,1)S(1)} %get-tuple-element.22), channel_id=1, source_target_pairs={{1,0},{3,2},{5,9},{7,11},{9,13},{11,15},{13,12},{15,14},{17,16},{1... | collective-permute-start | bytes 786440 | tf_op jit(solution)/shard_map/ppermute | solution.py:207
  16.9 4.8 %collective-permute-start.8 = (bf16[16,8192]{1,0:T(8,128)(2,1)S(1)}, bf16[16,8192]{1,0:T(8,128)(2,1)S(1)}, u32[]{:S(2)}, u32[]{:S(2)}) collective-permute-start(bf16[16,8192]{1,0:T(8,128)(2,1)S(1)} %get-tuple-element.25), channel_id=1, source_target_pairs={{2,0},{0,2},{11,4},{9,6},{15,8},{13,10},{14,12},{12,14},{18,16},{1... | collective-permute-start | bytes 786440 | tf_op jit(solution)/shard_map/ppermute | solution.py:207
  17.6 4.1 %collective-permute-start.9 = (bf16[16,8192]{1,0:T(8,128)(2,1)S(1)}, bf16[16,8192]{1,0:T(8,128)(2,1)S(1)}, u32[]{:S(2)}, u32[]{:S(2)}) collective-permute-start(bf16[16,8192]{1,0:T(8,128)(2,1)S(1)} %get-tuple-element.26), channel_id=1, source_target_pairs={{0,0},{2,2},{9,4},{11,6},{13,8},{15,10},{12,12},{14,14},{16,16},{1... | collective-permute-start | bytes 786440 | tf_op jit(solution)/shard_map/ppermute | solution.py:207
  19.1 27.6 %collective-permute-start.6 = (bf16[16,8192]{1,0:T(8,128)(2,1)S(1)}, bf16[16,8192]{1,0:T(8,128)(2,1)S(1)}, u32[]{:S(2)}, u32[]{:S(2)}) collective-permute-start(bf16[16,8192]{1,0:T(8,128)(2,1)S(1)} %get-tuple-element.23), channel_id=1, source_target_pairs={{2,1},{0,3},{11,5},{9,7},{15,9},{13,11},{14,13},{12,15},{18,17},{1... | collective-permute-start | bytes 786440 | tf_op jit(solution)/shard_map/ppermute | solution.py:207
  20.4 26.3 %collective-permute-start.7 = (bf16[16,8192]{1,0:T(8,128)(2,1)S(1)}, bf16[16,8192]{1,0:T(8,128)(2,1)S(1)}, u32[]{:S(2)}, u32[]{:S(2)}) collective-permute-start(bf16[16,8192]{1,0:T(8,128)(2,1)S(1)} %get-tuple-element.24), channel_id=1, source_target_pairs={{0,1},{2,3},{9,5},{11,7},{13,9},{15,11},{12,13},{14,15},{16,17},{1... | collective-permute-start | bytes 786440 | tf_op jit(solution)/shard_map/ppermute | solution.py:207

commit v6 on v4

--- a/solution.py
+++ b/solution.py
@@ -101,7 +101,7 @@
     counts_copy.wait()
 
 
-def gather_rest(low_ctx, counts, home, far, near, out):
+def gather_rest(low_ctx, counts, home, near, far, out):
     local_kv, _, most_pages = out.shape[:3]
     for p, here, which, rows in pages_of(low_ctx, counts, most_pages):
         @pl.when(here & (which == 0))
@@ -254,7 +254,7 @@
     )
     groups = [[(step, s) for step in heads[::-1]] for s in range(sub_size)]
     back = {}
-    pages, others = home, [vmem(far), vmem(near)]
+    pages, others = home, [vmem(near), vmem(far)]
     for keys in groups:
         outs = pl.pallas_call(
             functools.partial(attend_kernel, low_ctx, sub_size, [keys], len(others)),

time: 48.3 us -> 49.3 us (1.021)
  the two profiles are of different devices: /device:TPU:5 before, /device:TPU:1 now
where the time goes in v6:
time: 49.3 us; the launch traced here: 48.8 us
  waiting for transfers between devices  25.5 us (52%)
  starting transfers between devices  17.9 us (36%)
  Pallas kernels  5.05 us (10%)
    ppermute x10, waiting for transfers between devices, moved(): lax.ppermute(array, ('ctx', 'head', 'sub'), [(flat(a), flat(b)) for a, b...  25.5 us
    ppermute x10, starting transfers between devices, moved(): lax.ppermute(array, ('ctx', 'head', 'sub'), [(flat(a), flat(b)) for a, b...  17.9 us
    pallas_call x1, Pallas kernels, one_request_each(): pl.pallas_call(functools.partial(gather_home_kernel, low_ctx), out_shape=...  1.7 us
    pallas_call x2, Pallas kernels, one_request_each(): pl.pallas_call(functools.partial(attend_kernel, low_ctx, sub_size, [keys]...  1.45 us
    pallas_call x1, Pallas kernels, one_request_each(): pl.pallas_call(split_kernel, out_shape=[q_piece] * head_count, in_specs=[...  1.06 us
  transfers between devices with their start and end apart: 10, of which 1 were waited for; matrix products, arithmetic and copies ran while one was open for 0% of the time, Pallas kernels for 9%

profile of v6, /device:TPU:1, one launch (start us, length us, event | category | flops | bytes accessed | tf_op | source)
XLA Modules:
  0.0 48.8 jit_solution(14733944380215859689)
XLA Ops:
  0.0 0.7 %collective-permute-start.3 = (bf16[2,512,512]{2,1,0:T(8,128)(2,1)}, bf16[2,512,512]{2,1,0:T(8,128)(2,1)S(1)}, u32[]{:S(2)}, u32[]{:S(2)}) collective-permute-start(bf16[2,512,512]{2,1,0:T(8,128)(2,1)} %own.1), channel_id=1, source_target_pairs={{8,0},{10,2},{9,13},{11,15},{12,9},{14,11},{24,16},{26,18},{25,29}... | collective-permute-start | bytes 3145736 | tf_op jit(solution)/shard_map/ppermute | solution.py:208
  0.7 0.7 %collective-permute-start.2 = (bf16[2,512,512]{2,1,0:T(8,128)(2,1)}, bf16[2,512,512]{2,1,0:T(8,128)(2,1)S(1)}, u32[]{:S(2)}, u32[]{:S(2)}) collective-permute-start(bf16[2,512,512]{2,1,0:T(8,128)(2,1)} %own.1), channel_id=1, source_target_pairs={{8,9},{10,11},{9,0},{11,2},{12,13},{14,15},{13,12},{15,14},{24,25}... | collective-permute-start | bytes 3145736 | tf_op jit(solution)/shard_map/ppermute | solution.py:208
  1.5 1.1 %split.1 = (bf16[16,8192]{1,0:T(8,128)(2,1)S(1)}, bf16[16,8192]{1,0:T(8,128)(2,1)S(1)}) custom-call(bf16[16,16384]{1,0:T(8,128)(2,1)} %queries.1), custom_call_target="tpu_custom_call" | custom-call | tf_op jit(solution)/shard_map/split/pallas_call | solution.py:215
  2.5 0.7 %collective-permute-start = (bf16[16,8192]{1,0:T(8,128)(2,1)S(1)}, bf16[16,8192]{1,0:T(8,128)(2,1)S(1)}, u32[]{:S(2)}, u32[]{:S(2)}) collective-permute-start(bf16[16,8192]{1,0:T(8,128)(2,1)S(1)} %get-tuple-element.17), channel_id=1, source_target_pairs={{0,2},{2,0},{4,11},{6,9},{8,15},{10,13},{12,14},{14,12},{16,18},{1... | collective-permute-start | bytes 786440 | tf_op jit(solution)/shard_map/ppermute | solution.py:208
  3.2 0.7 %collective-permute-start.1 = (bf16[16,8192]{1,0:T(8,128)(2,1)S(1)}, bf16[16,8192]{1,0:T(8,128)(2,1)S(1)}, u32[]{:S(2)}, u32[]{:S(2)}) collective-permute-start(bf16[16,8192]{1,0:T(8,128)(2,1)S(1)} %get-tuple-element.22), channel_id=1, source_target_pairs={{0,0},{2,2},{4,9},{6,11},{8,13},{10,15},{12,12},{14,14},{16,16},{1... | collective-permute-start | bytes 786440 | tf_op jit(solution)/shard_map/ppermute | solution.py:208
  3.9 6.9 %collective-permute-start.4 = (bf16[16,8192]{1,0:T(8,128)(2,1)S(1)}, bf16[16,8192]{1,0:T(8,128)(2,1)S(1)}, u32[]{:S(2)}, u32[]{:S(2)}) collective-permute-start(bf16[16,8192]{1,0:T(8,128)(2,1)S(1)} %get-tuple-element.17), channel_id=1, source_target_pairs={{1,2},{3,0},{5,11},{7,9},{9,15},{11,13},{13,14},{15,12},{17,18},{1... | collective-permute-start | bytes 786440 | tf_op jit(solution)/shard_map/ppermute | solution.py:208
  10.8 0.0 collective-permute-done.after.refs_0_
  10.8 1.7 %gather_home.1 = (bf16[4,2,4,256,128]{4,3,2,1,0:T(8,128)(2,1)S(1)}, s32[4]{0:T(128)S(1)}) custom-call(s32[4]{0:T(128)} %counts_in.1, s32[4]{0:T(128)} %counts_in.1, bf16[2,512,512]{2,1,0:T(8,128)(2,1)} %own.1, bf16[16,8192]{1,0:T(8,128)(2,1)S(1)} %collective-permute-done.after.refs_0_), custom_call_target="tpu_custom_call" | custom-call | tf_op jit(solution)/shard_map/gather_home/pallas_call | solution.py:230
  12.5 4.2 %collective-permute-start.5 = (bf16[16,8192]{1,0:T(8,128)(2,1)S(1)}, bf16[16,8192]{1,0:T(8,128)(2,1)S(1)}, u32[]{:S(2)}, u32[]{:S(2)}) collective-permute-start(bf16[16,8192]{1,0:T(8,128)(2,1)S(1)} %get-tuple-element.22), channel_id=1, source_target_pairs={{1,0},{3,2},{5,9},{7,11},{9,13},{11,15},{13,12},{15,14},{17,16},{1... | collective-permute-start | bytes 786440 | tf_op jit(solution)/shard_map/ppermute | solution.py:208
  16.8 0.0 collective-permute-done.1.refs_1_
  16.8 0.0 collective-permute-done.3.refs_3_
  16.8 0.0 collective-permute-done.2.refs_2_
  16.8 0.7 %attend_0.1 = (bf16[16,8192]{1,0:T(8,128)(2,1)S(1)}, bf16[16,8192]{1,0:T(8,128)(2,1)S(1)}, bf16[4,2,4,256,128]{4,3,2,1,0:T(8,128)(2,1)S(1)}) custom-call(s32[4]{0:T(128)S(1)} %get-tuple-element.19.counts, bf16[4,2,4,256,128]{4,3,2,1,0:T(8,128)(2,1)S(1)} %get-tuple-element.20.home, bf16[16,8192]{1,0:T(8,128)(2,1)S(1)} %collective-permute-done.after.refs_0_, ...), custom_call_target="tpu_custom_call" | custom-call | flops 10000000000 | bytes 4194304 | tf_op jit(solution)/shard_map/attend_0/pallas_call | solution.py:259
  17.5 0.7 %collective-permute-start.8 = (bf16[16,8192]{1,0:T(8,128)(2,1)S(1)}, bf16[16,8192]{1,0:T(8,128)(2,1)S(1)}, u32[]{:S(2)}, u32[]{:S(2)}) collective-permute-start(bf16[16,8192]{1,0:T(8,128)(2,1)S(1)} %get-tuple-element.25), channel_id=1, source_target_pairs={{2,0},{0,2},{11,4},{9,6},{15,8},{13,10},{14,12},{12,14},{18,16},{1... | collective-permute-start | bytes 786440 | tf_op jit(solution)/shard_map/ppermute | solution.py:208
  18.2 0.7 %collective-permute-start.9 = (bf16[16,8192]{1,0:T(8,128)(2,1)S(1)}, bf16[16,8192]{1,0:T(8,128)(2,1)S(1)}, u32[]{:S(2)}, u32[]{:S(2)}) collective-permute-start(bf16[16,8192]{1,0:T(8,128)(2,1)S(1)} %get-tuple-element.26), channel_id=1, source_target_pairs={{0,0},{2,2},{9,4},{11,6},{13,8},{15,10},{12,12},{14,14},{16,16},{1... | collective-permute-start | bytes 786440 | tf_op jit(solution)/shard_map/ppermute | solution.py:208
  18.8 0.0 collective-permute-done.4.refs_0_
  18.9 0.0 collective-permute-done.5.refs_1_
  18.9 0.8 %attend_1.1 = (bf16[16,8192]{1,0:T(8,128)(2,1)S(1)}, bf16[16,8192]{1,0:T(8,128)(2,1)S(1)}) custom-call(s32[4]{0:T(128)S(1)} %get-tuple-element.19.counts, bf16[4,2,4,256,128]{4,3,2,1,0:T(8,128)(2,1)S(1)} %get-tuple-element.21.home, bf16[16,8192]{1,0:T(8,128)(2,1)S(1)} %collective-permute-done.4.refs_0_, bf16[16,8192]{1,0:T(8,128)(2,1)S(1)} %collective-permute-done.5.refs_1_), custom_call_target="tpu_custom_call" | custom-call | flops 10000000000 | bytes 4194304 | tf_op jit(solution)/shard_map/attend_1/pallas_call | solution.py:259
  19.7 1.3 %collective-permute-start.6 = (bf16[16,8192]{1,0:T(8,128)(2,1)S(1)}, bf16[16,8192]{1,0:T(8,128)(2,1)S(1)}, u32[]{:S(2)}, u32[]{:S(2)}) collective-permute-start(bf16[16,8192]{1,0:T(8,128)(2,1)S(1)} %get-tuple-element.23), channel_id=1, source_target_pairs={{2,1},{0,3},{11,5},{9,7},{15,9},{13,11},{14,13},{12,15},{18,17},{1... | collective-permute-start | bytes 786440 | tf_op jit(solution)/shard_map/ppermute | solution.py:208
  21.0 1.3 %collective-permute-start.7 = (bf16[16,8192]{1,0:T(8,128)(2,1)S(1)}, bf16[16,8192]{1,0:T(8,128)(2,1)S(1)}, u32[]{:S(2)}, u32[]{:S(2)}) collective-permute-start(bf16[16,8192]{1,0:T(8,128)(2,1)S(1)} %get-tuple-element.24), channel_id=1, source_target_pairs={{0,1},{2,3},{9,5},{11,7},{13,9},{15,11},{12,13},{14,15},{16,17},{1... | collective-permute-start | bytes 786440 | tf_op jit(solution)/shard_map/ppermute | solution.py:208
  22.3 0.0 collective-permute-done.8.refs_0_
  22.3 0.0 collective-permute-done.9.refs_1_
  22.3 25.5 %collective-permute-done.6.refs_0_ = bf16[16,8192]{1,0:T(8,128)(2,1)S(1)} collective-permute-done((bf16[16,8192]{1,0:T(8,128)(2,1)S(1)}, bf16[16,8192]{1,0:T(8,128)(2,1)S(1)}, u32[]{:S(2)}, u32[]{:S(2)}) %collective-permute-start.6) | collective-permute-done | bytes 262176 | tf_op jit(solution)/shard_map/ppermute | solution.py:208
  47.8 0.0 collective-permute-done.7.refs_1_
  47.8 0.8 %join_1.1 = bf16[16,16384]{1,0:T(8,128)(2,1)} custom-call(bf16[16,8192]{1,0:T(8,128)(2,1)S(1)} %collective-permute-done.6.refs_0_, bf16[16,8192]{1,0:T(8,128)(2,1)S(1)} %collective-permute-done.7.refs_1_, bf16[16,16384]{1,0:T(8,128)(2,1)} %join_0.1.refs_2_), custom_call_target="tpu_custom_call", output_to_operand_aliasing={{}: (2, {})} | custom-call | tf_op jit(solution)/shard_map/join_1/pallas_call | solution.py:276
  (1 shorter events, 0.0 us)
Async XLA Ops:
  0.0 16.8 %collective-permute-start.3 = (bf16[2,512,512]{2,1,0:T(8,128)(2,1)}, bf16[2,512,512]{2,1,0:T(8,128)(2,1)S(1)}, u32[]{:S(2)}, u32[]{:S(2)}) collective-permute-start(bf16[2,512,512]{2,1,0:T(8,128)(2,1)} %own.1), channel_id=1, source_target_pairs={{8,0},{10,2},{9,13},{11,15},{12,9},{14,11},{24,16},{26,18},{25,29}... | collective-permute-start | bytes 3145736 | tf_op jit(solution)/shard_map/ppermute | solution.py:208
  0.7 16.1 %collective-permute-start.2 = (bf16[2,512,512]{2,1,0:T(8,128)(2,1)}, bf16[2,512,512]{2,1,0:T(8,128)(2,1)S(1)}, u32[]{:S(2)}, u32[]{:S(2)}) collective-permute-start(bf16[2,512,512]{2,1,0:T(8,128)(2,1)} %own.1), channel_id=1, source_target_pairs={{8,9},{10,11},{9,0},{11,2},{12,13},{14,15},{13,12},{15,14},{24,25}... | collective-permute-start | bytes 3145736 | tf_op jit(solution)/shard_map/ppermute | solution.py:208
  2.5 8.3 %collective-permute-start = (bf16[16,8192]{1,0:T(8,128)(2,1)S(1)}, bf16[16,8192]{1,0:T(8,128)(2,1)S(1)}, u32[]{:S(2)}, u32[]{:S(2)}) collective-permute-start(bf16[16,8192]{1,0:T(8,128)(2,1)S(1)} %get-tuple-element.17), channel_id=1, source_target_pairs={{0,2},{2,0},{4,11},{6,9},{8,15},{10,13},{12,14},{14,12},{16,18},{1... | collective-permute-start | bytes 786440 | tf_op jit(solution)/shard_map/ppermute | solution.py:208
  3.2 13.6 %collective-permute-start.1 = (bf16[16,8192]{1,0:T(8,128)(2,1)S(1)}, bf16[16,8192]{1,0:T(8,128)(2,1)S(1)}, u32[]{:S(2)}, u32[]{:S(2)}) collective-permute-start(bf16[16,8192]{1,0:T(8,128)(2,1)S(1)} %get-tuple-element.22), channel_id=1, source_target_pairs={{0,0},{2,2},{4,9},{6,11},{8,13},{10,15},{12,12},{14,14},{16,16},{1... | collective-permute-start | bytes 786440 | tf_op jit(solution)/shard_map/ppermute | solution.py:208
  3.9 15.0 %collective-permute-start.4 = (bf16[16,8192]{1,0:T(8,128)(2,1)S(1)}, bf16[16,8192]{1,0:T(8,128)(2,1)S(1)}, u32[]{:S(2)}, u32[]{:S(2)}) collective-permute-start(bf16[16,8192]{1,0:T(8,128)(2,1)S(1)} %get-tuple-element.17), channel_id=1, source_target_pairs={{1,2},{3,0},{5,11},{7,9},{9,15},{11,13},{13,14},{15,12},{17,18},{1... | collective-permute-start | bytes 786440 | tf_op jit(solution)/shard_map/ppermute | solution.py:208
  12.5 6.3 %collective-permute-start.5 = (bf16[16,8192]{1,0:T(8,128)(2,1)S(1)}, bf16[16,8192]{1,0:T(8,128)(2,1)S(1)}, u32[]{:S(2)}, u32[]{:S(2)}) collective-permute-start(bf16[16,8192]{1,0:T(8,128)(2,1)S(1)} %get-tuple-element.22), channel_id=1, source_target_pairs={{1,0},{3,2},{5,9},{7,11},{9,13},{11,15},{13,12},{15,14},{17,16},{1... | collective-permute-start | bytes 786440 | tf_op jit(solution)/shard_map/ppermute | solution.py:208
  17.5 4.8 %collective-permute-start.8 = (bf16[16,8192]{1,0:T(8,128)(2,1)S(1)}, bf16[16,8192]{1,0:T(8,128)(2,1)S(1)}, u32[]{:S(2)}, u32[]{:S(2)}) collective-permute-start(bf16[16,8192]{1,0:T(8,128)(2,1)S(1)} %get-tuple-element.25), channel_id=1, source_target_pairs={{2,0},{0,2},{11,4},{9,6},{15,8},{13,10},{14,12},{12,14},{18,16},{1... | collective-permute-start | bytes 786440 | tf_op jit(solution)/shard_map/ppermute | solution.py:208
  18.2 4.1 %collective-permute-start.9 = (bf16[16,8192]{1,0:T(8,128)(2,1)S(1)}, bf16[16,8192]{1,0:T(8,128)(2,1)S(1)}, u32[]{:S(2)}, u32[]{:S(2)}) collective-permute-start(bf16[16,8192]{1,0:T(8,128)(2,1)S(1)} %get-tuple-element.26), channel_id=1, source_target_pairs={{0,0},{2,2},{9,4},{11,6},{13,8},{15,10},{12,12},{14,14},{16,16},{1... | collective-permute-start | bytes 786440 | tf_op jit(solution)/shard_map/ppermute | solution.py:208
  19.7 28.1 %collective-permute-start.6 = (bf16[16,8192]{1,0:T(8,128)(2,1)S(1)}, bf16[16,8192]{1,0:T(8,128)(2,1)S(1)}, u32[]{:S(2)}, u32[]{:S(2)}) collective-permute-start(bf16[16,8192]{1,0:T(8,128)(2,1)S(1)} %get-tuple-element.23), channel_id=1, source_target_pairs={{2,1},{0,3},{11,5},{9,7},{15,9},{13,11},{14,13},{12,15},{18,17},{1... | collective-permute-start | bytes 786440 | tf_op jit(solution)/shard_map/ppermute | solution.py:208
  21.0 26.8 %collective-permute-start.7 = (bf16[16,8192]{1,0:T(8,128)(2,1)S(1)}, bf16[16,8192]{1,0:T(8,128)(2,1)S(1)}, u32[]{:S(2)}, u32[]{:S(2)}) collective-permute-start(bf16[16,8192]{1,0:T(8,128)(2,1)S(1)} %get-tuple-element.24), channel_id=1, source_target_pairs={{0,1},{2,3},{9,5},{11,7},{13,9},{15,11},{12,13},{14,15},{16,17},{1... | collective-permute-start | bytes 786440 | tf_op jit(solution)/shard_map/ppermute | solution.py:208

commit v7 on v4

--- a/solution.py
+++ b/solution.py
@@ -133,8 +133,9 @@
 
     def attend(pages):
         span_rows = pages * PAGE
-        row = lax.broadcasted_iota(jnp.int32, (rows, PAGE), 0)
-        column = lax.broadcasted_iota(jnp.int32, (rows, PAGE), 1)
+        row = lax.broadcasted_iota(jnp.int32, (rows, 1), 0)
+        masked_from = (PAGE - QR) // HD * HD
+        column = masked_from + lax.broadcasted_iota(jnp.int32, (rows, PAGE - masked_from), 1)
 
         def visible_of(group):
             token = lax.rem(row, tokens)
@@ -153,7 +154,8 @@
                 q_rows, of_pages(g, 0), (((1,), (1,)), ((), ())), preferred_element_type=jnp.float32
             )
             scores = [scores[:, p * PAGE:(p + 1) * PAGE] for p in range(pages)]
-            scores[-1] = jnp.where(visible_of(group), scores[-1], NEG)
+            tail = jnp.where(visible_of(group), scores[-1][:, masked_from:], NEG)
+            scores[-1] = jnp.concatenate([scores[-1][:, :masked_from], tail], axis=1)
             return scores
 
         units = [(group, g) for group in groups for g in range(local_kv)]

time: 48.3 us -> 48.3 us (level)
  the two profiles are of different devices: /device:TPU:5 before, /device:TPU:1 now
where the time goes in v7:
time: 48.3 us; the launch traced here: 48.1 us
  waiting for transfers between devices  24.8 us (51%)
  starting transfers between devices  17.9 us (37%)
  Pallas kernels  5.05 us (10%)
    ppermute x10, waiting for transfers between devices, moved(): lax.ppermute(array, ('ctx', 'head', 'sub'), [(flat(a), flat(b)) for a, b...  24.8 us
    ppermute x10, starting transfers between devices, moved(): lax.ppermute(array, ('ctx', 'head', 'sub'), [(flat(a), flat(b)) for a, b...  17.9 us
    pallas_call x1, Pallas kernels, one_request_each(): pl.pallas_call(functools.partial(gather_home_kernel, low_ctx), out_shape=...  1.7 us
    pallas_call x2, Pallas kernels, one_request_each(): pl.pallas_call(functools.partial(attend_kernel, low_ctx, sub_size, [keys]...  1.45 us
    pallas_call x1, Pallas kernels, one_request_each(): pl.pallas_call(split_kernel, out_shape=[q_piece] * head_count, in_specs=[...  1.06 us
  transfers between devices with their start and end apart: 10, of which 1 were waited for; matrix products, arithmetic and copies ran while one was open for 0% of the time, Pallas kernels for 9%

profile of v7, /device:TPU:1, one launch (start us, length us, event | category | flops | bytes accessed | tf_op | source)
XLA Modules:
  0.0 48.1 jit_solution(13608380567668038585)
XLA Ops:
  0.0 0.7 %collective-permute-start.3 = (bf16[2,512,512]{2,1,0:T(8,128)(2,1)}, bf16[2,512,512]{2,1,0:T(8,128)(2,1)S(1)}, u32[]{:S(2)}, u32[]{:S(2)}) collective-permute-start(bf16[2,512,512]{2,1,0:T(8,128)(2,1)} %own.1), channel_id=1, source_target_pairs={{8,9},{10,11},{9,0},{11,2},{12,13},{14,15},{13,12},{15,14},{24,25}... | collective-permute-start | bytes 3145736 | tf_op jit(solution)/shard_map/ppermute | solution.py:210
  0.7 0.7 %collective-permute-start.2 = (bf16[2,512,512]{2,1,0:T(8,128)(2,1)}, bf16[2,512,512]{2,1,0:T(8,128)(2,1)S(1)}, u32[]{:S(2)}, u32[]{:S(2)}) collective-permute-start(bf16[2,512,512]{2,1,0:T(8,128)(2,1)} %own.1), channel_id=1, source_target_pairs={{8,0},{10,2},{9,13},{11,15},{12,9},{14,11},{24,16},{26,18},{25,29}... | collective-permute-start | bytes 3145736 | tf_op jit(solution)/shard_map/ppermute | solution.py:210
  1.5 1.1 %split.1 = (bf16[16,8192]{1,0:T(8,128)(2,1)S(1)}, bf16[16,8192]{1,0:T(8,128)(2,1)S(1)}) custom-call(bf16[16,16384]{1,0:T(8,128)(2,1)} %queries.1), custom_call_target="tpu_custom_call" | custom-call | tf_op jit(solution)/shard_map/split/pallas_call | solution.py:217
  2.5 0.7 %collective-permute-start = (bf16[16,8192]{1,0:T(8,128)(2,1)S(1)}, bf16[16,8192]{1,0:T(8,128)(2,1)S(1)}, u32[]{:S(2)}, u32[]{:S(2)}) collective-permute-start(bf16[16,8192]{1,0:T(8,128)(2,1)S(1)} %get-tuple-element.17), channel_id=1, source_target_pairs={{0,2},{2,0},{4,11},{6,9},{8,15},{10,13},{12,14},{14,12},{16,18},{1... | collective-permute-start | bytes 786440 | tf_op jit(solution)/shard_map/ppermute | solution.py:210
  3.2 0.7 %collective-permute-start.1 = (bf16[16,8192]{1,0:T(8,128)(2,1)S(1)}, bf16[16,8192]{1,0:T(8,128)(2,1)S(1)}, u32[]{:S(2)}, u32[]{:S(2)}) collective-permute-start(bf16[16,8192]{1,0:T(8,128)(2,1)S(1)} %get-tuple-element.22), channel_id=1, source_target_pairs={{0,0},{2,2},{4,9},{6,11},{8,13},{10,15},{12,12},{14,14},{16,16},{1... | collective-permute-start | bytes 786440 | tf_op jit(solution)/shard_map/ppermute | solution.py:210
  3.9 6.9 %collective-permute-start.4 = (bf16[16,8192]{1,0:T(8,128)(2,1)S(1)}, bf16[16,8192]{1,0:T(8,128)(2,1)S(1)}, u32[]{:S(2)}, u32[]{:S(2)}) collective-permute-start(bf16[16,8192]{1,0:T(8,128)(2,1)S(1)} %get-tuple-element.17), channel_id=1, source_target_pairs={{1,2},{3,0},{5,11},{7,9},{9,15},{11,13},{13,14},{15,12},{17,18},{1... | collective-permute-start | bytes 786440 | tf_op jit(solution)/shard_map/ppermute | solution.py:210
  10.8 0.0 collective-permute-done.after.refs_0_
  10.8 1.7 %gather_home.1 = (bf16[4,2,4,256,128]{4,3,2,1,0:T(8,128)(2,1)S(1)}, s32[4]{0:T(128)S(1)}) custom-call(s32[4]{0:T(128)} %counts_in.1, s32[4]{0:T(128)} %counts_in.1, bf16[2,512,512]{2,1,0:T(8,128)(2,1)} %own.1, bf16[16,8192]{1,0:T(8,128)(2,1)S(1)} %collective-permute-done.after.refs_0_), custom_call_target="tpu_custom_call" | custom-call | tf_op jit(solution)/shard_map/gather_home/pallas_call | solution.py:232
  12.5 4.2 %collective-permute-start.5 = (bf16[16,8192]{1,0:T(8,128)(2,1)S(1)}, bf16[16,8192]{1,0:T(8,128)(2,1)S(1)}, u32[]{:S(2)}, u32[]{:S(2)}) collective-permute-start(bf16[16,8192]{1,0:T(8,128)(2,1)S(1)} %get-tuple-element.22), channel_id=1, source_target_pairs={{1,0},{3,2},{5,9},{7,11},{9,13},{11,15},{13,12},{15,14},{17,16},{1... | collective-permute-start | bytes 786440 | tf_op jit(solution)/shard_map/ppermute | solution.py:210
  16.8 0.0 collective-permute-done.1.refs_1_
  16.8 0.0 collective-permute-done.3.refs_3_
  16.8 0.0 collective-permute-done.2.refs_2_
  16.8 0.7 %attend_0.1 = (bf16[16,8192]{1,0:T(8,128)(2,1)S(1)}, bf16[16,8192]{1,0:T(8,128)(2,1)S(1)}, bf16[4,2,4,256,128]{4,3,2,1,0:T(8,128)(2,1)S(1)}) custom-call(s32[4]{0:T(128)S(1)} %get-tuple-element.19.counts, bf16[4,2,4,256,128]{4,3,2,1,0:T(8,128)(2,1)S(1)} %get-tuple-element.20.home, bf16[16,8192]{1,0:T(8,128)(2,1)S(1)} %collective-permute-done.after.refs_0_, ...), custom_call_target="tpu_custom_call" | custom-call | flops 10000000000 | bytes 4194304 | tf_op jit(solution)/shard_map/attend_0/pallas_call | solution.py:261
  17.5 0.7 %collective-permute-start.8 = (bf16[16,8192]{1,0:T(8,128)(2,1)S(1)}, bf16[16,8192]{1,0:T(8,128)(2,1)S(1)}, u32[]{:S(2)}, u32[]{:S(2)}) collective-permute-start(bf16[16,8192]{1,0:T(8,128)(2,1)S(1)} %get-tuple-element.25), channel_id=1, source_target_pairs={{2,0},{0,2},{11,4},{9,6},{15,8},{13,10},{14,12},{12,14},{18,16},{1... | collective-permute-start | bytes 786440 | tf_op jit(solution)/shard_map/ppermute | solution.py:210
  18.2 0.7 %collective-permute-start.9 = (bf16[16,8192]{1,0:T(8,128)(2,1)S(1)}, bf16[16,8192]{1,0:T(8,128)(2,1)S(1)}, u32[]{:S(2)}, u32[]{:S(2)}) collective-permute-start(bf16[16,8192]{1,0:T(8,128)(2,1)S(1)} %get-tuple-element.26), channel_id=1, source_target_pairs={{0,0},{2,2},{9,4},{11,6},{13,8},{15,10},{12,12},{14,14},{16,16},{1... | collective-permute-start | bytes 786440 | tf_op jit(solution)/shard_map/ppermute | solution.py:210
  18.8 0.0 collective-permute-done.4.refs_0_
  18.9 0.0 collective-permute-done.5.refs_1_
  18.9 0.8 %attend_1.1 = (bf16[16,8192]{1,0:T(8,128)(2,1)S(1)}, bf16[16,8192]{1,0:T(8,128)(2,1)S(1)}) custom-call(s32[4]{0:T(128)S(1)} %get-tuple-element.19.counts, bf16[4,2,4,256,128]{4,3,2,1,0:T(8,128)(2,1)S(1)} %get-tuple-element.21.home, bf16[16,8192]{1,0:T(8,128)(2,1)S(1)} %collective-permute-done.4.refs_0_, bf16[16,8192]{1,0:T(8,128)(2,1)S(1)} %collective-permute-done.5.refs_1_), custom_call_target="tpu_custom_call" | custom-call | flops 10000000000 | bytes 4194304 | tf_op jit(solution)/shard_map/attend_1/pallas_call | solution.py:261
  19.7 1.3 %collective-permute-start.6 = (bf16[16,8192]{1,0:T(8,128)(2,1)S(1)}, bf16[16,8192]{1,0:T(8,128)(2,1)S(1)}, u32[]{:S(2)}, u32[]{:S(2)}) collective-permute-start(bf16[16,8192]{1,0:T(8,128)(2,1)S(1)} %get-tuple-element.23), channel_id=1, source_target_pairs={{2,1},{0,3},{11,5},{9,7},{15,9},{13,11},{14,13},{12,15},{18,17},{1... | collective-permute-start | bytes 786440 | tf_op jit(solution)/shard_map/ppermute | solution.py:210
  21.0 1.3 %collective-permute-start.7 = (bf16[16,8192]{1,0:T(8,128)(2,1)S(1)}, bf16[16,8192]{1,0:T(8,128)(2,1)S(1)}, u32[]{:S(2)}, u32[]{:S(2)}) collective-permute-start(bf16[16,8192]{1,0:T(8,128)(2,1)S(1)} %get-tuple-element.24), channel_id=1, source_target_pairs={{0,1},{2,3},{9,5},{11,7},{13,9},{15,11},{12,13},{14,15},{16,17},{1... | collective-permute-start | bytes 786440 | tf_op jit(solution)/shard_map/ppermute | solution.py:210
  22.3 0.0 collective-permute-done.8.refs_0_
  22.3 0.0 collective-permute-done.9.refs_1_
  22.3 24.8 %collective-permute-done.6.refs_0_ = bf16[16,8192]{1,0:T(8,128)(2,1)S(1)} collective-permute-done((bf16[16,8192]{1,0:T(8,128)(2,1)S(1)}, bf16[16,8192]{1,0:T(8,128)(2,1)S(1)}, u32[]{:S(2)}, u32[]{:S(2)}) %collective-permute-start.6) | collective-permute-done | bytes 262176 | tf_op jit(solution)/shard_map/ppermute | solution.py:210
  47.1 0.0 collective-permute-done.7.refs_1_
  47.1 0.8 %join_1.1 = bf16[16,16384]{1,0:T(8,128)(2,1)} custom-call(bf16[16,8192]{1,0:T(8,128)(2,1)S(1)} %collective-permute-done.6.refs_0_, bf16[16,8192]{1,0:T(8,128)(2,1)S(1)} %collective-permute-done.7.refs_1_, bf16[16,16384]{1,0:T(8,128)(2,1)} %join_0.1.refs_2_), custom_call_target="tpu_custom_call", output_to_operand_aliasing={{}: (2, {})} | custom-call | tf_op jit(solution)/shard_map/join_1/pallas_call | solution.py:278
  (1 shorter events, 0.0 us)
Async XLA Ops:
  0.0 16.8 %collective-permute-start.3 = (bf16[2,512,512]{2,1,0:T(8,128)(2,1)}, bf16[2,512,512]{2,1,0:T(8,128)(2,1)S(1)}, u32[]{:S(2)}, u32[]{:S(2)}) collective-permute-start(bf16[2,512,512]{2,1,0:T(8,128)(2,1)} %own.1), channel_id=1, source_target_pairs={{8,9},{10,11},{9,0},{11,2},{12,13},{14,15},{13,12},{15,14},{24,25}... | collective-permute-start | bytes 3145736 | tf_op jit(solution)/shard_map/ppermute | solution.py:210
  0.7 16.1 %collective-permute-start.2 = (bf16[2,512,512]{2,1,0:T(8,128)(2,1)}, bf16[2,512,512]{2,1,0:T(8,128)(2,1)S(1)}, u32[]{:S(2)}, u32[]{:S(2)}) collective-permute-start(bf16[2,512,512]{2,1,0:T(8,128)(2,1)} %own.1), channel_id=1, source_target_pairs={{8,0},{10,2},{9,13},{11,15},{12,9},{14,11},{24,16},{26,18},{25,29}... | collective-permute-start | bytes 3145736 | tf_op jit(solution)/shard_map/ppermute | solution.py:210
  2.5 8.3 %collective-permute-start = (bf16[16,8192]{1,0:T(8,128)(2,1)S(1)}, bf16[16,8192]{1,0:T(8,128)(2,1)S(1)}, u32[]{:S(2)}, u32[]{:S(2)}) collective-permute-start(bf16[16,8192]{1,0:T(8,128)(2,1)S(1)} %get-tuple-element.17), channel_id=1, source_target_pairs={{0,2},{2,0},{4,11},{6,9},{8,15},{10,13},{12,14},{14,12},{16,18},{1... | collective-permute-start | bytes 786440 | tf_op jit(solution)/shard_map/ppermute | solution.py:210
  3.2 13.6 %collective-permute-start.1 = (bf16[16,8192]{1,0:T(8,128)(2,1)S(1)}, bf16[16,8192]{1,0:T(8,128)(2,1)S(1)}, u32[]{:S(2)}, u32[]{:S(2)}) collective-permute-start(bf16[16,8192]{1,0:T(8,128)(2,1)S(1)} %get-tuple-element.22), channel_id=1, source_target_pairs={{0,0},{2,2},{4,9},{6,11},{8,13},{10,15},{12,12},{14,14},{16,16},{1... | collective-permute-start | bytes 786440 | tf_op jit(solution)/shard_map/ppermute | solution.py:210
  3.9 15.0 %collective-permute-start.4 = (bf16[16,8192]{1,0:T(8,128)(2,1)S(1)}, bf16[16,8192]{1,0:T(8,128)(2,1)S(1)}, u32[]{:S(2)}, u32[]{:S(2)}) collective-permute-start(bf16[16,8192]{1,0:T(8,128)(2,1)S(1)} %get-tuple-element.17), channel_id=1, source_target_pairs={{1,2},{3,0},{5,11},{7,9},{9,15},{11,13},{13,14},{15,12},{17,18},{1... | collective-permute-start | bytes 786440 | tf_op jit(solution)/shard_map/ppermute | solution.py:210
  12.5 6.3 %collective-permute-start.5 = (bf16[16,8192]{1,0:T(8,128)(2,1)S(1)}, bf16[16,8192]{1,0:T(8,128)(2,1)S(1)}, u32[]{:S(2)}, u32[]{:S(2)}) collective-permute-start(bf16[16,8192]{1,0:T(8,128)(2,1)S(1)} %get-tuple-element.22), channel_id=1, source_target_pairs={{1,0},{3,2},{5,9},{7,11},{9,13},{11,15},{13,12},{15,14},{17,16},{1... | collective-permute-start | bytes 786440 | tf_op jit(solution)/shard_map/ppermute | solution.py:210
  17.5 4.8 %collective-permute-start.8 = (bf16[16,8192]{1,0:T(8,128)(2,1)S(1)}, bf16[16,8192]{1,0:T(8,128)(2,1)S(1)}, u32[]{:S(2)}, u32[]{:S(2)}) collective-permute-start(bf16[16,8192]{1,0:T(8,128)(2,1)S(1)} %get-tuple-element.25), channel_id=1, source_target_pairs={{2,0},{0,2},{11,4},{9,6},{15,8},{13,10},{14,12},{12,14},{18,16},{1... | collective-permute-start | bytes 786440 | tf_op jit(solution)/shard_map/ppermute | solution.py:210
  18.2 4.1 %collective-permute-start.9 = (bf16[16,8192]{1,0:T(8,128)(2,1)S(1)}, bf16[16,8192]{1,0:T(8,128)(2,1)S(1)}, u32[]{:S(2)}, u32[]{:S(2)}) collective-permute-start(bf16[16,8192]{1,0:T(8,128)(2,1)S(1)} %get-tuple-element.26), channel_id=1, source_target_pairs={{0,0},{2,2},{9,4},{11,6},{13,8},{15,10},{12,12},{14,14},{16,16},{1... | collective-permute-start | bytes 786440 | tf_op jit(solution)/shard_map/ppermute | solution.py:210
  19.7 27.5 %collective-permute-start.6 = (bf16[16,8192]{1,0:T(8,128)(2,1)S(1)}, bf16[16,8192]{1,0:T(8,128)(2,1)S(1)}, u32[]{:S(2)}, u32[]{:S(2)}) collective-permute-start(bf16[16,8192]{1,0:T(8,128)(2,1)S(1)} %get-tuple-element.23), channel_id=1, source_target_pairs={{2,1},{0,3},{11,5},{9,7},{15,9},{13,11},{14,13},{12,15},{18,17},{1... | collective-permute-start | bytes 786440 | tf_op jit(solution)/shard_map/ppermute | solution.py:210
  21.0 26.2 %collective-permute-start.7 = (bf16[16,8192]{1,0:T(8,128)(2,1)S(1)}, bf16[16,8192]{1,0:T(8,128)(2,1)S(1)}, u32[]{:S(2)}, u32[]{:S(2)}) collective-permute-start(bf16[16,8192]{1,0:T(8,128)(2,1)S(1)} %get-tuple-element.24), channel_id=1, source_target_pairs={{0,1},{2,3},{9,5},{11,7},{13,9},{15,11},{12,13},{14,15},{16,17},{1... | collective-permute-start | bytes 786440 | tf_op jit(solution)/shard_map/ppermute | solution.py:210

commit v8 on v7

--- a/solution.py
+++ b/solution.py
@@ -101,31 +101,37 @@
     counts_copy.wait()
 
 
-def gather_rest(low_ctx, counts, home, far, near, out):
-    local_kv, _, most_pages = out.shape[:3]
+def gather_rest(low_ctx, counts, home, far, near, keys_out, values_out):
+    local_kv, most_pages = values_out.shape[:2]
+
+    def put(g, p, keys, values):
+        keys_out[g, :, p * PAGE:(p + 1) * PAGE] = keys.T
+        values_out[g, p] = values
+
     for p, here, which, rows in pages_of(low_ctx, counts, most_pages):
         @pl.when(here & (which == 0))
         def _():
             for g in range(local_kv):
-                out[g, :, p] = home[g, :, p]
+                put(g, p, home[g, 0, p], home[g, 1, p])
         for n, ref in enumerate((near, far)):
             @pl.when(here & (which == n + 1))
             def _():
                 for g in range(local_kv):
-                    for i in range(2):
-                        out[g, i, p] = ref[i, rows, g * HD:(g + 1) * HD]
-
-
-def attend_kernel(low_ctx, sub_count, groups, others, counts, home, *refs):
+                    part = slice(g * HD, (g + 1) * HD)
+                    put(g, p, ref[0, rows, part], ref[1, rows, part])
+
+
+def attend_kernel(low_ctx, sub_count, groups, others, counts, *refs):
     keys = [key for group in groups for key in group]
-    queries, outs = dict(zip(keys, refs)), dict(zip(keys, refs[len(keys) + others:]))
-    pages_in = home
+    before = 1 if others else 2
+    after = before + len(keys) + others
+    queries, outs = dict(zip(keys, refs[before:])), dict(zip(keys, refs[after:]))
+    keys_in, values_in = refs[-2:] if others else refs[:2]
     if others:
-        pages_in = refs[-1]
-        gather_rest(low_ctx, counts, home, *refs[len(keys):len(keys) + others], pages_in)
+        gather_rest(low_ctx, counts, refs[0], *refs[after - others:after], keys_in, values_in)
     head = lax.axis_index("head")
-    tokens, width = refs[0].shape
-    local_kv, _, most_pages = pages_in.shape[:3]
+    tokens, width = queries[keys[0]].shape
+    local_kv, most_pages = values_in.shape[:2]
     span = width // local_kv
     per_group = span // HD
     piece_rows = per_group * tokens
@@ -144,15 +150,10 @@
                 token = jnp.where(row // piece_rows == i, token + first_token, token)
             return column <= PAGE - QR + token
 
-        def of_pages(g, i):
-            return pages_in[g, i, 0:pages].reshape(span_rows, HD)
-
         def scores_of(group, g):
             q_blocks = [queries[key][:, g * span:(g + 1) * span] for key in group]
             q_rows = jnp.concatenate([q[:, j * HD:(j + 1) * HD] for q in q_blocks for j in range(per_group)], axis=0)
-            scores = lax.dot_general(
-                q_rows, of_pages(g, 0), (((1,), (1,)), ((), ())), preferred_element_type=jnp.float32
-            )
+            scores = jnp.dot(q_rows, keys_in[g, :, 0:span_rows], preferred_element_type=jnp.float32)
             scores = [scores[:, p * PAGE:(p + 1) * PAGE] for p in range(pages)]
             tail = jnp.where(visible_of(group), scores[-1][:, masked_from:], NEG)
             scores[-1] = jnp.concatenate([scores[-1][:, :masked_from], tail], axis=1)
@@ -166,7 +167,7 @@
             numerators = [jnp.exp2((s - top) * EXP2_SCALE) for s in scores]
             totals = jnp.sum(functools.reduce(jnp.add, numerators), axis=1, keepdims=True)
             weights = jnp.concatenate([s.astype(jnp.bfloat16) for s in numerators], axis=1)
-            product = jnp.dot(weights, of_pages(g, 1), preferred_element_type=jnp.float32)
+            product = jnp.dot(weights, values_in[g, 0:pages].reshape(span_rows, HD), preferred_element_type=jnp.float32)
             done = (product / totals).astype(jnp.bfloat16)
             for i, key in enumerate(group):
                 start = i * piece_rows
@@ -256,21 +257,25 @@
     )
     groups = [[(step, s) for step in heads[::-1]] for s in range(sub_size)]
     back = {}
-    pages, others = home, [vmem(far), vmem(near)]
+    pages, others = [vmem(home)], [vmem(far), vmem(near)]
+    gathered = [
+        pltpu.VMEM((local_kv, HD, most_pages * PAGE), kv_cache.dtype),
+        pltpu.VMEM((local_kv, most_pages, PAGE, HD), kv_cache.dtype),
+    ]
     for keys in groups:
         outs = pl.pallas_call(
             functools.partial(attend_kernel, low_ctx, sub_size, [keys], len(others)),
-            out_shape=[q_piece] * len(keys) + [pltpu.VMEM(home.shape, home.dtype)] * bool(others),
-            in_specs=[pl.BlockSpec(memory_space=pltpu.SMEM)] + [in_vmem] * (1 + len(keys) + len(others)),
-            out_specs=[in_vmem] * (len(keys) + bool(others)),
+            out_shape=[q_piece] * len(keys) + gathered * bool(others),
+            in_specs=[pl.BlockSpec(memory_space=pltpu.SMEM)] + [in_vmem] * (len(pages) + len(keys) + len(others)),
+            out_specs=[in_vmem] * (len(keys) + len(gathered) * bool(others)),
             compiler_params=pltpu.CompilerParams(vmem_limit_bytes=12 * 2**20),
             cost_estimate=pl.CostEstimate(flops=10**10, bytes_accessed=2**22, transcendentals=10**6),
             name=f"attend_{keys[0][1]}",
-        )(vmem(counts), vmem(pages), *[vmem(q_in[key]) for key in keys], *others)
+        )(vmem(counts), *pages, *[vmem(q_in[key]) for key in keys], *others)
         for key, out in zip(keys, outs):
             back[key] = moved(out, [(b, a) for a, b in routes[key]])
         if others:
-            pages, others = outs[-1], []
+            pages, others = [vmem(out) for out in outs[len(keys):]], []
 
     joined = []
     for keys in groups:

time: 48.3 us -> 46.9 us (0.971)
  the two profiles are of different devices: /device:TPU:1 before, /device:TPU:17 now
where the time goes in v8:
time: 46.9 us; the launch traced here: 46.5 us
  starting transfers between devices  20.3 us (43%)
  waiting for transfers between devices  13.6 us (29%)
  Pallas kernels  12.3 us (26%)
    ppermute x10, starting transfers between devices, moved(): lax.ppermute(array, ('ctx', 'head', 'sub'), [(flat(a), flat(b)) for a, b...  20.3 us
    ppermute x10, waiting for transfers between devices, moved(): lax.ppermute(array, ('ctx', 'head', 'sub'), [(flat(a), flat(b)) for a, b...  13.6 us
    pallas_call x2, Pallas kernels, one_request_each(): pl.pallas_call(functools.partial(attend_kernel, low_ctx, sub_size, [keys]...  8.15 us
    pallas_call x1, Pallas kernels, one_request_each(): pl.pallas_call(functools.partial(gather_home_kernel, low_ctx), out_shape=...  2.25 us
    pallas_call x1, Pallas kernels, one_request_each(): pl.pallas_call(split_kernel, out_shape=[q_piece] * head_count, in_specs=[...  1.06 us
  transfers between devices with their start and end apart: 10, of which 5 were waited for; matrix products, arithmetic and copies ran while one was open for 0% of the time, Pallas kernels for 25%

profile of v8, /device:TPU:17, one launch (start us, length us, event | category | flops | bytes accessed | tf_op | source)
XLA Modules:
  0.0 46.5 jit_solution(3642230069006365937)
XLA Ops:
  0.0 1.9 %collective-permute-start.3 = (bf16[2,512,512]{2,1,0:T(8,128)(2,1)}, bf16[2,512,512]{2,1,0:T(8,128)(2,1)S(1)}, u32[]{:S(2)}, u32[]{:S(2)}) collective-permute-start(bf16[2,512,512]{2,1,0:T(8,128)(2,1)} %own.1), channel_id=1, source_target_pairs={{8,9},{10,11},{9,0},{11,2},{12,13},{14,15},{13,12},{15,14},{24,25}... | collective-permute-start | bytes 3145736 | tf_op jit(solution)/shard_map/ppermute | solution.py:211
  1.9 3.9 %collective-permute-start.2 = (bf16[2,512,512]{2,1,0:T(8,128)(2,1)}, bf16[2,512,512]{2,1,0:T(8,128)(2,1)S(1)}, u32[]{:S(2)}, u32[]{:S(2)}) collective-permute-start(bf16[2,512,512]{2,1,0:T(8,128)(2,1)} %own.1), channel_id=1, source_target_pairs={{8,0},{10,2},{9,13},{11,15},{12,9},{14,11},{24,16},{26,18},{25,29}... | collective-permute-start | bytes 3145736 | tf_op jit(solution)/shard_map/ppermute | solution.py:211
  5.8 1.1 %split.1 = (bf16[16,8192]{1,0:T(8,128)(2,1)S(1)}, bf16[16,8192]{1,0:T(8,128)(2,1)S(1)}) custom-call(bf16[16,16384]{1,0:T(8,128)(2,1)} %queries.1), custom_call_target="tpu_custom_call" | custom-call | tf_op jit(solution)/shard_map/split/pallas_call | solution.py:218
  6.9 1.3 %collective-permute-start = (bf16[16,8192]{1,0:T(8,128)(2,1)S(1)}, bf16[16,8192]{1,0:T(8,128)(2,1)S(1)}, u32[]{:S(2)}, u32[]{:S(2)}) collective-permute-start(bf16[16,8192]{1,0:T(8,128)(2,1)S(1)} %get-tuple-element.18), channel_id=1, source_target_pairs={{0,2},{2,0},{4,11},{6,9},{8,15},{10,13},{12,14},{14,12},{16,18},{1... | collective-permute-start | bytes 786440 | tf_op jit(solution)/shard_map/ppermute | solution.py:211
  8.2 1.3 %collective-permute-start.1 = (bf16[16,8192]{1,0:T(8,128)(2,1)S(1)}, bf16[16,8192]{1,0:T(8,128)(2,1)S(1)}, u32[]{:S(2)}, u32[]{:S(2)}) collective-permute-start(bf16[16,8192]{1,0:T(8,128)(2,1)S(1)} %get-tuple-element.24), channel_id=1, source_target_pairs={{0,0},{2,2},{4,9},{6,11},{8,13},{10,15},{12,12},{14,14},{16,16},{1... | collective-permute-start | bytes 786440 | tf_op jit(solution)/shard_map/ppermute | solution.py:211
  9.5 2.2 %collective-permute-start.4 = (bf16[16,8192]{1,0:T(8,128)(2,1)S(1)}, bf16[16,8192]{1,0:T(8,128)(2,1)S(1)}, u32[]{:S(2)}, u32[]{:S(2)}) collective-permute-start(bf16[16,8192]{1,0:T(8,128)(2,1)S(1)} %get-tuple-element.18), channel_id=1, source_target_pairs={{1,2},{3,0},{5,11},{7,9},{9,15},{11,13},{13,14},{15,12},{17,18},{1... | collective-permute-start | bytes 786440 | tf_op jit(solution)/shard_map/ppermute | solution.py:211
  11.7 4.5 %collective-permute-done.after.refs_1_ = bf16[16,8192]{1,0:T(8,128)(2,1)S(1)} collective-permute-done((bf16[16,8192]{1,0:T(8,128)(2,1)S(1)}, bf16[16,8192]{1,0:T(8,128)(2,1)S(1)}, u32[]{:S(2)}, u32[]{:S(2)}) %collective-permute-start) | collective-permute-done | bytes 262176 | tf_op jit(solution)/shard_map/ppermute | solution.py:211
  16.2 2.3 %gather_home.1 = (bf16[4,2,4,256,128]{4,3,2,1,0:T(8,128)(2,1)S(1)}, s32[4]{0:T(128)S(1)}) custom-call(s32[4]{0:T(128)} %counts_in.1, s32[4]{0:T(128)} %counts_in.1, bf16[2,512,512]{2,1,0:T(8,128)(2,1)} %own.1, bf16[16,8192]{1,0:T(8,128)(2,1)S(1)} %collective-permute-done.after.refs_1_), custom_call_target="tpu_custom_call" | custom-call | tf_op jit(solution)/shard_map/gather_home/pallas_call | solution.py:233
  18.4 3.3 %collective-permute-start.5 = (bf16[16,8192]{1,0:T(8,128)(2,1)S(1)}, bf16[16,8192]{1,0:T(8,128)(2,1)S(1)}, u32[]{:S(2)}, u32[]{:S(2)}) collective-permute-start(bf16[16,8192]{1,0:T(8,128)(2,1)S(1)} %get-tuple-element.24), channel_id=1, source_target_pairs={{1,0},{3,2},{5,9},{7,11},{9,13},{11,15},{13,12},{15,14},{17,16},{1... | collective-permute-start | bytes 786440 | tf_op jit(solution)/shard_map/ppermute | solution.py:211
  21.7 0.0 collective-permute-done.1.refs_2_
  21.7 1.4 %collective-permute-done.3.refs_4_ = bf16[2,512,512]{2,1,0:T(8,128)(2,1)S(1)} collective-permute-done((bf16[2,512,512]{2,1,0:T(8,128)(2,1)}, bf16[2,512,512]{2,1,0:T(8,128)(2,1)S(1)}, u32[]{:S(2)}, u32[]{:S(2)}) %collective-permute-start.3) | collective-permute-done | bytes 1048608 | tf_op jit(solution)/shard_map/ppermute | solution.py:211
  23.1 0.4 collective-permute-done.2.refs_3_
  23.5 4.1 %attend_0.1 = (bf16[16,8192]{1,0:T(8,128)(2,1)S(1)}, bf16[16,8192]{1,0:T(8,128)(2,1)S(1)}, bf16[4,128,1024]{2,1,0:T(8,128)(2,1)S(1)}, bf16[4,4,256,128]{3,2,1,0:T(8,128)(2,1)S(1)}) custom-call(s32[4]{0:T(128)S(1)} %get-tuple-element.20.counts, bf16[4,2,4,256,128]{4,3,2,1,0:T(8,128)(2,1)S(1)} %get-tuple-element.21.refs_0_, ...), custom_call_target="tpu_custom_call" | custom-call | flops 10000000000 | bytes 4194304 | tf_op jit(solution)/shard_map/attend_0/pallas_call | solution.py:266
  27.6 1.3 %collective-permute-start.8 = (bf16[16,8192]{1,0:T(8,128)(2,1)S(1)}, bf16[16,8192]{1,0:T(8,128)(2,1)S(1)}, u32[]{:S(2)}, u32[]{:S(2)}) collective-permute-start(bf16[16,8192]{1,0:T(8,128)(2,1)S(1)} %get-tuple-element.27), channel_id=1, source_target_pairs={{2,0},{0,2},{11,4},{9,6},{15,8},{13,10},{14,12},{12,14},{18,16},{1... | collective-permute-start | bytes 786440 | tf_op jit(solution)/shard_map/ppermute | solution.py:211
  28.9 1.3 %collective-permute-start.9 = (bf16[16,8192]{1,0:T(8,128)(2,1)S(1)}, bf16[16,8192]{1,0:T(8,128)(2,1)S(1)}, u32[]{:S(2)}, u32[]{:S(2)}) collective-permute-start(bf16[16,8192]{1,0:T(8,128)(2,1)S(1)} %get-tuple-element.28), channel_id=1, source_target_pairs={{0,0},{2,2},{9,4},{11,6},{13,8},{15,10},{12,12},{14,14},{16,16},{1... | collective-permute-start | bytes 786440 | tf_op jit(solution)/shard_map/ppermute | solution.py:211
  30.2 0.0 collective-permute-done.4.refs_2_
  30.2 0.0 collective-permute-done.5.refs_3_
  30.3 4.0 %attend_1.1 = (bf16[16,8192]{1,0:T(8,128)(2,1)S(1)}, bf16[16,8192]{1,0:T(8,128)(2,1)S(1)}) custom-call(s32[4]{0:T(128)S(1)} %get-tuple-element.20.counts, bf16[4,128,1024]{2,1,0:T(8,128)(2,1)S(1)} %get-tuple-element.22.refs_0_, bf16[4,4,256,128]{3,2,1,0:T(8,128)(2,1)S(1)} %get-tuple-element.23.refs_1_, bf16[16,8192]{1,0:T(8,128)(2,1)S(1)} %collective-permute-done.4.refs_2_, ...), custom_call_target="tpu_custom_call" | custom-call | flops 10000000000 | bytes 4194304 | tf_op jit(solution)/shard_map/attend_1/pallas_call | solution.py:266
  34.3 1.9 %collective-permute-start.6 = (bf16[16,8192]{1,0:T(8,128)(2,1)S(1)}, bf16[16,8192]{1,0:T(8,128)(2,1)S(1)}, u32[]{:S(2)}, u32[]{:S(2)}) collective-permute-start(bf16[16,8192]{1,0:T(8,128)(2,1)S(1)} %get-tuple-element.25), channel_id=1, source_target_pairs={{2,1},{0,3},{11,5},{9,7},{15,9},{13,11},{14,13},{12,15},{18,17},{1... | collective-permute-start | bytes 786440 | tf_op jit(solution)/shard_map/ppermute | solution.py:211
  36.2 1.9 %collective-permute-start.7 = (bf16[16,8192]{1,0:T(8,128)(2,1)S(1)}, bf16[16,8192]{1,0:T(8,128)(2,1)S(1)}, u32[]{:S(2)}, u32[]{:S(2)}) collective-permute-start(bf16[16,8192]{1,0:T(8,128)(2,1)S(1)} %get-tuple-element.26), channel_id=1, source_target_pairs={{0,1},{2,3},{9,5},{11,7},{13,9},{15,11},{12,13},{14,15},{16,17},{1... | collective-permute-start | bytes 786440 | tf_op jit(solution)/shard_map/ppermute | solution.py:211
  38.1 0.0 collective-permute-done.8.refs_0_
  38.1 0.0 collective-permute-done.9.refs_1_
  38.2 4.1 %collective-permute-done.6.refs_0_ = bf16[16,8192]{1,0:T(8,128)(2,1)S(1)} collective-permute-done((bf16[16,8192]{1,0:T(8,128)(2,1)S(1)}, bf16[16,8192]{1,0:T(8,128)(2,1)S(1)}, u32[]{:S(2)}, u32[]{:S(2)}) %collective-permute-start.6) | collective-permute-done | bytes 262176 | tf_op jit(solution)/shard_map/ppermute | solution.py:211
  42.3 3.2 %collective-permute-done.7.refs_1_ = bf16[16,8192]{1,0:T(8,128)(2,1)S(1)} collective-permute-done((bf16[16,8192]{1,0:T(8,128)(2,1)S(1)}, bf16[16,8192]{1,0:T(8,128)(2,1)S(1)}, u32[]{:S(2)}, u32[]{:S(2)}) %collective-permute-start.7) | collective-permute-done | bytes 262176 | tf_op jit(solution)/shard_map/ppermute | solution.py:211
  45.5 0.8 %join_1.1 = bf16[16,16384]{1,0:T(8,128)(2,1)} custom-call(bf16[16,8192]{1,0:T(8,128)(2,1)S(1)} %collective-permute-done.6.refs_0_, bf16[16,8192]{1,0:T(8,128)(2,1)S(1)} %collective-permute-done.7.refs_1_, bf16[16,16384]{1,0:T(8,128)(2,1)} %join_0.1.refs_2_), custom_call_target="tpu_custom_call", output_to_operand_aliasing={{}: (2, {})} | custom-call | tf_op jit(solution)/shard_map/join_1/pallas_call | solution.py:283
  (1 shorter events, 0.0 us)
Async XLA Ops:
  0.0 23.1 %collective-permute-start.3 = (bf16[2,512,512]{2,1,0:T(8,128)(2,1)}, bf16[2,512,512]{2,1,0:T(8,128)(2,1)S(1)}, u32[]{:S(2)}, u32[]{:S(2)}) collective-permute-start(bf16[2,512,512]{2,1,0:T(8,128)(2,1)} %own.1), channel_id=1, source_target_pairs={{8,9},{10,11},{9,0},{11,2},{12,13},{14,15},{13,12},{15,14},{24,25}... | collective-permute-start | bytes 3145736 | tf_op jit(solution)/shard_map/ppermute | solution.py:211
  1.9 21.5 %collective-permute-start.2 = (bf16[2,512,512]{2,1,0:T(8,128)(2,1)}, bf16[2,512,512]{2,1,0:T(8,128)(2,1)S(1)}, u32[]{:S(2)}, u32[]{:S(2)}) collective-permute-start(bf16[2,512,512]{2,1,0:T(8,128)(2,1)} %own.1), channel_id=1, source_target_pairs={{8,0},{10,2},{9,13},{11,15},{12,9},{14,11},{24,16},{26,18},{25,29}... | collective-permute-start | bytes 3145736 | tf_op jit(solution)/shard_map/ppermute | solution.py:211
  6.9 9.3 %collective-permute-start = (bf16[16,8192]{1,0:T(8,128)(2,1)S(1)}, bf16[16,8192]{1,0:T(8,128)(2,1)S(1)}, u32[]{:S(2)}, u32[]{:S(2)}) collective-permute-start(bf16[16,8192]{1,0:T(8,128)(2,1)S(1)} %get-tuple-element.18), channel_id=1, source_target_pairs={{0,2},{2,0},{4,11},{6,9},{8,15},{10,13},{12,14},{14,12},{16,18},{1... | collective-permute-start | bytes 786440 | tf_op jit(solution)/shard_map/ppermute | solution.py:211
  8.2 13.5 %collective-permute-start.1 = (bf16[16,8192]{1,0:T(8,128)(2,1)S(1)}, bf16[16,8192]{1,0:T(8,128)(2,1)S(1)}, u32[]{:S(2)}, u32[]{:S(2)}) collective-permute-start(bf16[16,8192]{1,0:T(8,128)(2,1)S(1)} %get-tuple-element.24), channel_id=1, source_target_pairs={{0,0},{2,2},{4,9},{6,11},{8,13},{10,15},{12,12},{14,14},{16,16},{1... | collective-permute-start | bytes 786440 | tf_op jit(solution)/shard_map/ppermute | solution.py:211
  9.5 20.8 %collective-permute-start.4 = (bf16[16,8192]{1,0:T(8,128)(2,1)S(1)}, bf16[16,8192]{1,0:T(8,128)(2,1)S(1)}, u32[]{:S(2)}, u32[]{:S(2)}) collective-permute-start(bf16[16,8192]{1,0:T(8,128)(2,1)S(1)} %get-tuple-element.18), channel_id=1, source_target_pairs={{1,2},{3,0},{5,11},{7,9},{9,15},{11,13},{13,14},{15,12},{17,18},{1... | collective-permute-start | bytes 786440 | tf_op jit(solution)/shard_map/ppermute | solution.py:211
  18.4 11.8 %collective-permute-start.5 = (bf16[16,8192]{1,0:T(8,128)(2,1)S(1)}, bf16[16,8192]{1,0:T(8,128)(2,1)S(1)}, u32[]{:S(2)}, u32[]{:S(2)}) collective-permute-start(bf16[16,8192]{1,0:T(8,128)(2,1)S(1)} %get-tuple-element.24), channel_id=1, source_target_pairs={{1,0},{3,2},{5,9},{7,11},{9,13},{11,15},{13,12},{15,14},{17,16},{1... | collective-permute-start | bytes 786440 | tf_op jit(solution)/shard_map/ppermute | solution.py:211
  27.6 10.5 %collective-permute-start.8 = (bf16[16,8192]{1,0:T(8,128)(2,1)S(1)}, bf16[16,8192]{1,0:T(8,128)(2,1)S(1)}, u32[]{:S(2)}, u32[]{:S(2)}) collective-permute-start(bf16[16,8192]{1,0:T(8,128)(2,1)S(1)} %get-tuple-element.27), channel_id=1, source_target_pairs={{2,0},{0,2},{11,4},{9,6},{15,8},{13,10},{14,12},{12,14},{18,16},{1... | collective-permute-start | bytes 786440 | tf_op jit(solution)/shard_map/ppermute | solution.py:211
  28.9 9.2 %collective-permute-start.9 = (bf16[16,8192]{1,0:T(8,128)(2,1)S(1)}, bf16[16,8192]{1,0:T(8,128)(2,1)S(1)}, u32[]{:S(2)}, u32[]{:S(2)}) collective-permute-start(bf16[16,8192]{1,0:T(8,128)(2,1)S(1)} %get-tuple-element.28), channel_id=1, source_target_pairs={{0,0},{2,2},{9,4},{11,6},{13,8},{15,10},{12,12},{14,14},{16,16},{1... | collective-permute-start | bytes 786440 | tf_op jit(solution)/shard_map/ppermute | solution.py:211
  34.3 8.0 %collective-permute-start.6 = (bf16[16,8192]{1,0:T(8,128)(2,1)S(1)}, bf16[16,8192]{1,0:T(8,128)(2,1)S(1)}, u32[]{:S(2)}, u32[]{:S(2)}) collective-permute-start(bf16[16,8192]{1,0:T(8,128)(2,1)S(1)} %get-tuple-element.25), channel_id=1, source_target_pairs={{2,1},{0,3},{11,5},{9,7},{15,9},{13,11},{14,13},{12,15},{18,17},{1... | collective-permute-start | bytes 786440 | tf_op jit(solution)/shard_map/ppermute | solution.py:211
  36.2 9.3 %collective-permute-start.7 = (bf16[16,8192]{1,0:T(8,128)(2,1)S(1)}, bf16[16,8192]{1,0:T(8,128)(2,1)S(1)}, u32[]{:S(2)}, u32[]{:S(2)}) collective-permute-start(bf16[16,8192]{1,0:T(8,128)(2,1)S(1)} %get-tuple-element.26), channel_id=1, source_target_pairs={{0,1},{2,3},{9,5},{11,7},{13,9},{15,11},{12,13},{14,15},{16,17},{1... | collective-permute-start | bytes 786440 | tf_op jit(solution)/shard_map/ppermute | solution.py:211

commit v9 on v7

--- a/solution.py
+++ b/solution.py
@@ -51,7 +51,7 @@
 
 
 def worker_places(low_ctx):
-    return (0, 0), (low_ctx, 1), (low_ctx + 1, 1), (low_ctx + 1, 0)
+    return (0, 1), (low_ctx, 1), (low_ctx + 1, 1), (low_ctx + 1, 0)
 
 
 def own_request(low_ctx):

time: 48.3 us -> 47.1 us (0.975); the launches traced: 48.1 us -> 47.5 us
  Pallas kernels: 5.05 us -> 11.7 us
  waiting for transfers between devices: 24.8 us -> 19.2 us
  starting transfers between devices: 17.9 us -> 16.2 us
    pallas_call x2, Pallas kernels: 1.45 us -> 8.08 us  [one_request_each(): pl.pallas_call(functools.partial(attend_kernel, low_ctx, sub_size, [keys]...]
    ppermute x10, waiting for transfers between devices: 24.8 us -> 19.2 us  [moved(): lax.ppermute(array, ('ctx', 'head', 'sub'), [(flat(a), flat(b)) for a, b...]
    ppermute x10, starting transfers between devices: 17.9 us -> 16.2 us  [moved(): lax.ppermute(array, ('ctx', 'head', 'sub'), [(flat(a), flat(b)) for a, b...]
  transfers between devices with their start and end apart: 10 -> 10, of which waited for: 1 -> 4; matrix products, arithmetic and copies ran while one was open for 0% -> 0% of each run, Pallas kernels for 9% -> 23%
where the time goes in v9:
time: 47.1 us; the launch traced here: 47.5 us
  waiting for transfers between devices  19.2 us (41%)
  starting transfers between devices  16.2 us (34%)
  Pallas kernels  11.7 us (25%)
    ppermute x10, waiting for transfers between devices, moved(): lax.ppermute(array, ('ctx', 'head', 'sub'), [(flat(a), flat(b)) for a, b...  19.2 us
    ppermute x10, starting transfers between devices, moved(): lax.ppermute(array, ('ctx', 'head', 'sub'), [(flat(a), flat(b)) for a, b...  16.2 us
    pallas_call x2, Pallas kernels, one_request_each(): pl.pallas_call(functools.partial(attend_kernel, low_ctx, sub_size, [keys]...  8.08 us
    pallas_call x1, Pallas kernels, one_request_each(): pl.pallas_call(functools.partial(gather_home_kernel, low_ctx), out_shape=...  1.7 us
    pallas_call x1, Pallas kernels, one_request_each(): pl.pallas_call(split_kernel, out_shape=[q_piece] * head_count, in_specs=[...  1.06 us
  transfers between devices with their start and end apart: 10, of which 4 were waited for; matrix products, arithmetic and copies ran while one was open for 0% of the time, Pallas kernels for 23%

profile of v9, /device:TPU:1, one launch (start us, length us, event | category | flops | bytes accessed | tf_op | source)
XLA Modules:
  0.0 47.5 jit_solution(8480834254107425709)
XLA Ops:
  0.0 1.3 %collective-permute-start.3 = (bf16[2,512,512]{2,1,0:T(8,128)(2,1)}, bf16[2,512,512]{2,1,0:T(8,128)(2,1)S(1)}, u32[]{:S(2)}, u32[]{:S(2)}) collective-permute-start(bf16[2,512,512]{2,1,0:T(8,128)(2,1)} %own.1), channel_id=1, source_target_pairs={{8,9},{10,11},{9,1},{11,3},{12,13},{14,15},{13,12},{15,14},{24,25}... | collective-permute-start | bytes 3145736 | tf_op jit(solution)/shard_map/ppermute | solution.py:210
  1.3 1.3 %collective-permute-start.2 = (bf16[2,512,512]{2,1,0:T(8,128)(2,1)}, bf16[2,512,512]{2,1,0:T(8,128)(2,1)S(1)}, u32[]{:S(2)}, u32[]{:S(2)}) collective-permute-start(bf16[2,512,512]{2,1,0:T(8,128)(2,1)} %own.1), channel_id=1, source_target_pairs={{8,1},{10,3},{9,13},{11,15},{12,9},{14,11},{24,17},{26,19},{25,29}... | collective-permute-start | bytes 3145736 | tf_op jit(solution)/shard_map/ppermute | solution.py:210
  2.6 1.1 %split.1 = (bf16[16,8192]{1,0:T(8,128)(2,1)S(1)}, bf16[16,8192]{1,0:T(8,128)(2,1)S(1)}) custom-call(bf16[16,16384]{1,0:T(8,128)(2,1)} %queries.1), custom_call_target="tpu_custom_call" | custom-call | tf_op jit(solution)/shard_map/split/pallas_call | solution.py:217
  3.7 1.3 %collective-permute-start = (bf16[16,8192]{1,0:T(8,128)(2,1)S(1)}, bf16[16,8192]{1,0:T(8,128)(2,1)S(1)}, u32[]{:S(2)}, u32[]{:S(2)}) collective-permute-start(bf16[16,8192]{1,0:T(8,128)(2,1)S(1)} %get-tuple-element.17), channel_id=1, source_target_pairs={{0,3},{2,1},{4,11},{6,9},{8,15},{10,13},{12,14},{14,12},{16,19},{1... | collective-permute-start | bytes 786440 | tf_op jit(solution)/shard_map/ppermute | solution.py:210
  5.0 1.3 %collective-permute-start.1 = (bf16[16,8192]{1,0:T(8,128)(2,1)S(1)}, bf16[16,8192]{1,0:T(8,128)(2,1)S(1)}, u32[]{:S(2)}, u32[]{:S(2)}) collective-permute-start(bf16[16,8192]{1,0:T(8,128)(2,1)S(1)} %get-tuple-element.22), channel_id=1, source_target_pairs={{0,1},{2,3},{4,9},{6,11},{8,13},{10,15},{12,12},{14,14},{16,17},{1... | collective-permute-start | bytes 786440 | tf_op jit(solution)/shard_map/ppermute | solution.py:210
  6.3 3.9 %collective-permute-start.4 = (bf16[16,8192]{1,0:T(8,128)(2,1)S(1)}, bf16[16,8192]{1,0:T(8,128)(2,1)S(1)}, u32[]{:S(2)}, u32[]{:S(2)}) collective-permute-start(bf16[16,8192]{1,0:T(8,128)(2,1)S(1)} %get-tuple-element.17), channel_id=1, source_target_pairs={{1,3},{3,1},{5,11},{7,9},{9,15},{11,13},{13,14},{15,12},{17,19},{1... | collective-permute-start | bytes 786440 | tf_op jit(solution)/shard_map/ppermute | solution.py:210
  10.2 1.3 %collective-permute-done.after.refs_0_ = bf16[16,8192]{1,0:T(8,128)(2,1)S(1)} collective-permute-done((bf16[16,8192]{1,0:T(8,128)(2,1)S(1)}, bf16[16,8192]{1,0:T(8,128)(2,1)S(1)}, u32[]{:S(2)}, u32[]{:S(2)}) %collective-permute-start) | collective-permute-done | bytes 262176 | tf_op jit(solution)/shard_map/ppermute | solution.py:210
  11.5 1.7 %gather_home.1 = (bf16[4,2,4,256,128]{4,3,2,1,0:T(8,128)(2,1)S(1)}, s32[4]{0:T(128)S(1)}) custom-call(s32[4]{0:T(128)} %counts_in.1, s32[4]{0:T(128)} %counts_in.1, bf16[2,512,512]{2,1,0:T(8,128)(2,1)} %own.1, bf16[16,8192]{1,0:T(8,128)(2,1)S(1)} %collective-permute-done.after.refs_0_), custom_call_target="tpu_custom_call" | custom-call | tf_op jit(solution)/shard_map/gather_home/pallas_call | solution.py:232
  13.2 0.7 %collective-permute-start.5 = (bf16[16,8192]{1,0:T(8,128)(2,1)S(1)}, bf16[16,8192]{1,0:T(8,128)(2,1)S(1)}, u32[]{:S(2)}, u32[]{:S(2)}) collective-permute-start(bf16[16,8192]{1,0:T(8,128)(2,1)S(1)} %get-tuple-element.22), channel_id=1, source_target_pairs={{1,1},{3,3},{5,9},{7,11},{9,13},{11,15},{13,12},{15,14},{17,17},{1... | collective-permute-start | bytes 786440 | tf_op jit(solution)/shard_map/ppermute | solution.py:210
  13.9 0.0 collective-permute-done.1.refs_1_
  13.9 12.7 %collective-permute-done.3.refs_3_ = bf16[2,512,512]{2,1,0:T(8,128)(2,1)S(1)} collective-permute-done((bf16[2,512,512]{2,1,0:T(8,128)(2,1)}, bf16[2,512,512]{2,1,0:T(8,128)(2,1)S(1)}, u32[]{:S(2)}, u32[]{:S(2)}) %collective-permute-start.3) | collective-permute-done | bytes 1048608 | tf_op jit(solution)/shard_map/ppermute | solution.py:210
  26.6 2.1 %collective-permute-done.2.refs_2_ = bf16[2,512,512]{2,1,0:T(8,128)(2,1)S(1)} collective-permute-done((bf16[2,512,512]{2,1,0:T(8,128)(2,1)}, bf16[2,512,512]{2,1,0:T(8,128)(2,1)S(1)}, u32[]{:S(2)}, u32[]{:S(2)}) %collective-permute-start.2) | collective-permute-done | bytes 1048608 | tf_op jit(solution)/shard_map/ppermute | solution.py:210
  28.7 4.1 %attend_0.1 = (bf16[16,8192]{1,0:T(8,128)(2,1)S(1)}, bf16[16,8192]{1,0:T(8,128)(2,1)S(1)}, bf16[4,2,4,256,128]{4,3,2,1,0:T(8,128)(2,1)S(1)}) custom-call(s32[4]{0:T(128)S(1)} %get-tuple-element.19.counts, bf16[4,2,4,256,128]{4,3,2,1,0:T(8,128)(2,1)S(1)} %get-tuple-element.20.home, bf16[16,8192]{1,0:T(8,128)(2,1)S(1)} %collective-permute-done.after.refs_0_, ...), custom_call_target="tpu_custom_call" | custom-call | flops 10000000000 | bytes 4194304 | tf_op jit(solution)/shard_map/attend_0/pallas_call | solution.py:261
  32.7 1.3 %collective-permute-start.8 = (bf16[16,8192]{1,0:T(8,128)(2,1)S(1)}, bf16[16,8192]{1,0:T(8,128)(2,1)S(1)}, u32[]{:S(2)}, u32[]{:S(2)}) collective-permute-start(bf16[16,8192]{1,0:T(8,128)(2,1)S(1)} %get-tuple-element.25), channel_id=1, source_target_pairs={{3,0},{1,2},{11,4},{9,6},{15,8},{13,10},{14,12},{12,14},{19,16},{1... | collective-permute-start | bytes 786440 | tf_op jit(solution)/shard_map/ppermute | solution.py:210
  34.1 1.3 %collective-permute-start.9 = (bf16[16,8192]{1,0:T(8,128)(2,1)S(1)}, bf16[16,8192]{1,0:T(8,128)(2,1)S(1)}, u32[]{:S(2)}, u32[]{:S(2)}) collective-permute-start(bf16[16,8192]{1,0:T(8,128)(2,1)S(1)} %get-tuple-element.26), channel_id=1, source_target_pairs={{1,0},{3,2},{9,4},{11,6},{13,8},{15,10},{12,12},{14,14},{17,16},{1... | collective-permute-start | bytes 786440 | tf_op jit(solution)/shard_map/ppermute | solution.py:210
  35.4 0.0 collective-permute-done.4.refs_0_
  35.4 0.0 collective-permute-done.5.refs_1_
  35.4 4.0 %attend_1.1 = (bf16[16,8192]{1,0:T(8,128)(2,1)S(1)}, bf16[16,8192]{1,0:T(8,128)(2,1)S(1)}) custom-call(s32[4]{0:T(128)S(1)} %get-tuple-element.19.counts, bf16[4,2,4,256,128]{4,3,2,1,0:T(8,128)(2,1)S(1)} %get-tuple-element.21.home, bf16[16,8192]{1,0:T(8,128)(2,1)S(1)} %collective-permute-done.4.refs_0_, bf16[16,8192]{1,0:T(8,128)(2,1)S(1)} %collective-permute-done.5.refs_1_), custom_call_target="tpu_custom_call" | custom-call | flops 10000000000 | bytes 4194304 | tf_op jit(solution)/shard_map/attend_1/pallas_call | solution.py:261
  39.4 3.2 %collective-permute-start.6 = (bf16[16,8192]{1,0:T(8,128)(2,1)S(1)}, bf16[16,8192]{1,0:T(8,128)(2,1)S(1)}, u32[]{:S(2)}, u32[]{:S(2)}) collective-permute-start(bf16[16,8192]{1,0:T(8,128)(2,1)S(1)} %get-tuple-element.23), channel_id=1, source_target_pairs={{3,1},{1,3},{11,5},{9,7},{15,9},{13,11},{14,13},{12,15},{19,17},{1... | collective-permute-start | bytes 786440 | tf_op jit(solution)/shard_map/ppermute | solution.py:210
  42.6 0.7 %collective-permute-start.7 = (bf16[16,8192]{1,0:T(8,128)(2,1)S(1)}, bf16[16,8192]{1,0:T(8,128)(2,1)S(1)}, u32[]{:S(2)}, u32[]{:S(2)}) collective-permute-start(bf16[16,8192]{1,0:T(8,128)(2,1)S(1)} %get-tuple-element.24), channel_id=1, source_target_pairs={{1,1},{3,3},{9,5},{11,7},{13,9},{15,11},{12,13},{14,15},{17,17},{1... | collective-permute-start | bytes 786440 | tf_op jit(solution)/shard_map/ppermute | solution.py:210
  43.3 0.0 collective-permute-done.8.refs_0_
  43.3 0.0 collective-permute-done.9.refs_1_
  43.3 3.2 %collective-permute-done.6.refs_0_ = bf16[16,8192]{1,0:T(8,128)(2,1)S(1)} collective-permute-done((bf16[16,8192]{1,0:T(8,128)(2,1)S(1)}, bf16[16,8192]{1,0:T(8,128)(2,1)S(1)}, u32[]{:S(2)}, u32[]{:S(2)}) %collective-permute-start.6) | collective-permute-done | bytes 262176 | tf_op jit(solution)/shard_map/ppermute | solution.py:210
  46.5 0.0 collective-permute-done.7.refs_1_
  46.5 0.8 %join_1.1 = bf16[16,16384]{1,0:T(8,128)(2,1)} custom-call(bf16[16,8192]{1,0:T(8,128)(2,1)S(1)} %collective-permute-done.6.refs_0_, bf16[16,8192]{1,0:T(8,128)(2,1)S(1)} %collective-permute-done.7.refs_1_, bf16[16,16384]{1,0:T(8,128)(2,1)} %join_0.1.refs_2_), custom_call_target="tpu_custom_call", output_to_operand_aliasing={{}: (2, {})} | custom-call | tf_op jit(solution)/shard_map/join_1/pallas_call | solution.py:278
  (1 shorter events, 0.0 us)
Async XLA Ops:
  0.0 26.6 %collective-permute-start.3 = (bf16[2,512,512]{2,1,0:T(8,128)(2,1)}, bf16[2,512,512]{2,1,0:T(8,128)(2,1)S(1)}, u32[]{:S(2)}, u32[]{:S(2)}) collective-permute-start(bf16[2,512,512]{2,1,0:T(8,128)(2,1)} %own.1), channel_id=1, source_target_pairs={{8,9},{10,11},{9,1},{11,3},{12,13},{14,15},{13,12},{15,14},{24,25}... | collective-permute-start | bytes 3145736 | tf_op jit(solution)/shard_map/ppermute | solution.py:210
  1.3 27.4 %collective-permute-start.2 = (bf16[2,512,512]{2,1,0:T(8,128)(2,1)}, bf16[2,512,512]{2,1,0:T(8,128)(2,1)S(1)}, u32[]{:S(2)}, u32[]{:S(2)}) collective-permute-start(bf16[2,512,512]{2,1,0:T(8,128)(2,1)} %own.1), channel_id=1, source_target_pairs={{8,1},{10,3},{9,13},{11,15},{12,9},{14,11},{24,17},{26,19},{25,29}... | collective-permute-start | bytes 3145736 | tf_op jit(solution)/shard_map/ppermute | solution.py:210
  3.7 7.8 %collective-permute-start = (bf16[16,8192]{1,0:T(8,128)(2,1)S(1)}, bf16[16,8192]{1,0:T(8,128)(2,1)S(1)}, u32[]{:S(2)}, u32[]{:S(2)}) collective-permute-start(bf16[16,8192]{1,0:T(8,128)(2,1)S(1)} %get-tuple-element.17), channel_id=1, source_target_pairs={{0,3},{2,1},{4,11},{6,9},{8,15},{10,13},{12,14},{14,12},{16,19},{1... | collective-permute-start | bytes 786440 | tf_op jit(solution)/shard_map/ppermute | solution.py:210
  5.0 8.9 %collective-permute-start.1 = (bf16[16,8192]{1,0:T(8,128)(2,1)S(1)}, bf16[16,8192]{1,0:T(8,128)(2,1)S(1)}, u32[]{:S(2)}, u32[]{:S(2)}) collective-permute-start(bf16[16,8192]{1,0:T(8,128)(2,1)S(1)} %get-tuple-element.22), channel_id=1, source_target_pairs={{0,1},{2,3},{4,9},{6,11},{8,13},{10,15},{12,12},{14,14},{16,17},{1... | collective-permute-start | bytes 786440 | tf_op jit(solution)/shard_map/ppermute | solution.py:210
  6.3 29.1 %collective-permute-start.4 = (bf16[16,8192]{1,0:T(8,128)(2,1)S(1)}, bf16[16,8192]{1,0:T(8,128)(2,1)S(1)}, u32[]{:S(2)}, u32[]{:S(2)}) collective-permute-start(bf16[16,8192]{1,0:T(8,128)(2,1)S(1)} %get-tuple-element.17), channel_id=1, source_target_pairs={{1,3},{3,1},{5,11},{7,9},{9,15},{11,13},{13,14},{15,12},{17,19},{1... | collective-permute-start | bytes 786440 | tf_op jit(solution)/shard_map/ppermute | solution.py:210
  13.2 22.2 %collective-permute-start.5 = (bf16[16,8192]{1,0:T(8,128)(2,1)S(1)}, bf16[16,8192]{1,0:T(8,128)(2,1)S(1)}, u32[]{:S(2)}, u32[]{:S(2)}) collective-permute-start(bf16[16,8192]{1,0:T(8,128)(2,1)S(1)} %get-tuple-element.22), channel_id=1, source_target_pairs={{1,1},{3,3},{5,9},{7,11},{9,13},{11,15},{13,12},{15,14},{17,17},{1... | collective-permute-start | bytes 786440 | tf_op jit(solution)/shard_map/ppermute | solution.py:210
  32.7 10.5 %collective-permute-start.8 = (bf16[16,8192]{1,0:T(8,128)(2,1)S(1)}, bf16[16,8192]{1,0:T(8,128)(2,1)S(1)}, u32[]{:S(2)}, u32[]{:S(2)}) collective-permute-start(bf16[16,8192]{1,0:T(8,128)(2,1)S(1)} %get-tuple-element.25), channel_id=1, source_target_pairs={{3,0},{1,2},{11,4},{9,6},{15,8},{13,10},{14,12},{12,14},{19,16},{1... | collective-permute-start | bytes 786440 | tf_op jit(solution)/shard_map/ppermute | solution.py:210
  34.1 9.2 %collective-permute-start.9 = (bf16[16,8192]{1,0:T(8,128)(2,1)S(1)}, bf16[16,8192]{1,0:T(8,128)(2,1)S(1)}, u32[]{:S(2)}, u32[]{:S(2)}) collective-permute-start(bf16[16,8192]{1,0:T(8,128)(2,1)S(1)} %get-tuple-element.26), channel_id=1, source_target_pairs={{1,0},{3,2},{9,4},{11,6},{13,8},{15,10},{12,12},{14,14},{17,16},{1... | collective-permute-start | bytes 786440 | tf_op jit(solution)/shard_map/ppermute | solution.py:210
  39.4 7.1 %collective-permute-start.6 = (bf16[16,8192]{1,0:T(8,128)(2,1)S(1)}, bf16[16,8192]{1,0:T(8,128)(2,1)S(1)}, u32[]{:S(2)}, u32[]{:S(2)}) collective-permute-start(bf16[16,8192]{1,0:T(8,128)(2,1)S(1)} %get-tuple-element.23), channel_id=1, source_target_pairs={{3,1},{1,3},{11,5},{9,7},{15,9},{13,11},{14,13},{12,15},{19,17},{1... | collective-permute-start | bytes 786440 | tf_op jit(solution)/shard_map/ppermute | solution.py:210
  42.6 3.9 %collective-permute-start.7 = (bf16[16,8192]{1,0:T(8,128)(2,1)S(1)}, bf16[16,8192]{1,0:T(8,128)(2,1)S(1)}, u32[]{:S(2)}, u32[]{:S(2)}) collective-permute-start(bf16[16,8192]{1,0:T(8,128)(2,1)S(1)} %get-tuple-element.24), channel_id=1, source_target_pairs={{1,1},{3,3},{9,5},{11,7},{13,9},{15,11},{12,13},{14,15},{17,17},{1... | collective-permute-start | bytes 786440 | tf_op jit(solution)/shard_map/ppermute | solution.py:210
